TPU v7x, 32 devices: a whole 2x2x4 slice. The times are simulated.
32 devices in a mesh: dp: 8 (over y, x, core), tensor: 4 (over z).
Axes of the slice: x: 2, y: 2, z: 4, core: 2. Of those that a mesh axis runs over, the one named last changes fastest.
Arguments:
- tokens: bfloat16 [64, 261, 768], P('dp'), may hold values from -6 to 6
- patch_mask: int32 [64, 256], P('dp'), may hold values from 0 to 1, as said below
- cotangent: bfloat16 [64, 261, 768], P('dp'), may hold values from -6 to 6
- qkv_weight: float32 [3, 768, 768], P(None, 'dp', 'tensor'), may hold values from -0.21875 to 0.21875
- qkv_first: float32 [3, 768, 768], P(None, 'dp', 'tensor'), may hold values from -0.005859375 to 0.005859375
- qkv_second: float32 [3, 768, 768], P(None, 'dp', 'tensor'), may hold values from 1.410555e-07 to 5.64222e-07
- proj_weight: float32 [768, 768], P('tensor', 'dp'), may hold values from -0.625 to 0.625
- proj_first: float32 [768, 768], P('tensor', 'dp'), may hold values from -0.005859375 to 0.005859375
- proj_second: float32 [768, 768], P('tensor', 'dp'), may hold values from 1.410555e-07 to 5.64222e-07
- fc1_weight: float32 [768, 3072], P('dp', 'tensor'), may hold values from -0.21875 to 0.21875
- fc1_first: float32 [768, 3072], P('dp', 'tensor'), may hold values from -0.005859375 to 0.005859375
- fc1_second: float32 [768, 3072], P('dp', 'tensor'), may hold values from 1.410555e-07 to 5.64222e-07
- fc2_weight: float32 [3072, 768], P('tensor', 'dp'), may hold values from -0.109375 to 0.109375
- fc2_first: float32 [3072, 768], P('tensor', 'dp'), may hold values from -0.005859375 to 0.005859375
- fc2_second: float32 [3072, 768], P('tensor', 'dp'), may hold values from 1.410555e-07 to 5.64222e-07
- vectors: float32 [9, 768], replicated, may hold values from -3 to 4, as said below
- vectors_first: float32 [9, 768], replicated, may hold values from -0.005859375 to 0.005859375
- vectors_second: float32 [9, 768], replicated, may hold values from 1.410555e-07 to 5.64222e-07
- head_bias: float32 [2, 768], P(None, 'tensor'), may hold values from -1 to 2
- head_bias_first: float32 [2, 768], P(None, 'tensor'), may hold values from -0.0234375 to 0.0234375
- head_bias_second: float32 [2, 768], P(None, 'tensor'), may hold values from 2.256888e-06 to 9.027552e-06
- fc1_bias: float32 [3072], P('tensor'), may hold values from -2 to 2
- fc1_bias_first: float32 [3072], P('tensor'), may hold values from -0.001953125 to 0.001953125
- fc1_bias_second: float32 [3072], P('tensor'), may hold values from 2.8211101e-08 to 1.12844404e-07
Outputs:
- block_out: bfloat16 [64, 261, 768], P('dp')
- tokens_grad: bfloat16 [64, 261, 768], P('dp')
- grad_norm: float32 [], replicated
- qkv_new: float32 [3, 768, 768], P(None, 'dp', 'tensor')
- qkv_first_new: float32 [3, 768, 768], P(None, 'dp', 'tensor')
- qkv_second_new: float32 [3, 768, 768], P(None, 'dp', 'tensor')
- proj_new: float32 [768, 768], P('tensor', 'dp')
- proj_first_new: float32 [768, 768], P('tensor', 'dp')
- proj_second_new: float32 [768, 768], P('tensor', 'dp')
- fc1_new: float32 [768, 3072], P('dp', 'tensor')
- fc1_first_new: float32 [768, 3072], P('dp', 'tensor')
- fc1_second_new: float32 [768, 3072], P('dp', 'tensor')
- fc2_new: float32 [3072, 768], P('tensor', 'dp')
- fc2_first_new: float32 [3072, 768], P('tensor', 'dp')
- fc2_second_new: float32 [3072, 768], P('tensor', 'dp')
- vectors_new: float32 [9, 768], replicated
- vectors_first_new: float32 [9, 768], replicated
- vectors_second_new: float32 [9, 768], replicated
- head_bias_new: float32 [2, 768], P(None, 'tensor')
- head_bias_first_new: float32 [2, 768], P(None, 'tensor')
- head_bias_second_new: float32 [2, 768], P(None, 'tensor')
- fc1_bias_new: float32 [3072], P('tensor')
- fc1_bias_first_new: float32 [3072], P('tensor')
- fc1_bias_second_new: float32 [3072], P('tensor')
- qkv_copy: bfloat16 [3, 768, 768], P(None, 'dp', 'tensor')
- proj_copy: bfloat16 [768, 768], P('tensor', 'dp')
- fc1_copy: bfloat16 [768, 3072], P('dp', 'tensor')
- fc2_copy: bfloat16 [3072, 768], P('tensor', 'dp')
Inputs may be any that keep to these rules, and one draw needn't show every extreme that they name: `patch_mask`: per crop, 1 exactly on the patches (row-major on the 16 x 16 grid) covered by four rectangles, each 2 to 8 patches on a side. `vectors`: rows 0, 2, 4, 6 are positive.
All inputs are finite; a program needn't handle non-finite values.
Results may differ from a plain program's by a relative error of at most 0.02.
Values may be sent and summed in bfloat16 or wider, within the bound.
A program may use at most 192 MiB of HBM per device.

v0:
```python
import jax
import jax.numpy as jnp
from jax import lax
from jax.sharding import PartitionSpec as P

HD = 64
REG = 4
STEP = 10


norm_eps = 1e-06
clip_norm = 1.0
rate_matrix = 0.04
rate_vector = 0.2
decay_matrix = 0.04
moment_decay = 0.5
adam_eps = 1e-08


def layer_norm(values, gain_row, shift_row):
    middle_val = jnp.mean(values, axis=-1, keepdims=True)
    centred = values - middle_val
    spread = jnp.mean(centred * centred, axis=-1, keepdims=True)
    return centred * lax.rsqrt(spread + norm_eps) * gain_row + shift_row


def gelu_exact(values):
    return jax.nn.gelu(values, approximate=False)


def inner_rows(first_op, second_op):
    return lax.dot_general(
        first_op, second_op, (((0,), (0,)), ((), ())), preferred_element_type=jnp.float32
    )


def outer_cols(first_op, second_op):
    return lax.dot_general(
        first_op, second_op, (((1,), (1,)), ((), ())), preferred_element_type=jnp.float32
    )


def square_sum(values):
    return jnp.sum(values * values)


def adam_step(weight, first, second, grad, rate, decay):
    first_new = moment_decay * first + (1.0 - moment_decay) * grad
    second_new = moment_decay * second + (1.0 - moment_decay) * grad * grad
    correct = 1.0 - moment_decay**STEP
    weight_new = weight - rate * (
        first_new / correct / (jnp.sqrt(second_new / correct) + adam_eps) + decay * weight
    )
    return (weight_new, first_new, second_new)


def per_device(
    tokens,
    patch_mask,
    cotangent,
    qkv_weight,
    qkv_first,
    qkv_second,
    proj_weight,
    proj_first,
    proj_second,
    fc1_weight,
    fc1_first,
    fc1_second,
    fc2_weight,
    fc2_first,
    fc2_second,
    vectors,
    vectors_first,
    vectors_second,
    head_bias,
    head_bias_first,
    head_bias_second,
    fc1_bias,
    fc1_bias_first,
    fc1_bias_second,
):
    crops, seq_len, width = tokens.shape
    rows_here = crops * seq_len
    scale = HD ** (-0.5)
    low_shards = (
        qkv_weight.astype(jnp.bfloat16),
        proj_weight.astype(jnp.bfloat16),
        fc1_weight.astype(jnp.bfloat16),
        fc2_weight.astype(jnp.bfloat16),
    )
    qkv_full, proj_full, up_full, down_full = (
        lax.all_gather(low_shards[0], "dp", axis=1, tiled=True),
        lax.all_gather(low_shards[1], "dp", axis=1, tiled=True),
        lax.all_gather(low_shards[2], "dp", axis=0, tiled=True),
        lax.all_gather(low_shards[3], "dp", axis=1, tiled=True),
    )
    head_cols = qkv_full.shape[2]
    heads_here = head_cols // HD
    joined = jnp.concatenate([qkv_full[0], qkv_full[1], qkv_full[2]], axis=1)
    bias_row = jnp.concatenate([head_bias[0], jnp.zeros((head_cols,), jnp.float32), head_bias[1]])
    chosen = jnp.concatenate(
        [jnp.zeros((crops, 1 + REG), jnp.bool_), patch_mask == 1], axis=1
    ).reshape(rows_here, 1)
    inputs = tokens.astype(jnp.float32).reshape(rows_here, width)
    start = jnp.where(chosen, vectors[8], inputs)
    norm_one = layer_norm(start, vectors[0], vectors[1]).astype(jnp.bfloat16)

    def attend(norm_in):
        mixed = (jnp.dot(norm_in, joined, preferred_element_type=jnp.float32) + bias_row).astype(
            jnp.bfloat16
        )
        query = mixed[:, :head_cols].reshape(crops, seq_len, heads_here, HD)
        keys_part = mixed[:, head_cols : 2 * head_cols].reshape(crops, seq_len, heads_here, HD)
        values_part = mixed[:, 2 * head_cols :].reshape(crops, seq_len, heads_here, HD)
        scores = (
            jnp.einsum("bqhe,bkhe->bhqk", query, keys_part, preferred_element_type=jnp.float32)
            * scale
        )
        probs = jax.nn.softmax(scores, axis=-1)
        probs_low = probs.astype(jnp.bfloat16)
        context = jnp.einsum(
            "bhqk,bkhe->bqhe", probs_low, values_part, preferred_element_type=jnp.float32
        )
        context_low = context.astype(jnp.bfloat16).reshape(rows_here, head_cols)
        return (query, keys_part, values_part, probs, probs_low, context_low)

    def expand(norm_in):
        hidden = jnp.dot(norm_in, up_full, preferred_element_type=jnp.float32) + fc1_bias
        return (hidden, gelu_exact(hidden).astype(jnp.bfloat16))

    query, keys_part, values_part, probs, probs_low, context_low = attend(norm_one)
    attn_part = jnp.dot(context_low, proj_full, preferred_element_type=jnp.float32)
    attn = lax.psum(attn_part.astype(jnp.bfloat16), "tensor").astype(jnp.float32) + vectors[3]
    middle = start + vectors[2] * attn
    norm_two = layer_norm(middle, vectors[4], vectors[5]).astype(jnp.bfloat16)
    hidden, active = expand(norm_two)
    mlp_part = jnp.dot(active, down_full, preferred_element_type=jnp.float32)
    mlp = lax.psum(mlp_part.astype(jnp.bfloat16), "tensor").astype(jnp.float32) + vectors[7]
    block_out = (middle + vectors[6] * mlp).astype(jnp.bfloat16).reshape(crops, seq_len, width)
    cot = cotangent.astype(jnp.float32).reshape(rows_here, width)
    hidden_again, active_again = expand(norm_two)
    mlp_grad = vectors[6] * cot
    grad_scale_two = jnp.sum(cot * mlp, axis=0)
    grad_bias_out = jnp.sum(mlp_grad, axis=0)
    mlp_grad_low = mlp_grad.astype(jnp.bfloat16)
    grad_down = inner_rows(active_again, mlp_grad_low)
    grad_active = outer_cols(mlp_grad_low, down_full)
    gelu_value, gelu_back = jax.vjp(gelu_exact, hidden_again)
    grad_hidden = gelu_back(grad_active)[0].astype(jnp.bfloat16)
    grad_up = inner_rows(norm_two, grad_hidden)
    grad_fc1_bias = jnp.sum(grad_hidden.astype(jnp.float32), axis=0)
    back_two = outer_cols(grad_hidden, up_full)
    grad_norm_two = lax.psum(back_two.astype(jnp.bfloat16), "tensor").astype(jnp.float32)
    norm_value, norm_two_back = jax.vjp(layer_norm, middle, vectors[4], vectors[5])
    grad_from_two, grad_gain_two, grad_shift_two = norm_two_back(grad_norm_two)
    grad_middle = cot + grad_from_two
    query, keys_part, values_part, probs, probs_low, context_low = attend(norm_one)
    attn_grad = vectors[2] * grad_middle
    grad_scale_one = jnp.sum(grad_middle * attn, axis=0)
    grad_bias_proj = jnp.sum(attn_grad, axis=0)
    attn_grad_low = attn_grad.astype(jnp.bfloat16)
    grad_proj = inner_rows(context_low, attn_grad_low)
    grad_context = (
        outer_cols(attn_grad_low, proj_full)
        .astype(jnp.bfloat16)
        .reshape(crops, seq_len, heads_here, HD)
    )
    grad_probs = jnp.einsum(
        "bqhe,bkhe->bhqk", grad_context, values_part, preferred_element_type=jnp.float32
    )
    grad_scores = probs * (grad_probs - jnp.sum(grad_probs * probs, axis=-1, keepdims=True))
    grad_scores_low = grad_scores.astype(jnp.bfloat16)
    grad_query = (
        jnp.einsum(
            "bhqk,bkhe->bqhe", grad_scores_low, keys_part, preferred_element_type=jnp.float32
        )
        * scale
    ).astype(jnp.bfloat16)
    grad_keys = (
        jnp.einsum("bhqk,bqhe->bkhe", grad_scores_low, query, preferred_element_type=jnp.float32)
        * scale
    ).astype(jnp.bfloat16)
    grad_values = jnp.einsum(
        "bhqk,bqhe->bkhe", probs_low, grad_context, preferred_element_type=jnp.float32
    ).astype(jnp.bfloat16)
    grad_mixed = jnp.concatenate(
        [
            grad_query.reshape(rows_here, head_cols),
            grad_keys.reshape(rows_here, head_cols),
            grad_values.reshape(rows_here, head_cols),
        ],
        axis=1,
    )
    grad_joined = inner_rows(norm_one, grad_mixed)
    grad_qkv = jnp.stack(
        [
            grad_joined[:, :head_cols],
            grad_joined[:, head_cols : 2 * head_cols],
            grad_joined[:, 2 * head_cols :],
        ]
    )
    mixed_sums = jnp.sum(grad_mixed.astype(jnp.float32), axis=0)
    grad_head_bias = jnp.stack([mixed_sums[:head_cols], mixed_sums[2 * head_cols :]])
    back_one = outer_cols(grad_mixed, joined)
    grad_norm_one = lax.psum(back_one.astype(jnp.bfloat16), "tensor").astype(jnp.float32)
    norm_one_value, norm_one_back = jax.vjp(layer_norm, start, vectors[0], vectors[1])
    grad_from_one, grad_gain_one, grad_shift_one = norm_one_back(grad_norm_one)
    grad_start = grad_middle + grad_from_one
    grad_token_row = jnp.sum(jnp.where(chosen, grad_start, 0.0), axis=0)
    tokens_grad = (
        jnp.where(chosen, 0.0, grad_start).astype(jnp.bfloat16).reshape(crops, seq_len, width)
    )
    vector_grads = jnp.stack(
        [
            grad_gain_one,
            grad_shift_one,
            grad_scale_one,
            grad_bias_proj,
            grad_gain_two,
            grad_shift_two,
            grad_scale_two,
            grad_bias_out,
            grad_token_row,
        ]
    )
    qkv_shard, proj_shard, up_shard, down_shard = (
        lax.psum_scatter(grad_qkv, "dp", scatter_dimension=1, tiled=True),
        lax.psum_scatter(grad_proj, "dp", scatter_dimension=1, tiled=True),
        lax.psum_scatter(grad_up, "dp", scatter_dimension=0, tiled=True),
        lax.psum_scatter(grad_down, "dp", scatter_dimension=1, tiled=True),
    )
    vector_sum, head_sum, fc1b_sum = lax.psum((vector_grads, grad_head_bias, grad_fc1_bias), "dp")
    first_data = (lax.axis_index("dp") == 0).astype(jnp.float32)
    first_tensor = (lax.axis_index("tensor") == 0).astype(jnp.float32)
    local_squares = (
        square_sum(qkv_shard)
        + square_sum(proj_shard)
        + square_sum(up_shard)
        + square_sum(down_shard)
    )
    local_squares = local_squares + first_data * (square_sum(head_sum) + square_sum(fc1b_sum))
    local_squares = local_squares + first_data * first_tensor * square_sum(vector_sum)
    total_squares = lax.psum(local_squares, ("dp", "tensor"))
    grad_norm = jnp.sqrt(total_squares)
    factor = jnp.minimum(1.0, clip_norm / (grad_norm + 1e-06))
    qkv_set = adam_step(
        qkv_weight, qkv_first, qkv_second, factor * qkv_shard, rate_matrix, decay_matrix
    )
    proj_set = adam_step(
        proj_weight, proj_first, proj_second, factor * proj_shard, rate_matrix, decay_matrix
    )
    fc1_set = adam_step(
        fc1_weight, fc1_first, fc1_second, factor * up_shard, rate_matrix, decay_matrix
    )
    fc2_set = adam_step(
        fc2_weight, fc2_first, fc2_second, factor * down_shard, rate_matrix, decay_matrix
    )
    vectors_set = adam_step(
        vectors, vectors_first, vectors_second, factor * vector_sum, rate_vector, 0.0
    )
    head_set = adam_step(
        head_bias, head_bias_first, head_bias_second, factor * head_sum, rate_vector, 0.0
    )
    fc1b_set = adam_step(
        fc1_bias, fc1_bias_first, fc1_bias_second, factor * fc1b_sum, rate_vector, 0.0
    )
    return (
        block_out,
        tokens_grad,
        grad_norm,
        qkv_set[0],
        qkv_set[1],
        qkv_set[2],
        proj_set[0],
        proj_set[1],
        proj_set[2],
        fc1_set[0],
        fc1_set[1],
        fc1_set[2],
        fc2_set[0],
        fc2_set[1],
        fc2_set[2],
        vectors_set[0],
        vectors_set[1],
        vectors_set[2],
        head_set[0],
        head_set[1],
        head_set[2],
        fc1b_set[0],
        fc1b_set[1],
        fc1b_set[2],
        qkv_set[0].astype(jnp.bfloat16),
        proj_set[0].astype(jnp.bfloat16),
        fc1_set[0].astype(jnp.bfloat16),
        fc2_set[0].astype(jnp.bfloat16),
    )


def solution(mesh):
    placed = (
        P("dp", None, None),
        P("dp", None),
        P("dp", None, None),
        P(None, "dp", "tensor"),
        P(None, "dp", "tensor"),
        P(None, "dp", "tensor"),
        P("tensor", "dp"),
        P("tensor", "dp"),
        P("tensor", "dp"),
        P("dp", "tensor"),
        P("dp", "tensor"),
        P("dp", "tensor"),
        P("tensor", "dp"),
        P("tensor", "dp"),
        P("tensor", "dp"),
        P(),
        P(),
        P(),
        P(None, "tensor"),
        P(None, "tensor"),
        P(None, "tensor"),
        P("tensor"),
        P("tensor"),
        P("tensor"),
    )
    return jax.shard_map(
        per_device,
        mesh=mesh,
        in_specs=placed,
        out_specs=(
            P("dp", None, None),
            P("dp", None, None),
            P(),
            P(None, "dp", "tensor"),
            P(None, "dp", "tensor"),
            P(None, "dp", "tensor"),
            P("tensor", "dp"),
            P("tensor", "dp"),
            P("tensor", "dp"),
            P("dp", "tensor"),
            P("dp", "tensor"),
            P("dp", "tensor"),
            P("tensor", "dp"),
            P("tensor", "dp"),
            P("tensor", "dp"),
            P(),
            P(),
            P(),
            P(None, "tensor"),
            P(None, "tensor"),
            P(None, "tensor"),
            P("tensor"),
            P("tensor"),
            P("tensor"),
            P(None, "dp", "tensor"),
            P("tensor", "dp"),
            P("dp", "tensor"),
            P("tensor", "dp"),
        ),
        check_vma=False,
    )
```

profile of v0, /device:TPU:0, one launch (start us, length us, event | category | flops | bytes accessed | tf_op | source)
XLA Modules:
  0.0 832.9 jit_solution(966068109369206359)
XLA Ops:
  11.4 5.3 select_reduce_fusion.1
  17.7 5.3 copy.139
  26.0 5.6 multiply_reduce_fusion.6
  32.7 12.9 %all_gather.13 = bf16[192,768]{0,1:T(8,128)(2,1)} all-gather(bf16[192,96]{0,1:T(8,128)(2,1)} %copy.149), channel_id=1, replica_groups=mesh['dp'=8,'tensor'=4] {'dp'}, dimensions={1}, use_global_device_ids=true | all-gather | bytes 331776 | tf_op jit(solution)/shard_map/all_gather | solution.py:94
  45.6 10.9 %all_gather.12 = bf16[3,768,192]{2,1,0:T(8,128)(2,1)S(1)} all-gather(bf16[3,96,192]{2,1,0:T(8,128)(2,1)S(1)} %convert_element_type.130), channel_id=1, replica_groups=mesh['dp'=8,'tensor'=4] {'dp'}, dimensions={1}, use_global_device_ids=true | all-gather | bytes 995328 | tf_op jit(solution)/shard_map/all_gather | solution.py:93
  56.7 6.8 reshape.215
  63.6 3.9 add_convert_fusion.3
  67.6 2.4 fusion.19
  72.5 2.9 reshape.218
  75.4 2.4 reshape.216
  79.7 5.3 fusion.79
  85.0 5.0 fusion.33
  92.5 4.2 convolution_convert_fusion.3
  99.3 3.3 copy.150
  102.6 6.5 reshape.221
  109.1 111.2 %all-reduce.7.cloned.1.call-done = bf16[2088,768]{1,0:T(8,128)(2,1)} async-done(((bf16[2088,768]{1,0:T(8,128)(2,1)}), bf16[2088,768]{1,0:T(8,128)(2,1)}) %all-reduce.7.cloned.1.call-update) | async-done | bytes 3207184 | tf_op jit(solution)/shard_map/psum | solution.py:134
  220.3 5.4 fusion.75
  230.3 19.9 %multiply_convert_fusion.2 = (bf16[2088,768]{1,0:T(8,128)(2,1)}, f32[2088,768]{1,0:T(8,128)}, f32[2088,768]{1,0:T(8,128)}) fusion(f32[768]{0:T(1024)S(1)} %copy-done.71, bf16[2088,768]{1,0:T(8,128)(2,1)S(1)} %add_convert_fusion.2, bf16[768,768]{1,0:T(8,128)(2,1)} %all-gather.3.cloned.1.call-done), kind=kOutput, calls=%fused_computation.36 | convolution fusion | flops 2568941568 | bytes 20425728 | tf_op jit(solution)/shard_map/dot_general | solution.py:129
  250.3 12.2 %convert_reduce_fusion.2 = (f32[768]{0:T(1024)}, bf16[2088,768]{1,0:T(8,128)(2,1)S(1)}) fusion(f32[2088,768]{1,0:T(8,128)} %get-tuple-element.192, f32[2088,768]{1,0:T(8,128)} %get-tuple-element.213, bf16[768,768]{0,1:T(8,128)(2,1)} %all-gather.5.cloned.1.call-done, f32[2088,768]{1,0:T(8,128)} %reshape.221, f32[768]{0:T(1024)S(1)} %copy-done.63), kind=kOutput, calls=%fused_computation.28 | convolution fusion | flops 2491968768 | bytes 23635968 | tf_op jit(solution)/shard_map/dot_general | solution.py:38
  264.2 4.1 convolution_convert_fusion.1
  268.5 6.3 fusion.81
  274.9 8.2 fusion.38
  283.2 107.4 %all-reduce.9.cloned.1.call-done = bf16[2088,768]{1,0:T(8,128)(2,1)} async-done(((bf16[2088,768]{1,0:T(8,128)(2,1)}), bf16[2088,768]{1,0:T(8,128)(2,1)}) %all-reduce.9.cloned.1.call-update) | async-done | bytes 3207184 | tf_op jit(solution)/shard_map/psum | solution.py:154
  390.6 6.0 convert_reduce_fusion.1
  396.6 6.2 fusion.9
  402.9 5.1 add_add_fusion.3
  407.9 2.6 copy-done.1
  411.8 2.4 reshape.222
  414.2 9.9 %multiply_reduce_fusion = (f32[8,3,261]{2,1,0:T(4,128)S(1)}, f32[8,3,261,261]{2,3,1,0:T(8,128)}) fusion(f32[8,3,261,261]{2,3,1,0:T(8,128)} %get-tuple-element.212, f32[8,3,261]{2,1,0:T(4,128)S(1)} %copy-done.47, bf16[8,261,3,64]{1,0,3,2:T(8,128)(2,1)S(1)} %copy-done.22, bf16[8,261,3,64]{1,0,3,2:T(8,128)(2,1)} %reshape.222), kind=kOutput, calls=%fused_computation.2 | convolution fusion | flops 214166176 | bytes 14732928 | tf_op jit(solution)/shard_map/bqhe,bkhe->bhqk/dot_general | solution.py:169
  428.6 10.1 %multiply_convert_fusion = bf16[8,3,261,261]{2,3,1,0:T(8,128)(2,1)} fusion(f32[8,3,261,261]{2,3,1,0:T(8,128)} %get-tuple-element.215, f32[8,3,261]{2,1,0:T(4,128)S(1)} %get-tuple-element.214, f32[8,3,261,261]{2,3,1,0:T(8,128)} %get-tuple-element.212, f32[8,3,261]{2,1,0:T(4,128)S(1)} %copy-done.47), kind=kLoop, calls=%fused_computation.1 | loop fusion | flops 6539616 | bytes 16399152 | tf_op jit(solution)/shard_map/convert_element_type | solution.py:173
  438.8 3.7 fusion.36
  445.4 4.4 fusion.37
  453.5 5.2 convolution_bitcast_fusion
  461.3 5.1 fusion.80
  467.9 3.0 copy.176
  470.9 2.8 reshape.231
  473.9 6.8 convolution_convert_fusion.2
  480.8 4.5 convolution_convert_fusion
  490.9 2.3 convert_reduce_fusion.3
  498.8 37.7 %reduce-scatter.13.cloned.1.call-done = f32[96,576]{1,0:T(8,128)} async-done(((f32[768,576]{1,0:T(8,128)}), f32[96,576]{1,0:T(8,128)}) %reduce-scatter.13.cloned.1.call-update) | async-done | bytes 221200
  541.0 170.7 %all-reduce.11.cloned.1.call-done = (bf16[2088,768]{1,0:T(8,128)(2,1)}, bf16[2088,768]{1,0:T(8,128)(2,1)}) async-done(((bf16[2088,768]{1,0:T(8,128)(2,1)}, bf16[2088,768]{1,0:T(8,128)(2,1)}), (bf16[2088,768]{1,0:T(8,128)(2,1)}, bf16[2088,768]{1,0:T(8,128)(2,1)})) %all-reduce.11.cloned.1.call-update) | async-done | bytes 6414352 | tf_op jit(solution)/shard_map/psum | solution.py:139
  711.8 6.7 fusion.10
  718.6 11.3 %multiply_reduce_fusion.3 = (f32[768]{0:T(1024)S(1)}, bf16[2088,768]{1,0:T(8,128)(2,1)}, f32[2088]{0:T(1024)S(1)}, f32[2088,768]{1,0:T(8,128)}) fusion(f32[2088,768]{1,0:T(8,128)} %reshape.221, bf16[2088,768]{1,0:T(8,128)(2,1)} %get-tuple-element.162, f32[768]{0:T(1024)} %get-tuple-element.158, f32[2088,768]{1,0:T(8,128)S(1)} %bitcast.77, ...), kind=kLoop, calls=%fused_computation.26 | loop fusion | flops 25654488 | bytes 35329704 | tf_op jit(solution)/shard_map/reduce_sum | solution.py:144
  730.0 7.6 select_reduce_fusion
  737.7 24.5 %all-reduce.1 = (f32[2,192]{1,0:T(2,128)S(1)}, f32[768]{0:T(1024)S(1)}, f32[9,768]{1,0:T(8,128)S(1)}) all-reduce(f32[2,192]{1,0:T(2,128)S(1)} %copy-done.69, f32[768]{0:T(1024)S(1)} %copy-done.75, f32[9,768]{1,0:T(8,128)S(1)} %stack.55), channel_id=1, replica_groups=mesh['dp'=8,'tensor'=4] {'dp'}, use_global_device_ids=true, to_apply=%region_24.25 | all-reduce | flops 8064 | bytes 64512 | tf_op jit(solution)/shard_map/psum | solution.py:233
  766.2 38.2 %psum.63 = f32[]{:T(128)} all-reduce(f32[]{:T(128)S(6)} %add.279), channel_id=1, replica_groups=mesh['dp'=8,'tensor'=4] {'dp','tensor'}, use_global_device_ids=true, to_apply=%region_40.41 | all-reduce | flops 1 | bytes 8 | tf_op jit(solution)/shard_map/psum | solution.py:244
  808.8 2.9 reshape.226
  814.0 2.9 reshape.220
  (294 shorter events, 69.7 us)
Async XLA Ops:
  8.0 212.3 %all-reduce.7.cloned.1.call-start = ((), (), s32[]{:S(2)}) async-start(), calls=%async_computation.4 | async-start | bytes 6414336 | tf_op jit(solution)/shard_map/psum | solution.py:134
  11.4 208.9 %copy-start.38 = (f32[768]{0:T(1024)}, f32[768]{0:T(1024)S(1)}, u32[]{:S(2)}) copy-start(f32[768]{0:T(1024)S(1)} %get-tuple-element.157) | copy-start | bytes 9220
  11.4 14.5 %copy-start.3 = (bf16[8,261,768]{2,0,1:T(8,128)(2,1)S(1)}, bf16[8,261,768]{2,0,1:T(8,128)(2,1)}, u32[]{:S(2)}) copy-start(bf16[8,261,768]{2,0,1:T(8,128)(2,1)} %param.24) | copy-start | bytes 9621508
  16.9 46.7 %copy-start.40 = (f32[2088]{0:T(1024)}, f32[2088]{0:T(1024)S(1)}, u32[]{:S(2)}) copy-start(f32[2088]{0:T(1024)S(1)} %div.121) | copy-start | bytes 25060
  17.7 15.0 %copy-start.20 = (f32[3,96,192]{2,1,0:T(8,128)S(1)}, f32[3,96,192]{2,1,0:T(8,128)}, u32[]{:S(2)}) copy-start(f32[3,96,192]{2,1,0:T(8,128)} %param.27) | copy-start | bytes 663556
  32.7 23.9 %copy-start.51 = (f32[2088]{0:T(1024)}, f32[2088]{0:T(1024)S(1)}, u32[]{:S(2)}) copy-start(f32[2088]{0:T(1024)S(1)} %add.252) | copy-start | bytes 25060
  32.7 30.9 %copy-start.42 = (f32[2088]{0:T(1024)}, f32[2088]{0:T(1024)S(1)}, u32[]{:S(2)}) copy-start(f32[2088]{0:T(1024)S(1)} %rsqrt.22) | copy-start | bytes 25060
  56.6 10.9 %copy-start.26 = (bf16[768,192]{1,0:T(8,128)(2,1)}, bf16[768,192]{1,0:T(8,128)(2,1)S(1)}, u32[]{:S(2)}) copy-start(bf16[768,192]{1,0:T(8,128)(2,1)S(1)} %get-tuple-element.204) | copy-start | bytes 884740
  56.7 10.9 %copy-start.28 = (bf16[768,192]{1,0:T(8,128)(2,1)}, bf16[768,192]{1,0:T(8,128)(2,1)S(1)}, u32[]{:S(2)}) copy-start(bf16[768,192]{1,0:T(8,128)(2,1)S(1)} %get-tuple-element.205) | copy-start | bytes 884740
  56.7 10.9 %copy-start.30 = (bf16[768,192]{1,0:T(8,128)(2,1)}, bf16[768,192]{1,0:T(8,128)(2,1)S(1)}, u32[]{:S(2)}) copy-start(bf16[768,192]{1,0:T(8,128)(2,1)S(1)} %get-tuple-element.206) | copy-start | bytes 884740
  96.7 133.6 %all-gather.3.cloned.1.call-start = ((), (), s32[]{:S(2)}) async-start(), calls=%async_computation.5 | async-start | bytes 1327104 | tf_op jit(solution)/shard_map/all_gather | solution.py:95
  98.4 151.8 %all-gather.5.cloned.1.call-start = ((), (), s32[]{:S(2)}) async-start(), calls=%async_computation.6 | async-start | bytes 1327104 | tf_op jit(solution)/shard_map/all_gather | solution.py:96
  99.2 291.4 %all-reduce.9.cloned.1.call-start = ((), (), s32[]{:S(2)}) async-start(), calls=%async_computation.7 | async-start | bytes 6414336 | tf_op jit(solution)/shard_map/psum | solution.py:154
  102.5 117.8 %copy-start.54 = (f32[768]{0:T(1024)S(1)}, f32[768]{0:T(1024)}, u32[]{:S(2)}) copy-start(f32[768]{0:T(1024)} %get-tuple-element.156) | copy-start | bytes 9220
  102.6 117.8 %copy-start.61 = (f32[768]{0:T(1024)S(1)}, f32[768]{0:T(1024)}, u32[]{:S(2)}) copy-start(f32[768]{0:T(1024)} %get-tuple-element.153) | copy-start | bytes 9220
  230.3 20.0 %copy-start.63 = (f32[768]{0:T(1024)S(1)}, f32[768]{0:T(1024)}, u32[]{:S(2)}) copy-start(f32[768]{0:T(1024)} %get-tuple-element.150) | copy-start | bytes 9220
  250.3 13.9 %copy-start.80 = (bf16[768,768]{1,0:T(8,128)(2,1)S(1)}, bf16[768,768]{1,0:T(8,128)(2,1)}, u32[]{:S(2)}) copy-start(bf16[768,768]{1,0:T(8,128)(2,1)} %all-gather.3.cloned.1.call-done) | copy-start | bytes 3538948
  268.3 225.5 %reduce-scatter.9.cloned.1.call-start = ((), (), s32[]{:S(2)}) async-start(), calls=%async_computation.8 | async-start | bytes 2654208 | tf_op jit(solution)/shard_map/reduce_scatter | solution.py:230
  274.9 220.6 %reduce-scatter.11.cloned.1.call-start = ((), (), s32[]{:S(2)}) async-start(), calls=%async_computation.9 | async-start | bytes 2654208 | tf_op jit(solution)/shard_map/reduce_scatter | solution.py:231
  283.2 214.0 %reduce-scatter.15.cloned.1.call-start = ((), (), s32[]{:S(2)}) async-start(), calls=%async_computation.11 | async-start | bytes 884736
  390.6 12.2 %slice-start = ((s8[6414336]{0:T(1024)(128)(4,1)}), s8[4194304]{0:T(1024)(128)(4,1)S(1)}, s32[]{:S(2)}) async-start(s8[6414336]{0:T(1024)(128)(4,1)} %bitcast.74), calls=%async_computation.13 | async-start | bytes 8388608
  402.9 7.7 copy-start.13
  410.6 13.5 %slice-start.6 = ((s8[9732096]{0:T(1024)(128)(4,1)}), s8[1343488]{0:T(1024)(128)(4,1)S(1)}, s32[]{:S(2)}) async-start(s8[9732096]{0:T(1024)(128)(4,1)} %bitcast.80), calls=%async_computation.19 | async-start | bytes 2686976
  414.1 10.0 %slice-start.7 = ((s8[9732096]{0:T(1024)(128)(4,1)}), s8[4194304]{0:T(1024)(128)(4,1)S(1)}, s32[]{:S(2)}) async-start(s8[9732096]{0:T(1024)(128)(4,1)} %bitcast.80), calls=%async_computation.20 | async-start | bytes 8388608
  414.1 10.0 %slice-start.8 = ((s8[9732096]{0:T(1024)(128)(4,1)}), s8[4194304]{0:T(1024)(128)(4,1)S(1)}, s32[]{:S(2)}) async-start(s8[9732096]{0:T(1024)(128)(4,1)} %bitcast.80), calls=%async_computation.21 | async-start | bytes 8388608
  414.2 10.0 %copy-start.23 = (bf16[8,261,3,64]{1,0,3,2:T(8,128)(2,1)S(1)}, bf16[8,261,3,64]{1,0,3,2:T(8,128)(2,1)}, u32[]{:S(2)}) copy-start(bf16[8,261,3,64]{1,0,3,2:T(8,128)(2,1)} %reshape.222) | copy-start | bytes 2405380
  428.6 10.1 %copy-start.5 = (bf16[8,261,3,64]{1,0,3,2:T(8,128)(2,1)S(1)}, bf16[8,261,3,64]{1,0,3,2:T(8,128)(2,1)}, u32[]{:S(2)}) copy-start(bf16[8,261,3,64]{1,0,3,2:T(8,128)(2,1)} %copy-done.4) | copy-start | bytes 2405380
  445.4 8.1 copy-start.10
  458.8 77.7 %reduce-scatter.13.cloned.1.call-start = ((), (), s32[]{:S(2)}) async-start(), calls=%async_computation.10 | async-start | bytes 2211840
  473.7 238.0 %all-reduce.11.cloned.1.call-start = ((), (), s32[]{:S(2)}) async-start(), calls=%async_computation.12 | async-start | bytes 12828672 | tf_op jit(solution)/shard_map/psum | solution.py:139
  485.3 226.5 %copy-start.39 = (f32[768]{0:T(1024)S(1)}, f32[768]{0:T(1024)}, u32[]{:S(2)}) copy-start(f32[768]{0:T(1024)} %copy-done.38) | copy-start | bytes 9220
  485.3 226.5 %copy-start.41 = (f32[2088]{0:T(1024)S(1)}, f32[2088]{0:T(1024)}, u32[]{:S(2)}) copy-start(f32[2088]{0:T(1024)} %copy-done.40) | copy-start | bytes 25060
  485.3 226.5 %copy-start.43 = (f32[2088]{0:T(1024)S(1)}, f32[2088]{0:T(1024)}, u32[]{:S(2)}) copy-start(f32[2088]{0:T(1024)} %copy-done.42) | copy-start | bytes 25060
  485.3 226.5 %copy-start.50 = (pred[2088]{0:T(1024)(128)(4,1)S(1)}, pred[2088]{0:T(1024)(128)(4,1)}, u32[]{:S(2)}) copy-start(pred[2088]{0:T(1024)(128)(4,1)} %broadcast_in_dim.40) | copy-start | bytes 6268
  485.3 226.5 %copy-start.58 = (f32[768]{0:T(1024)S(1)}, f32[768]{0:T(1024)}, u32[]{:S(2)}) copy-start(f32[768]{0:T(1024)} %get-tuple-element.155) | copy-start | bytes 9220
  493.2 225.3 %copy-start.52 = (f32[2088]{0:T(1024)S(1)}, f32[2088]{0:T(1024)}, u32[]{:S(2)}) copy-start(f32[2088]{0:T(1024)} %copy-done.51) | copy-start | bytes 25060
  493.2 225.3 %slice-start.2 = ((s8[6414336]{0:T(1024)(128)(4,1)}), s8[2220032]{0:T(1024)(128)(4,1)S(1)}, s32[]{:S(2)}) async-start(s8[6414336]{0:T(1024)(128)(4,1)} %bitcast.76), calls=%async_computation.15 | async-start | bytes 4440064
  498.1 39.4 %copy-start.24 = (f32[192,96]{1,0:T(8,128)}, f32[192,96]{1,0:T(8,128)S(1)}, u32[]{:S(2)}) copy-start(f32[192,96]{1,0:T(8,128)S(1)} %copy.179) | copy-start | bytes 221188
  711.8 18.1 %slice-start.4 = ((s8[6414336]{0:T(1024)(128)(4,1)}), s8[4194304]{0:T(1024)(128)(4,1)S(1)}, s32[]{:S(2)}) async-start(s8[6414336]{0:T(1024)(128)(4,1)} %bitcast.78), calls=%async_computation.17 | async-start | bytes 8388608
  718.5 11.3 %slice-start.5 = ((s8[6414336]{0:T(1024)(128)(4,1)}), s8[2220032]{0:T(1024)(128)(4,1)S(1)}, s32[]{:S(2)}) async-start(s8[6414336]{0:T(1024)(128)(4,1)} %bitcast.78), calls=%async_computation.18 | async-start | bytes 4440064
  718.6 11.3 %copy-start.62 = (f32[768]{0:T(1024)S(1)}, f32[768]{0:T(1024)}, u32[]{:S(2)}) copy-start(f32[768]{0:T(1024)} %get-tuple-element.153) | copy-start | bytes 9220
  729.9 7.7 copy-start.66
  729.9 7.7 copy-start.67
  729.9 7.7 copy-start.68
  729.9 7.8 copy-start.69
  729.9 7.8 copy-start.75
  730.0 36.1 %copy-start.37 = (f32[3,96,192]{2,1,0:T(8,128)S(1)}, f32[3,96,192]{2,1,0:T(8,128)}, u32[]{:S(2)}) copy-start(f32[3,96,192]{2,1,0:T(8,128)} %param.29) | copy-start | bytes 663556
  814.0 8.2 copy-start.16
  (52 other events, 254.3 us)
Sparse Core Ops, SparseCore 0:
  96.8 123.4 all-reduce.6
  268.4 122.1 all-reduce.8
  485.5 226.2 all-reduce.10
Sparse Core Ops, SparseCore 1:
  99.8 24.1 all-gather.2
  126.5 23.9 all-gather.4
  275.0 41.3 reduce-scatter.8
  320.1 42.3 reduce-scatter.10
  458.8 33.9 reduce-scatter.14
  496.2 40.1 reduce-scatter.12
where the time goes:
time: 839 us; the launch traced here: 833 us
  waiting for transfers between devices  427 us (51%)
  matrix products  107 us (13%)
  other arithmetic  101 us (12%)
  local copies, waits for them, and re-layouts  87.3 us (10%)
  blocking collectives  86.6 us (10%)
  between operations  23.3 us (3%)
    psum x1, waiting for transfers between devices, per_device(): lax.psum(mlp_part.astype(jnp.bfloat16), 'tensor').astype(jnp.float32)  171 us
    psum x1, waiting for transfers between devices, per_device(): lax.psum(attn_part.astype(jnp.bfloat16), 'tensor').astype(jnp.float32)  111 us
    psum x1, waiting for transfers between devices, per_device(): lax.psum(back_two.astype(jnp.bfloat16), 'tensor').astype(jnp.float32)  107 us
    psum x1, blocking collectives, per_device(): total_squares = lax.psum(local_squares, ('dp', 'tensor'))  38.2 us
    unnamed x11, waiting for transfers between devices  37.8 us
    unnamed x199, local copies, waits for them, and re-layouts  29.8 us
    psum x1, blocking collectives, per_device(): lax.psum((vector_grads, grad_head_bias, grad_fc1_bias), 'dp')  24.5 us
    dot_general x4, matrix products, outer_cols(): lax.dot_general(first_op, second_op, (((1,), (1,)), ((), ())), preferred_...  22.1 us
  transfers between devices with their start and end apart: 9, of which 4 were waited for; matrix products, arithmetic and copies ran while one was open for 19% of the time, Pallas kernels for 0%

commit v1 on v0

--- a/solution.py
+++ b/solution.py
@@ -80,29 +80,63 @@
     fc1_bias_first,
     fc1_bias_second,
 ):
-    crops, seq_len, width = tokens.shape
+    all_crops, seq_len, width = tokens.shape
+    n_dp = lax.axis_size("dp")
+    n_tensor = lax.axis_size("tensor")
+    crops = all_crops // n_tensor
+    first_crop = lax.axis_index("tensor") * crops
     rows_here = crops * seq_len
     scale = HD ** (-0.5)
-    low_shards = (
-        qkv_weight.astype(jnp.bfloat16),
-        proj_weight.astype(jnp.bfloat16),
-        fc1_weight.astype(jnp.bfloat16),
-        fc2_weight.astype(jnp.bfloat16),
-    )
-    qkv_full, proj_full, up_full, down_full = (
-        lax.all_gather(low_shards[0], "dp", axis=1, tiled=True),
-        lax.all_gather(low_shards[1], "dp", axis=1, tiled=True),
-        lax.all_gather(low_shards[2], "dp", axis=0, tiled=True),
-        lax.all_gather(low_shards[3], "dp", axis=1, tiled=True),
-    )
+    both = ("dp", "tensor")
+
+    def gather(shard, dp_axis, tensor_axis):
+        low_shard = shard.astype(jnp.bfloat16)
+        part = lax.all_gather(low_shard, both, axis=0, tiled=False)
+        part = part.reshape((n_dp, n_tensor) + shard.shape)
+        part = jnp.moveaxis(part, 0, dp_axis + 1)
+        part = jnp.moveaxis(part, 0, tensor_axis + (1 if tensor_axis > dp_axis else 0))
+        shape = list(shard.shape)
+        shape[dp_axis] *= n_dp
+        shape[tensor_axis] *= n_tensor
+        return part.reshape(shape)
+
+    def scatter(full, dp_axis, tensor_axis):
+        shape = list(full.shape)
+        low = full.astype(jnp.bfloat16)
+        pieces = []
+        for at, extent in enumerate(shape):
+            if at == dp_axis:
+                pieces += [n_dp, extent // n_dp]
+            elif at == tensor_axis:
+                pieces += [n_tensor, extent // n_tensor]
+            else:
+                pieces += [extent]
+        split = low.reshape(pieces)
+        later = max(dp_axis, tensor_axis)
+        earlier = min(dp_axis, tensor_axis)
+        place = {earlier: earlier, later: later + 1}
+        split = jnp.moveaxis(split, (place[dp_axis], place[tensor_axis]), (0, 1))
+        split = split.reshape((n_dp * n_tensor,) + split.shape[2:])
+        return lax.psum_scatter(split, both, scatter_dimension=0, tiled=False).astype(jnp.float32)
+
+    qkv_full = gather(qkv_weight, 1, 2)
+    proj_full = gather(proj_weight, 1, 0)
+    up_full = gather(fc1_weight, 0, 1)
+    down_full = gather(fc2_weight, 1, 0)
+    head_full = lax.all_gather(head_bias, "tensor", axis=1, tiled=True)
+    fc1_bias_full = lax.all_gather(fc1_bias, "tensor", axis=0, tiled=True)
+    tokens_here = lax.dynamic_slice_in_dim(tokens, first_crop, crops, 0)
+    mask_here = lax.dynamic_slice_in_dim(patch_mask, first_crop, crops, 0)
+    cot_here = lax.dynamic_slice_in_dim(cotangent, first_crop, crops, 0)
+
     head_cols = qkv_full.shape[2]
     heads_here = head_cols // HD
     joined = jnp.concatenate([qkv_full[0], qkv_full[1], qkv_full[2]], axis=1)
-    bias_row = jnp.concatenate([head_bias[0], jnp.zeros((head_cols,), jnp.float32), head_bias[1]])
+    bias_row = jnp.concatenate([head_full[0], jnp.zeros((head_cols,), jnp.float32), head_full[1]])
     chosen = jnp.concatenate(
-        [jnp.zeros((crops, 1 + REG), jnp.bool_), patch_mask == 1], axis=1
+        [jnp.zeros((crops, 1 + REG), jnp.bool_), mask_here == 1], axis=1
     ).reshape(rows_here, 1)
-    inputs = tokens.astype(jnp.float32).reshape(rows_here, width)
+    inputs = tokens_here.astype(jnp.float32).reshape(rows_here, width)
     start = jnp.where(chosen, vectors[8], inputs)
     norm_one = layer_norm(start, vectors[0], vectors[1]).astype(jnp.bfloat16)
 
@@ -125,42 +159,39 @@
         context_low = context.astype(jnp.bfloat16).reshape(rows_here, head_cols)
         return (query, keys_part, values_part, probs, probs_low, context_low)
 
-    def expand(norm_in):
-        hidden = jnp.dot(norm_in, up_full, preferred_element_type=jnp.float32) + fc1_bias
-        return (hidden, gelu_exact(hidden).astype(jnp.bfloat16))
-
     query, keys_part, values_part, probs, probs_low, context_low = attend(norm_one)
     attn_part = jnp.dot(context_low, proj_full, preferred_element_type=jnp.float32)
-    attn = lax.psum(attn_part.astype(jnp.bfloat16), "tensor").astype(jnp.float32) + vectors[3]
+    attn = attn_part + vectors[3]
     middle = start + vectors[2] * attn
     norm_two = layer_norm(middle, vectors[4], vectors[5]).astype(jnp.bfloat16)
-    hidden, active = expand(norm_two)
-    mlp_part = jnp.dot(active, down_full, preferred_element_type=jnp.float32)
-    mlp = lax.psum(mlp_part.astype(jnp.bfloat16), "tensor").astype(jnp.float32) + vectors[7]
-    block_out = (middle + vectors[6] * mlp).astype(jnp.bfloat16).reshape(crops, seq_len, width)
-    cot = cotangent.astype(jnp.float32).reshape(rows_here, width)
-    hidden_again, active_again = expand(norm_two)
+    hidden = jnp.dot(norm_two, up_full, preferred_element_type=jnp.float32) + fc1_bias_full
+    active = gelu_exact(hidden).astype(jnp.bfloat16)
+    mlp = jnp.dot(active, down_full, preferred_element_type=jnp.float32) + vectors[7]
+    block_here = (middle + vectors[6] * mlp).astype(jnp.bfloat16).reshape(crops, seq_len, width)
+    block_out = lax.all_gather(block_here, "tensor", axis=0, tiled=True)
+    cot = cot_here.astype(jnp.float32).reshape(rows_here, width)
     mlp_grad = vectors[6] * cot
     grad_scale_two = jnp.sum(cot * mlp, axis=0)
     grad_bias_out = jnp.sum(mlp_grad, axis=0)
     mlp_grad_low = mlp_grad.astype(jnp.bfloat16)
-    grad_down = inner_rows(active_again, mlp_grad_low)
+    grad_down = inner_rows(active, mlp_grad_low)
+    down_shard = scatter(grad_down, 1, 0)
     grad_active = outer_cols(mlp_grad_low, down_full)
-    gelu_value, gelu_back = jax.vjp(gelu_exact, hidden_again)
+    gelu_value, gelu_back = jax.vjp(gelu_exact, hidden)
     grad_hidden = gelu_back(grad_active)[0].astype(jnp.bfloat16)
     grad_up = inner_rows(norm_two, grad_hidden)
+    up_shard = scatter(grad_up, 0, 1)
     grad_fc1_bias = jnp.sum(grad_hidden.astype(jnp.float32), axis=0)
-    back_two = outer_cols(grad_hidden, up_full)
-    grad_norm_two = lax.psum(back_two.astype(jnp.bfloat16), "tensor").astype(jnp.float32)
+    grad_norm_two = outer_cols(grad_hidden, up_full)
     norm_value, norm_two_back = jax.vjp(layer_norm, middle, vectors[4], vectors[5])
     grad_from_two, grad_gain_two, grad_shift_two = norm_two_back(grad_norm_two)
     grad_middle = cot + grad_from_two
-    query, keys_part, values_part, probs, probs_low, context_low = attend(norm_one)
     attn_grad = vectors[2] * grad_middle
     grad_scale_one = jnp.sum(grad_middle * attn, axis=0)
     grad_bias_proj = jnp.sum(attn_grad, axis=0)
     attn_grad_low = attn_grad.astype(jnp.bfloat16)
     grad_proj = inner_rows(context_low, attn_grad_low)
+    proj_shard = scatter(grad_proj, 1, 0)
     grad_context = (
         outer_cols(attn_grad_low, proj_full)
         .astype(jnp.bfloat16)
@@ -200,17 +231,18 @@
             grad_joined[:, 2 * head_cols :],
         ]
     )
+    qkv_shard = scatter(grad_qkv, 1, 2)
     mixed_sums = jnp.sum(grad_mixed.astype(jnp.float32), axis=0)
     grad_head_bias = jnp.stack([mixed_sums[:head_cols], mixed_sums[2 * head_cols :]])
-    back_one = outer_cols(grad_mixed, joined)
-    grad_norm_one = lax.psum(back_one.astype(jnp.bfloat16), "tensor").astype(jnp.float32)
+    grad_norm_one = outer_cols(grad_mixed, joined)
     norm_one_value, norm_one_back = jax.vjp(layer_norm, start, vectors[0], vectors[1])
     grad_from_one, grad_gain_one, grad_shift_one = norm_one_back(grad_norm_one)
     grad_start = grad_middle + grad_from_one
     grad_token_row = jnp.sum(jnp.where(chosen, grad_start, 0.0), axis=0)
-    tokens_grad = (
+    grad_here = (
         jnp.where(chosen, 0.0, grad_start).astype(jnp.bfloat16).reshape(crops, seq_len, width)
     )
+    tokens_grad = lax.all_gather(grad_here, "tensor", axis=0, tiled=True)
     vector_grads = jnp.stack(
         [
             grad_gain_one,
@@ -224,13 +256,12 @@
             grad_token_row,
         ]
     )
-    qkv_shard, proj_shard, up_shard, down_shard = (
-        lax.psum_scatter(grad_qkv, "dp", scatter_dimension=1, tiled=True),
-        lax.psum_scatter(grad_proj, "dp", scatter_dimension=1, tiled=True),
-        lax.psum_scatter(grad_up, "dp", scatter_dimension=0, tiled=True),
-        lax.psum_scatter(grad_down, "dp", scatter_dimension=1, tiled=True),
-    )
-    vector_sum, head_sum, fc1b_sum = lax.psum((vector_grads, grad_head_bias, grad_fc1_bias), "dp")
+    vector_sum, head_all, fc1b_all = lax.psum((vector_grads, grad_head_bias, grad_fc1_bias), both)
+    tensor_at = lax.axis_index("tensor")
+    head_len = head_bias.shape[1]
+    fc1b_len = fc1_bias.shape[0]
+    head_sum = lax.dynamic_slice_in_dim(head_all, tensor_at * head_len, head_len, 1)
+    fc1b_sum = lax.dynamic_slice_in_dim(fc1b_all, tensor_at * fc1b_len, fc1b_len, 0)
     first_data = (lax.axis_index("dp") == 0).astype(jnp.float32)
     first_tensor = (lax.axis_index("tensor") == 0).astype(jnp.float32)
     local_squares = (

time: 839 us -> 995 us (1.19)
  local copies, waits for them, and re-layouts: 87.3 us -> 186 us
  waiting for transfers between devices: 427 us -> 507 us
  other arithmetic: 101 us -> 61.3 us
  blocking collectives: 86.6 us -> 105 us
    psum x3 -> x0, waiting for transfers between devices: 389 us -> none  [the longest x1 171 us: per_device(): lax.psum(mlp_part.astype(jnp.bfloat16), 'tensor').astype(jnp.float32)]
    reduce_scatter x2 -> x4, waiting for transfers between devices: 0.01 us -> 266 us  [scatter(): lax.psum_scatter(split, both, scatter_dimension=0, tiled=False)]
    all_gather x2 -> x6, waiting for transfers between devices: 0.03 us -> 241 us  [the longest x4 115 us: gather(): part = lax.all_gather(low_shard, both, axis=0, tiled=False)]
    reshape x2 -> x11, local copies, waits for them, and re-layouts: 13.3 us -> 56.6 us  [the longest x5 27.3 us: gather(): part = part.reshape((n_dp, n_tensor) + shard.shape)]
    unnamed x11 -> x10, waiting for transfers between devices: 37.8 us -> 0.16 us
    reduce_sum x4 -> x1, other arithmetic: 30.1 us -> 0.76 us  [layer_norm(): centred = values - middle_val]
    dot_general x3 -> x2, matrix products: 28.6 us -> 11.2 us  [the longest x1 8.42 us: per_device(): jnp.dot(active, down_full, preferred_element_type=jnp.float32) + vectors[7]]
    transpose x0 -> x4, local copies, waits for them, and re-layouts: none -> 15.5 us  [scatter(): split = jnp.moveaxis(split, (place[dp_axis], place[tensor_axis]), (0, 1))]
  transfers between devices with their start and end apart: 9 -> 10, of which waited for: 4 -> 8; matrix products, arithmetic and copies ran while one was open for 19% -> 24% of each run, Pallas kernels for 0% -> 0%
where the time goes in v1:
time: 995 us; the launch traced here: 986 us
  waiting for transfers between devices  507 us (51%)
  local copies, waits for them, and re-layouts  186 us (19%)
  blocking collectives  105 us (11%)
  matrix products  103 us (10%)
  other arithmetic  61.3 us (6%)
  between operations  22.1 us (2%)
    reduce_scatter x4, waiting for transfers between devices, scatter(): lax.psum_scatter(split, both, scatter_dimension=0, tiled=False)  266 us
    all_gather x4, waiting for transfers between devices, gather(): part = lax.all_gather(low_shard, both, axis=0, tiled=False)  115 us
    all_gather x1, waiting for transfers between devices, per_device(): tokens_grad = lax.all_gather(grad_here, 'tensor', axis=0, tiled=True)  63.3 us
    all_gather x1, waiting for transfers between devices, per_device(): block_out = lax.all_gather(block_here, 'tensor', axis=0, tiled=True)  63 us
    psum x1, blocking collectives, per_device(): lax.psum((vector_grads, grad_head_bias, grad_fc1_bias), both)  39.7 us
    psum x1, blocking collectives, per_device(): total_squares = lax.psum(local_squares, ('dp', 'tensor'))  38.9 us
    dot_general x4, matrix products, outer_cols(): lax.dot_general(first_op, second_op, (((1,), (1,)), ((), ())), preferred_...  31.5 us
    reshape x5, local copies, waits for them, and re-layouts, gather(): part = part.reshape((n_dp, n_tensor) + shard.shape)  27.3 us
  transfers between devices with their start and end apart: 10, of which 8 were waited for; matrix products, arithmetic and copies ran while one was open for 24% of the time, Pallas kernels for 0%

profile of v1, /device:TPU:0, one launch (start us, length us, event | category | flops | bytes accessed | tf_op | source)
XLA Modules:
  0.0 985.7 jit_solution(2886899876894901889)
XLA Ops:
  15.8 13.7 %all-gather.4 = f32[4,192,2]{1,2,0:T(2,128)S(1)} all-gather(f32[1,192,2]{1,2,0:T(2,128)} %bitcast.163), channel_id=1, replica_groups=mesh['dp'=8,'tensor'=4] {'tensor'}, dimensions={0}, use_global_device_ids=true | all-gather | bytes 7680 | tf_op jit(solution)/shard_map/all_gather | solution.py:126
  31.3 5.2 fusion.29
  36.5 5.5 multiply_reduce_fusion.9
  42.3 4.3 dynamic-slice_convert_fusion
  55.7 13.0 %all-gather.5 = f32[4,1,768]{2,1,0:T(1,128)S(1)} all-gather(f32[1,1,768]{2,1,0:T(1,128)S(1)} %reshape.332), channel_id=1, replica_groups=mesh['dp'=8,'tensor'=4] {'tensor'}, dimensions={0}, use_global_device_ids=true | all-gather | bytes 15360 | tf_op jit(solution)/shard_map/all_gather | solution.py:127
  74.1 61.1 %all-gather.17.cloned.1.call-done = bf16[96,96,192]{2,1,0:T(8,128)(2,1)} async-done(((bf16[3,96,192]{2,1,0:T(8,128)(2,1)}), bf16[96,96,192]{2,1,0:T(8,128)(2,1)}) %all-gather.17.cloned.1.call-update) | async-done | bytes 3538960 | tf_op jit(solution)/shard_map/all_gather | solution.py:94
  135.1 7.1 copy.189
  142.2 4.3 fusion.66
  150.4 3.8 squeeze.20
  168.0 4.1 reshape.335
  172.0 4.0 copy.194
  176.0 3.8 reshape.334
  179.9 4.4 copy.196
  184.3 8.4 fusion.70
  192.6 5.5 fusion.24
  205.0 6.2 copy.200
  214.4 53.2 %all-gather.23.cloned.1.call-done = bf16[24576,96]{0,1:T(8,128)(2,1)} async-done(((bf16[768,96]{0,1:T(8,128)(2,1)}), bf16[24576,96]{0,1:T(8,128)(2,1)}) %all-gather.23.cloned.1.call-update) | async-done | bytes 4718608 | tf_op jit(solution)/shard_map/all_gather | solution.py:94
  267.6 7.5 reshape.302
  275.1 4.1 copy.201
  283.2 19.6 %convert_reduce_fusion = (f32[3072]{0:T(1024)S(1)}, bf16[522,3072]{1,0:T(8,128)(2,1)S(1)}, f32[522,3072]{1,0:T(8,128)S(1)}) fusion(f32[522,3072]{1,0:T(8,128)S(1)} %fusion.50, f32[3072]{0:T(1024)S(1)} %bitcast.160, bf16[522,768]{1,0:T(8,128)(2,1)S(1)} %copy-done.28, bf16[3072,768]{0,1:T(8,128)(2,1)S(1)} %bitcast.151), kind=kOutput, calls=%fused_computation.8 | convolution fusion | flops 2583370752 | bytes 21580800 | tf_op jit(solution)/shard_map/dot_general | solution.py:38
  302.8 4.7 multiply_reduce_fusion.3
  311.0 8.4 multiply_reduce_fusion.2
  330.7 7.2 fusion.21
  338.0 5.1 multiply_reduce_fusion
  343.0 10.2 %multiply_convert_fusion = bf16[2,12,261,261]{2,3,1,0:T(8,128)(2,1)} fusion(f32[2,12,261,261]{2,3,1,0:T(8,128)} %get-tuple-element.220, f32[2,12,261]{2,1,0:T(8,128)S(1)} %get-tuple-element.219, f32[2,12,261,261]{2,3,1,0:T(8,128)} %get-tuple-element.216, f32[2,12,261]{2,1,0:T(8,128)S(1)} %get-tuple-element.215), kind=kLoop, calls=%fused_computation.1 | loop fusion | flops 6539616 | bytes 16399152 | tf_op jit(solution)/shard_map/convert_element_type | solution.py:204
  353.3 4.5 fusion.28
  368.4 4.0 reshape.309
  382.5 4.0 convolution_convert_fusion.2
  391.9 4.4 stack.45
  396.3 4.6 stack.44
  400.9 5.4 maximum_bitcast_fusion
  411.9 7.8 convolution_convert_fusion.1
  419.7 9.8 reshape.314
  429.5 5.4 copy.217
  436.3 7.6 convolution_convert_fusion
  444.0 6.7 copy.218
  450.6 9.7 reshape.316
  460.4 5.5 copy.219
  466.1 5.5 multiply_reduce_fusion.5
  478.2 39.7 %all-reduce.1 = (f32[2,768]{1,0:T(2,128)S(1)}, f32[3072]{0:T(1024)S(1)}, f32[9,768]{1,0:T(8,128)S(1)}) all-reduce(f32[2,768]{1,0:T(2,128)S(1)} %pad_maximum_fusion.1, f32[3072]{0:T(1024)S(1)} %get-tuple-element.188, f32[9,768]{1,0:T(8,128)S(1)} %stack.55), channel_id=1, replica_groups=mesh['dp'=8,'tensor'=4] {'dp','tensor'}, use_global_device_ids=true, to_apply=%region_20.21 | all-reduce | flops 11520 | bytes 92160 | tf_op jit(solution)/shard_map/psum | solution.py:259
  523.4 48.6 %reduce-scatter.5.cloned.1.call-done = bf16[1,3,96,192]{3,2,1,0:T(8,128)(2,1)} async-done(((bf16[32,3,96,192]{3,2,1,0:T(8,128)(2,1)}), bf16[1,3,96,192]{3,2,1,0:T(8,128)(2,1)}) %reduce-scatter.5.cloned.1.call-update) | async-done | bytes 110608 | tf_op jit(solution)/shard_map/reduce_scatter | solution.py:120
  574.9 63.0 %all-gather.13.cloned.1.call-done = bf16[8,261,768]{2,1,0:T(8,128)(2,1)} async-done(((bf16[2,261,768]{2,1,0:T(8,128)(2,1)}), bf16[8,261,768]{2,1,0:T(8,128)(2,1)}) %all-gather.13.cloned.1.call-update) | async-done | bytes 3207184 | tf_op jit(solution)/shard_map/all_gather | solution.py:171
  637.8 4.2 copy.220
  642.1 107.8 %reduce-scatter.9.cloned.1.call-done = bf16[1,96,768]{2,1,0:T(8,128)(2,1)} async-done(((bf16[32,96,768]{2,1,0:T(8,128)(2,1)}), bf16[1,96,768]{2,1,0:T(8,128)(2,1)}) %reduce-scatter.9.cloned.1.call-update) | async-done | bytes 147472 | tf_op jit(solution)/shard_map/reduce_scatter | solution.py:120
  752.1 109.4 %reduce-scatter.11.cloned.1.call-done = bf16[1,768,96]{1,2,0:T(8,128)(2,1)} async-done(((bf16[32,768,96]{1,2,0:T(8,128)(2,1)}), bf16[1,768,96]{1,2,0:T(8,128)(2,1)}) %reduce-scatter.11.cloned.1.call-update) | async-done | bytes 147472 | tf_op jit(solution)/shard_map/reduce_scatter | solution.py:120
  863.9 63.3 %all-gather.15.cloned.1.call-done = bf16[8,261,768]{2,1,0:T(8,128)(2,1)} async-done(((bf16[2,261,768]{2,1,0:T(8,128)(2,1)}), bf16[8,261,768]{2,1,0:T(8,128)(2,1)}) %all-gather.15.cloned.1.call-update) | async-done | bytes 3207184 | tf_op jit(solution)/shard_map/all_gather | solution.py:245
  927.2 4.2 copy.221
  931.5 38.9 %psum.31 = f32[]{:T(128)} all-reduce(f32[]{:T(128)S(6)} %add.277), channel_id=1, replica_groups=mesh['dp'=8,'tensor'=4] {'dp','tensor'}, use_global_device_ids=true, to_apply=%region_36.37 | all-reduce | flops 1 | bytes 8 | tf_op jit(solution)/shard_map/psum | solution.py:275
  (309 shorter events, 125.2 us)
Async XLA Ops:
  7.2 62.1 %all-gather.19.cloned.1.call-start = ((), (), s32[]{:S(2)}) async-start(), calls=%async_computation.11 | async-start | bytes 1622016 | tf_op jit(solution)/shard_map/all_gather | solution.py:94
  8.8 126.3 %all-gather.17.cloned.1.call-start = ((), (), s32[]{:S(2)}) async-start(), calls=%async_computation.10 | async-start | bytes 4866048 | tf_op jit(solution)/shard_map/all_gather | solution.py:94
  10.5 194.5 %all-gather.21.cloned.1.call-start = ((), (), s32[]{:S(2)}) async-start(), calls=%async_computation.12 | async-start | bytes 4866048 | tf_op jit(solution)/shard_map/all_gather | solution.py:94
  12.2 255.3 %all-gather.23.cloned.1.call-start = ((), (), s32[]{:S(2)}) async-start(), calls=%async_computation.13 | async-start | bytes 4866048 | tf_op jit(solution)/shard_map/all_gather | solution.py:94
  13.9 508.0 %reduce-scatter.7.cloned.1.call-start = ((), (), s32[]{:S(2)}) async-start(), calls=%async_computation.7 | async-start | bytes 1622016 | tf_op jit(solution)/shard_map/reduce_scatter | solution.py:120
  14.9 186.1 %copy-start.62 = (pred[522]{0:T(1024)(128)(4,1)}, pred[522]{0:T(1024)(128)(4,1)S(1)}, u32[]{:S(2)}) copy-start(pred[522]{0:T(1024)(128)(4,1)S(1)} %broadcast_in_dim.61) | copy-start | bytes 1570
  31.2 18.4 %copy-start.52 = (f32[768]{0:T(1024)}, f32[768]{0:T(1024)S(1)}, u32[]{:S(2)}) copy-start(f32[768]{0:T(1024)S(1)} %get-tuple-element.149) | copy-start | bytes 9220
  31.2 127.2 %copy-start.56 = (f32[768]{0:T(1024)}, f32[768]{0:T(1024)S(1)}, u32[]{:S(2)}) copy-start(f32[768]{0:T(1024)S(1)} %get-tuple-element.154) | copy-start | bytes 9220
  31.2 127.2 %copy-start.69 = (f32[768]{0:T(1024)}, f32[768]{0:T(1024)S(1)}, u32[]{:S(2)}) copy-start(f32[768]{0:T(1024)S(1)} %get-tuple-element.153) | copy-start | bytes 9220
  31.2 169.7 %copy-start.42 = (f32[768]{0:T(1024)}, f32[768]{0:T(1024)S(1)}, u32[]{:S(2)}) copy-start(f32[768]{0:T(1024)S(1)} %get-tuple-element.156) | copy-start | bytes 9220
  31.2 169.7 %copy-start.48 = (f32[768]{0:T(1024)}, f32[768]{0:T(1024)S(1)}, u32[]{:S(2)}) copy-start(f32[768]{0:T(1024)S(1)} %get-tuple-element.152) | copy-start | bytes 9220
  31.2 249.0 %copy-start.65 = (f32[768]{0:T(1024)}, f32[768]{0:T(1024)S(1)}, u32[]{:S(2)}) copy-start(f32[768]{0:T(1024)S(1)} %get-tuple-element.150) | copy-start | bytes 9220
  31.3 279.7 %copy-start.67 = (f32[768]{0:T(1024)}, f32[768]{0:T(1024)S(1)}, u32[]{:S(2)}) copy-start(f32[768]{0:T(1024)S(1)} %get-tuple-element.151) | copy-start | bytes 9220
  42.2 116.2 %copy-start.58 = (f32[522]{0:T(1024)}, f32[522]{0:T(1024)S(1)}, u32[]{:S(2)}) copy-start(f32[522]{0:T(1024)S(1)} %div.117) | copy-start | bytes 6268
  42.3 116.1 %copy-start.60 = (f32[522]{0:T(1024)}, f32[522]{0:T(1024)S(1)}, u32[]{:S(2)}) copy-start(f32[522]{0:T(1024)S(1)} %rsqrt.22) | copy-start | bytes 6268
  49.6 151.4 %copy-start.1 = (f32[522,768]{1,0:T(8,128)}, f32[522,768]{1,0:T(8,128)S(1)}, u32[]{:S(2)}) copy-start(f32[522,768]{1,0:T(8,128)S(1)} %reshape.292) | copy-start | bytes 4810756
  167.9 16.3 %copy-start.12 = (bf16[2,261,12,64]{1,3,2,0:T(8,128)(2,1)}, bf16[2,261,12,64]{1,3,2,0:T(8,128)(2,1)S(1)}, u32[]{:S(2)}) copy-start(bf16[2,261,12,64]{1,3,2,0:T(8,128)(2,1)S(1)} %copy.195) | copy-start | bytes 2405380
  204.6 106.3 %copy-start.8 = (f32[522,768]{1,0:T(8,128)}, f32[522,768]{1,0:T(8,128)S(1)}, u32[]{:S(2)}) copy-start(f32[522,768]{1,0:T(8,128)S(1)} %get-tuple-element.196) | copy-start | bytes 4810756
  205.0 106.0 %copy-start.75 = (f32[522]{0:T(1024)}, f32[522]{0:T(1024)S(1)}, u32[]{:S(2)}) copy-start(f32[522]{0:T(1024)S(1)} %fusion.47) | copy-start | bytes 6268
  280.3 22.5 %slice-start.5 = ((s8[4718592]{0:T(1024)(128)(4,1)}), s8[4194304]{0:T(1024)(128)(4,1)S(1)}, s32[]{:S(2)}) async-start(s8[4718592]{0:T(1024)(128)(4,1)} %bitcast.156), calls=%async_computation.19 | async-start | bytes 8388608
  283.2 19.7 %slice-start.6 = ((s8[4718592]{0:T(1024)(128)(4,1)}), s8[524288]{0:T(1024)(128)(4,1)S(1)}, s32[]{:S(2)}) async-start(s8[4718592]{0:T(1024)(128)(4,1)} %bitcast.156), calls=%async_computation.20 | async-start | bytes 1048576
  324.6 13.3 %slice-start = ((s8[9732096]{0:T(1024)(128)(4,1)}), s8[1343488]{0:T(1024)(128)(4,1)S(1)}, s32[]{:S(2)}) async-start(s8[9732096]{0:T(1024)(128)(4,1)} %bitcast.144), calls=%async_computation.14 | async-start | bytes 2686976
  364.8 207.2 %reduce-scatter.5.cloned.1.call-start = ((), (), s32[]{:S(2)}) async-start(), calls=%async_computation.6 | async-start | bytes 4866048 | tf_op jit(solution)/shard_map/reduce_scatter | solution.py:120
  409.4 228.4 %all-gather.13.cloned.1.call-start = ((), (), s32[]{:S(2)}) async-start(), calls=%async_computation.4 | async-start | bytes 4055040 | tf_op jit(solution)/shard_map/all_gather | solution.py:171
  411.8 338.0 %reduce-scatter.9.cloned.1.call-start = ((), (), s32[]{:S(2)}) async-start(), calls=%async_computation.8 | async-start | bytes 4866048 | tf_op jit(solution)/shard_map/reduce_scatter | solution.py:120
  434.9 426.5 %reduce-scatter.11.cloned.1.call-start = ((), (), s32[]{:S(2)}) async-start(), calls=%async_computation.9 | async-start | bytes 4866048 | tf_op jit(solution)/shard_map/reduce_scatter | solution.py:120
  465.9 461.4 %all-gather.15.cloned.1.call-start = ((), (), s32[]{:S(2)}) async-start(), calls=%async_computation.5 | async-start | bytes 4055040 | tf_op jit(solution)/shard_map/all_gather | solution.py:245
  863.7 107.4 %copy-start.55 = (f32[768]{0:T(1024)S(1)}, f32[768]{0:T(1024)}, u32[]{:S(2)}) copy-start(f32[768]{0:T(1024)} %param.45) | copy-start | bytes 9220
  863.7 107.4 %copy-start.77 = (f32[768]{0:T(1024)S(1)}, f32[768]{0:T(1024)}, u32[]{:S(2)}) copy-start(f32[768]{0:T(1024)} %param.46) | copy-start | bytes 9220
  863.8 107.4 %copy-start.78 = (f32[768]{0:T(1024)S(1)}, f32[768]{0:T(1024)}, u32[]{:S(2)}) copy-start(f32[768]{0:T(1024)} %param.47) | copy-start | bytes 9220
  863.8 108.1 %copy-start.64 = (f32[2,192]{1,0:T(2,128)S(1)}, f32[2,192]{1,0:T(2,128)}, u32[]{:S(2)}) copy-start(f32[2,192]{1,0:T(2,128)} %param.42) | copy-start | bytes 4612
  863.8 108.0 %copy-start.79 = (f32[2,192]{1,0:T(2,128)S(1)}, f32[2,192]{1,0:T(2,128)}, u32[]{:S(2)}) copy-start(f32[2,192]{1,0:T(2,128)} %param.43) | copy-start | bytes 4612
  863.8 108.0 %copy-start.80 = (f32[2,192]{1,0:T(2,128)S(1)}, f32[2,192]{1,0:T(2,128)}, u32[]{:S(2)}) copy-start(f32[2,192]{1,0:T(2,128)} %param.44) | copy-start | bytes 4612
  863.8 108.7 %copy-start.41 = (f32[9,768]{1,0:T(8,128)S(1)}, f32[9,768]{1,0:T(8,128)}, u32[]{:S(2)}) copy-start(f32[9,768]{1,0:T(8,128)} %param.39) | copy-start | bytes 82948
  863.8 108.7 %copy-start.46 = (f32[9,768]{1,0:T(8,128)S(1)}, f32[9,768]{1,0:T(8,128)}, u32[]{:S(2)}) copy-start(f32[9,768]{1,0:T(8,128)} %param.40) | copy-start | bytes 82948
  863.8 108.7 %copy-start.47 = (f32[9,768]{1,0:T(8,128)S(1)}, f32[9,768]{1,0:T(8,128)}, u32[]{:S(2)}) copy-start(f32[9,768]{1,0:T(8,128)} %param.41) | copy-start | bytes 82948
  863.8 109.4 %copy-start.32 = (f32[192,96]{1,0:T(8,128)S(1)}, f32[192,96]{1,0:T(8,128)}, u32[]{:S(2)}) copy-start(f32[192,96]{1,0:T(8,128)} %param.30) | copy-start | bytes 221188
  863.9 109.4 %copy-start.40 = (bf16[1,192,96]{2,1,0:T(8,128)(2,1)S(1)}, bf16[1,192,96]{2,1,0:T(8,128)(2,1)}, u32[]{:S(2)}) copy-start(bf16[1,192,96]{2,1,0:T(8,128)(2,1)} %reduce-scatter.7.cloned.1.call-done) | copy-start | bytes 110596
  863.9 109.3 %copy-start.44 = (f32[192,96]{1,0:T(8,128)S(1)}, f32[192,96]{1,0:T(8,128)}, u32[]{:S(2)}) copy-start(f32[192,96]{1,0:T(8,128)} %param.31) | copy-start | bytes 221188
  863.9 109.3 %copy-start.45 = (f32[192,96]{1,0:T(8,128)S(1)}, f32[192,96]{1,0:T(8,128)}, u32[]{:S(2)}) copy-start(f32[192,96]{1,0:T(8,128)} %param.32) | copy-start | bytes 221188
  863.9 110.2 %copy-start.23 = (f32[768,96]{0,1:T(8,128)S(1)}, f32[768,96]{0,1:T(8,128)}, u32[]{:S(2)}) copy-start(f32[768,96]{0,1:T(8,128)} %param.36) | copy-start | bytes 884740
  863.9 110.1 %copy-start.31 = (bf16[1,768,96]{1,2,0:T(8,128)(2,1)S(1)}, bf16[1,768,96]{1,2,0:T(8,128)(2,1)}, u32[]{:S(2)}) copy-start(bf16[1,768,96]{1,2,0:T(8,128)(2,1)} %reduce-scatter.11.cloned.1.call-done) | copy-start | bytes 442372
  863.9 110.1 %copy-start.34 = (f32[768,96]{0,1:T(8,128)S(1)}, f32[768,96]{0,1:T(8,128)}, u32[]{:S(2)}) copy-start(f32[768,96]{0,1:T(8,128)} %param.37) | copy-start | bytes 884740
  863.9 110.1 %copy-start.35 = (f32[768,96]{0,1:T(8,128)S(1)}, f32[768,96]{0,1:T(8,128)}, u32[]{:S(2)}) copy-start(f32[768,96]{0,1:T(8,128)} %param.38) | copy-start | bytes 884740
  931.5 43.7 %copy-start.24 = (f32[96,768]{1,0:T(8,128)S(1)}, f32[96,768]{1,0:T(8,128)}, u32[]{:S(2)}) copy-start(f32[96,768]{1,0:T(8,128)} %param.33) | copy-start | bytes 884740
  931.5 43.7 %copy-start.30 = (bf16[1,96,768]{2,1,0:T(8,128)(2,1)S(1)}, bf16[1,96,768]{2,1,0:T(8,128)(2,1)}, u32[]{:S(2)}) copy-start(bf16[1,96,768]{2,1,0:T(8,128)(2,1)} %reduce-scatter.9.cloned.1.call-done) | copy-start | bytes 442372
  931.5 43.7 %copy-start.36 = (f32[96,768]{1,0:T(8,128)S(1)}, f32[96,768]{1,0:T(8,128)}, u32[]{:S(2)}) copy-start(f32[96,768]{1,0:T(8,128)} %param.34) | copy-start | bytes 884740
  931.5 43.7 %copy-start.37 = (f32[96,768]{1,0:T(8,128)S(1)}, f32[96,768]{1,0:T(8,128)}, u32[]{:S(2)}) copy-start(f32[96,768]{1,0:T(8,128)} %param.35) | copy-start | bytes 884740
  (51 other events, 165.7 us)
Sparse Core Ops, SparseCore 0:
  11.5 57.7 all-gather.18
  72.7 62.3 all-gather.16
  138.5 62.3 all-gather.20
  204.2 63.2 all-gather.22
  364.9 95.1 reduce-scatter.6
  465.4 106.5 reduce-scatter.4
  573.6 64.1 all-gather.12
  644.2 105.6 reduce-scatter.8
  755.3 106.0 reduce-scatter.10
  863.0 64.2 all-gather.14

commit v2 on v0

v2 whole, which is shorter than its diff:
```python
import functools

import jax
import jax.numpy as jnp
from jax import lax
from jax.experimental import pallas as pl
from jax.experimental.pallas import tpu as pltpu
from jax.sharding import PartitionSpec as P

HD = 64
REG = 4
STEP = 10
GROUP = 8
PIECES = 3
CHUNK = 16

norm_eps = 1e-06
clip_norm = 1.0
rate_matrix = 0.04
rate_vector = 0.2
decay_matrix = 0.04
moment_decay = 0.5
adam_eps = 1e-08

def square_sum(values):
    return jnp.sum(values * values)


def adam_step(weight, first, second, grad, rate, decay):
    first_new = moment_decay * first + (1.0 - moment_decay) * grad
    second_new = moment_decay * second + (1.0 - moment_decay) * grad * grad
    correct = 1.0 - moment_decay**STEP
    weight_new = weight - rate * (
        first_new / correct / (jnp.sqrt(second_new / correct) + adam_eps) + decay * weight
    )
    return (weight_new, first_new, second_new)


def nn(a, b):
    return lax.dot_general(a, b, (((1,), (0,)), ((), ())), preferred_element_type=jnp.float32)


def nt(a, b):
    return lax.dot_general(a, b, (((1,), (1,)), ((), ())), preferred_element_type=jnp.float32)


def tn(a, b):
    return lax.dot_general(a, b, (((0,), (0,)), ((), ())), preferred_element_type=jnp.float32)


def low(values):
    return values.astype(jnp.bfloat16)


def wide(values):
    return values.astype(jnp.float32)


def fold(values):
    return values[:8] + values[8:]


def remote(src, dst, send, recv, device):
    return pltpu.make_async_remote_copy(
        src_ref=src,
        dst_ref=dst,
        send_sem=send,
        recv_sem=recv,
        device_id=device,
        device_id_type=pl.DeviceIdType.MESH,
    )


def block_kernel(
    dims,
    pack,
    x_in,
    cot_in,
    mask_in,
    vec,
    mix_bias,
    up_bias,
    out_block,
    out_tokens,
    shard_out,
    vec_out,
    mix_out,
    up_out,
    store,
    norm_one,
    turned_one,
    mixed,
    probs,
    context,
    attn_sum,
    middle,
    norm_two,
    turned_two,
    mlp_grad,
    turned_mlp,
    active,
    slope,
    wide_one,
    wide_two,
    grad_mid,
    attn_grad,
    turned_attn,
    gmixed,
    result,
    core_ring,
    diag_ring,
    dir_ring,
    line_in,
    z_send,
    z_recv,
    xy_send,
    xy_recv,
    diag_send,
    diag_recv,
    core_send,
    core_recv,
    rc_send,
    rc_recv,
    rd_send,
    rd_recv,
    rx_send,
    rx_recv,
    rz_send,
    rz_recv,
    ob_send,
    ob_recv,
    og_send,
    og_recv,
    own_sem,
):
    n_dp, n_t, seq, pad_seq, crops, heads = dims
    stride = n_dp // GROUP
    rows = crops * pad_seq
    unit = pack.shape[1]
    half = unit // 2
    width = pack.shape[2]
    head_cols = heads * HD
    mix_cols = 3 * head_cols
    scale = HD ** (-0.5)
    n_chunks = rows // CHUNK

    d = lax.axis_index("dp")
    z = lax.axis_index("tensor")
    place = d // stride
    c = place % 2
    yx = place // 2
    xbit = yx % 2
    ybit = yx // 2
    yx_x = yx + 1 - 2 * xbit
    yx_y = yx + 2 - 4 * ybit
    yx_d = 3 - yx
    to_core = (d + (1 - 2 * c) * stride, z)
    to_x = (d + (1 - 2 * xbit) * 2 * stride, z)
    to_y = (d + (1 - 2 * ybit) * 4 * stride, z)

    def to_line(k):
        return (d, (z + k) % n_t)

    barrier = pltpu.get_barrier_semaphore()
    peers = [to_core, to_x, to_y] + [to_line(k) for k in range(1, n_t)]
    for peer in peers:
        pl.semaphore_signal(
            barrier, inc=1, device_id=peer, device_id_type=pl.DeviceIdType.MESH
        )
    pl.semaphore_wait(barrier, len(peers))

    n_jobs = PIECES * n_t

    def z_copy(m, k):
        src = store.at[m, z, yx, c]
        return remote(src, src, z_send.at[m, k - 1], z_recv.at[m, k - 1], to_line(k))

    def block_at(i, which):
        m, k = i // n_t, i % n_t
        return store.at[m, (z + n_t - k) % n_t, which, c]

    def direct(i, axis):
        src = block_at(i, yx)
        return remote(
            src, src, xy_send.at[i, axis], xy_recv.at[i, axis], to_x if axis == 0 else to_y
        )

    def diagonal(i, axis):
        which = yx_x if axis == 1 else yx_y
        src = block_at(i, which).at[pl.ds(0 if axis == 1 else half, half)]
        return remote(
            src, src, diag_send.at[i, axis], diag_recv.at[i, axis], to_x if axis == 0 else to_y
        )

    def across(i, slot):
        src = block_at(i, (yx, yx_x, yx_y, yx_d)[slot])
        return remote(src, src, core_send.at[i, slot], core_recv.at[i, slot], to_core)

    def start_line(m):
        for k in range(1, n_t):
            z_copy(m, k).start()

    def gather_tick(i):
        @pl.when(jnp.logical_and(i >= 2, i - 2 < n_jobs))
        def _():
            j = jnp.maximum(i - 2, 0)
            diagonal(j, 0).wait_recv()
            diagonal(j, 1).wait_recv()
            across(j, 3).start()

        @pl.when(jnp.logical_and(i >= 1, i - 1 < n_jobs))
        def _():
            j = jnp.maximum(i - 1, 0)
            direct(j, 0).wait_recv()
            diagonal(j, 1).start()
            direct(j, 1).wait_recv()
            diagonal(j, 0).start()
            across(j, 1).start()
            across(j, 2).start()

        @pl.when(i < n_jobs)
        def _():
            j = jnp.minimum(i, n_jobs - 1)
            m, k = j // n_t, j % n_t

            @pl.when(k > 0)
            def _():
                z_copy(m, jnp.maximum(k, 1)).wait_recv()

            direct(j, 0).start()
            direct(j, 1).start()
            across(j, 0).start()

            @pl.when(jnp.logical_and(k == n_t - 1, m < PIECES - 1))
            def _():
                start_line(m + 1)

    def gather_end(m):
        def body(k, carry):
            for slot in range(4):
                across(m * n_t + k, slot).wait_recv()
            return carry

        lax.fori_loop(0, n_t, body, 0)

    def gather_sent(m):
        for k in range(1, n_t):
            z_copy(m, k).wait_send()

        def body(k, carry):
            i = m * n_t + k
            for axis in range(2):
                direct(i, axis).wait_send()
                diagonal(i, axis).wait_send()
            for slot in range(4):
                across(i, slot).wait_send()
            return carry

        lax.fori_loop(0, n_t, body, 0)

    def job_slot(j):
        return 3 - j // n_t, j % n_t

    def rs_core(j):
        slot, t = job_slot(j)
        return remote(
            store.at[slot, t, :, 1 - c],
            core_ring.at[j % 2],
            rc_send.at[j],
            rc_recv.at[j],
            to_core,
        )

    def rs_diag(j, axis):
        slot, t = job_slot(j)
        return remote(
            store.at[slot, t, yx_d, c, pl.ds(axis * half, half)],
            diag_ring.at[j % 2, axis],
            rd_send.at[j, axis],
            rd_recv.at[j, axis],
            to_x if axis == 0 else to_y,
        )

    def rs_direct(j, axis):
        slot, t = job_slot(j)
        return remote(
            store.at[slot, t, yx_x if axis == 0 else yx_y, c],
            dir_ring.at[j % 2, axis],
            rx_send.at[j, axis],
            rx_recv.at[j, axis],
            to_x if axis == 0 else to_y,
        )

    def rs_line_out(j):
        slot, t = job_slot(j)
        k = (z + n_t - t) % n_t
        m = PIECES - 1 - j // n_t
        return remote(
            store.at[slot, t, yx, c],
            line_in.at[m, jnp.maximum(k, 1) - 1],
            rz_send.at[j],
            rz_recv.at[m, jnp.maximum(k, 1) - 1],
            (d, t),
        )

    def rs_line_in(m, k):
        return remote(
            line_in.at[m, k - 1],
            line_in.at[m, k - 1],
            rz_send.at[0],
            rz_recv.at[m, k - 1],
            to_line(1),
        )

    def reduce_stage(stage, j):
        slot, t = job_slot(j)
        if stage == 0:
            rs_core(j).start()
        if stage == 1:
            rs_core(j).wait_recv()
            per = unit // CHUNK

            def body(s, carry):
                at = pl.ds(pl.multiple_of((s % per) * CHUNK, CHUNK), CHUNK)
                which = s // per
                store[slot, t, which, c, at] = low(
                    wide(store[slot, t, which, c, at]) + wide(core_ring[j % 2, which, at])
                )
                return carry

            lax.fori_loop(0, 4 * per, body, 0)
            rs_diag(j, 0).start()
            rs_diag(j, 1).start()
        if stage == 2:
            for axis in range(2):
                rs_diag(j, axis).wait_recv()
                which = yx_y if axis == 0 else yx_x
                at = pl.ds(axis * half, half)
                store[slot, t, which, c, at] = low(
                    wide(store[slot, t, which, c, at]) + wide(diag_ring[j % 2, axis])
                )
            rs_direct(j, 0).start()
            rs_direct(j, 1).start()
        if stage == 3:
            rs_direct(j, 0).wait_recv()
            rs_direct(j, 1).wait_recv()
            total = (
                wide(store[slot, t, yx, c])
                + wide(dir_ring[j % 2, 0])
                + wide(dir_ring[j % 2, 1])
            )

            @pl.when(t == z)
            def _():
                shard_out[PIECES - 1 - j // n_t] = total

            @pl.when(t != z)
            def _():
                store[slot, t, yx, c] = low(total)
                rs_line_out(j).start()

    def reduce_tick(i):
        for stage in (3, 2, 1, 0):

            @pl.when(jnp.logical_and(i >= stage, i - stage < n_jobs))
            def _():
                reduce_stage(stage, jnp.clip(i - stage, 0, n_jobs - 1))

    def line_step(s, out, send, recv, first_src):
        def up():
            shard = jnp.maximum(z - s + 1, 0)
            src = first_src if s == 1 else out.at[shard]
            return remote(src, out.at[shard], send.at[0, s - 1], recv.at[0, s - 1], to_line(1))

        def down():
            shard = jnp.minimum(z + s - 1, n_t - 1)
            src = first_src if s == 1 else out.at[shard]
            return remote(
                src, out.at[shard], send.at[1, s - 1], recv.at[1, s - 1], to_line(n_t - 1)
            )

        return up, down

    def line_start(s, out, send, recv, first_src):
        up, down = line_step(s, out, send, recv, first_src)

        @pl.when(jnp.logical_and(z - s + 1 >= 0, z < n_t - 1))
        def _():
            up().start()

        @pl.when(jnp.logical_and(z + s - 1 <= n_t - 1, z > 0))
        def _():
            down().start()

    def line_recv(s, out, send, recv, first_src):
        up, down = line_step(s, out, send, recv, first_src)

        @pl.when(z - s >= 0)
        def _():
            up().wait_recv()

        @pl.when(z + s <= n_t - 1)
        def _():
            down().wait_recv()

    def line_sent(s, out, send, recv, first_src):
        up, down = line_step(s, out, send, recv, first_src)

        @pl.when(jnp.logical_and(z - s + 1 >= 0, z < n_t - 1))
        def _():
            up().wait_send()

        @pl.when(jnp.logical_and(z + s - 1 <= n_t - 1, z > 0))
        def _():
            down().wait_send()

    line_block = (out_block, ob_send, ob_recv, result.at[0])
    line_tokens = (out_tokens, og_send, og_recv, result.at[1])

    for m in range(PIECES):
        store[m, z, yx, c] = pack[m]
    start_line(0)
    gather_tick(0)

    def matrix(slot, t):
        return store[slot, t].reshape(GROUP * unit, width)

    def chunk_at(i):
        return pl.ds(pl.multiple_of(i * CHUNK, CHUNK), CHUNK)

    def start_of(at):
        chosen = mask_in[at, :] > 0.5
        return jnp.where(chosen, vec[8:9, :], wide(x_in[at, :])), chosen

    def normal(values):
        mean = jnp.mean(values, axis=-1, keepdims=True)
        centred = values - mean
        spread = jnp.mean(centred * centred, axis=-1, keepdims=True)
        rate = lax.rsqrt(spread + norm_eps)
        return centred * rate, rate

    def first_norm(i, total):
        at = chunk_at(i)
        begin, _ = start_of(at)
        hat, _ = normal(begin)
        norm_one[at, :] = low(hat * vec[0:1, :] + vec[1:2, :])
        cot = wide(cot_in[at, :])
        mlp_grad[at, :] = low(vec[6:7, :] * cot)
        return total + fold(cot)

    zero8 = jnp.zeros((8, width), jnp.float32)
    cot_total = lax.fori_loop(0, n_chunks, first_norm, zero8)
    vec_out[7:8, :] = vec[6:7, :] * jnp.sum(cot_total, axis=0, keepdims=True)
    turned_one[...] = norm_one[...].T
    turned_mlp[...] = mlp_grad[...].T
    attn_sum[...] = jnp.zeros_like(attn_sum)

    def early(i, carry):
        gather_tick(i)
        return carry

    lax.fori_loop(1, n_t + 2, early, 0)
    gather_end(0)

    key_ok = lax.broadcasted_iota(jnp.int32, (1, pad_seq), 1) < seq

    def attend(t, carry):
        mixed[t] = low(nn(norm_one[...], matrix(0, t)[:, :mix_cols]) + mix_bias[t])

        def crop_body(b, inner):
            at = pl.ds(pl.multiple_of(b * pad_seq, CHUNK), pad_seq)
            mine = mixed[t, at, :]
            parts = []
            for h in range(heads):
                q = mine[:, h * HD : (h + 1) * HD]
                k = mine[:, head_cols + h * HD : head_cols + (h + 1) * HD]
                v = mine[:, 2 * head_cols + h * HD : 2 * head_cols + (h + 1) * HD]
                s = jnp.where(key_ok, nt(q, k) * scale, -1e30)
                e = jnp.exp(s - jnp.max(s, axis=-1, keepdims=True))
                p = low(e / jnp.sum(e, axis=-1, keepdims=True))
                probs[t, b, h] = p
                parts.append(low(nn(p, v)))
            context[t, at, :] = jnp.concatenate(parts, axis=1)
            return inner

        lax.fori_loop(0, crops, crop_body, 0)
        attn_sum[...] += nt(context[t], matrix(0, t)[:, mix_cols:])
        gather_tick(n_t + 2 + t)
        return carry

    lax.fori_loop(0, n_t, attend, 0)

    def second_norm(i, carry):
        at = chunk_at(i)
        begin, _ = start_of(at)
        mid = begin + vec[2:3, :] * (attn_sum[at, :] + vec[3:4, :])
        middle[at, :] = mid
        hat, _ = normal(mid)
        norm_two[at, :] = low(hat * vec[4:5, :] + vec[5:6, :])
        return carry

    lax.fori_loop(0, n_chunks, second_norm, 0)
    turned_two[...] = norm_two[...].T
    gather_end(1)

    def hidden_units(t, carry):
        wide_one[...] = nn(norm_two[...], matrix(1, t)) + up_bias[t]

        def bend(i, inner):
            at = chunk_at(i)
            h = wide_one[at, :]
            cdf = 0.5 + 0.5 * lax.erf(h * 0.7071067811865476)
            active[t, at, :] = low(h * cdf)
            slope[t, at, :] = low(cdf + h * jnp.exp(-0.5 * h * h) * 0.3989422804014327)
            return inner

        lax.fori_loop(0, n_chunks, bend, 0)
        store[3, t] = low(nn(turned_mlp[...], active[t])).reshape(4, 2, unit, width)
        reduce_tick(t)
        gather_tick(2 * n_t + 2 + t)
        return carry

    lax.fori_loop(0, n_t, hidden_units, 0)
    gather_sent(1)
    gather_end(2)

    wide_one[...] = jnp.zeros_like(wide_one)

    def mlp_out(t, carry):
        wide_one[...] += nt(active[t], matrix(2, t))
        return carry

    lax.fori_loop(0, n_t, mlp_out, 0)

    def finish_block(i, total):
        at = chunk_at(i)
        mlp = wide_one[at, :] + vec[7:8, :]
        result[0, at, :] = low(middle[at, :] + vec[6:7, :] * mlp)
        return total + fold(wide(cot_in[at, :]) * mlp)

    mlp_total = lax.fori_loop(0, n_chunks, finish_block, zero8)
    vec_out[6:7, :] = jnp.sum(mlp_total, axis=0, keepdims=True)
    line_start(1, *line_block)
    own_block = pltpu.make_async_copy(result.at[0], out_block.at[z], own_sem.at[0])
    own_block.start()
    gather_sent(2)

    wide_one[...] = jnp.zeros_like(wide_one)
    ones = jnp.ones((CHUNK, rows), jnp.bfloat16)

    def hidden_back(t, carry):
        wide_two[...] = nn(mlp_grad[...], matrix(2, t))

        def bend(i, inner):
            at = chunk_at(i)
            slope[t, at, :] = low(wide(slope[t, at, :]) * wide_two[at, :])
            return inner

        lax.fori_loop(0, n_chunks, bend, 0)
        up_out[t] = nn(ones, slope[t])[:1]
        store[2, t] = low(nn(turned_two[...], slope[t])).reshape(4, 2, unit, width)
        wide_one[...] += nt(slope[t], matrix(1, t))
        reduce_tick(n_t + t)
        return carry

    lax.fori_loop(0, n_t, hidden_back, 0)
    line_recv(1, *line_block)
    line_start(2, *line_block)

    def second_back(i, totals):
        gain, shift, scale_one, bias_proj = totals
        at = chunk_at(i)
        upstream = wide_one[at, :]
        hat, rate = normal(middle[at, :])
        e = vec[4:5, :] * upstream
        inner = e - jnp.mean(e, axis=-1, keepdims=True)
        inner = inner - hat * jnp.mean(e * hat, axis=-1, keepdims=True)
        g = wide(cot_in[at, :]) + rate * inner
        grad_mid[at, :] = g
        attn_grad[at, :] = low(vec[2:3, :] * g)
        return (
            gain + fold(upstream * hat),
            shift + fold(upstream),
            scale_one + fold(g * (attn_sum[at, :] + vec[3:4, :])),
            bias_proj + fold(g),
        )

    gain, shift, scale_one, bias_proj = lax.fori_loop(0, n_chunks, second_back, (zero8,) * 4)
    vec_out[4:5, :] = jnp.sum(gain, axis=0, keepdims=True)
    vec_out[5:6, :] = jnp.sum(shift, axis=0, keepdims=True)
    vec_out[2:3, :] = jnp.sum(scale_one, axis=0, keepdims=True)
    vec_out[3:4, :] = vec[2:3, :] * jnp.sum(bias_proj, axis=0, keepdims=True)
    turned_attn[...] = attn_grad[...].T
    wide_one[...] = jnp.zeros_like(wide_one)

    def attend_back(t, carry):
        gctx = low(nn(attn_grad[...], matrix(0, t)[:, mix_cols:]))
        gmixed[:, :head_cols] = gctx

        def crop_body(b, inner):
            at = pl.ds(pl.multiple_of(b * pad_seq, CHUNK), pad_seq)
            mine = mixed[t, at, :]
            theirs = gmixed[at, :head_cols]
            gq, gk, gv = [], [], []
            for h in range(heads):
                q = mine[:, h * HD : (h + 1) * HD]
                k = mine[:, head_cols + h * HD : head_cols + (h + 1) * HD]
                v = mine[:, 2 * head_cols + h * HD : 2 * head_cols + (h + 1) * HD]
                g = theirs[:, h * HD : (h + 1) * HD]
                p_low = probs[t, b, h]
                p = wide(p_low)
                gp = nt(g, v)
                gs = low(p * (gp - jnp.sum(gp * p, axis=-1, keepdims=True)))
                gq.append(low(nn(gs, k) * scale))
                gk.append(low(tn(gs, q) * scale))
                gv.append(low(tn(p_low, g)))
            gmixed[at, :] = jnp.concatenate(gq + gk + gv, axis=1)
            return inner

        lax.fori_loop(0, crops, crop_body, 0)
        mix_out[t] = nn(ones, gmixed[...])[:1]
        fresh = jnp.concatenate(
            [
                low(nn(turned_one[...], gmixed[...])),
                low(nn(turned_attn[...], context[t])),
            ],
            axis=1,
        )
        store[1, t] = fresh.reshape(4, 2, unit, width)
        wide_one[...] += nt(gmixed[...], matrix(0, t)[:, :mix_cols])
        reduce_tick(2 * n_t + t)
        return carry

    lax.fori_loop(0, n_t, attend_back, 0)
    line_recv(2, *line_block)
    line_start(3, *line_block)

    def first_back(i, totals):
        gain, shift, token = totals
        at = chunk_at(i)
        upstream = wide_one[at, :]
        begin, chosen = start_of(at)
        hat, rate = normal(begin)
        e = vec[0:1, :] * upstream
        inner = e - jnp.mean(e, axis=-1, keepdims=True)
        inner = inner - hat * jnp.mean(e * hat, axis=-1, keepdims=True)
        g = grad_mid[at, :] + rate * inner
        result[1, at, :] = low(jnp.where(chosen, 0.0, g))
        return (
            gain + fold(upstream * hat),
            shift + fold(upstream),
            token + fold(jnp.where(chosen, g, 0.0)),
        )

    gain, shift, token = lax.fori_loop(0, n_chunks, first_back, (zero8,) * 3)
    vec_out[0:1, :] = jnp.sum(gain, axis=0, keepdims=True)
    vec_out[1:2, :] = jnp.sum(shift, axis=0, keepdims=True)
    vec_out[8:9, :] = jnp.sum(token, axis=0, keepdims=True)
    line_start(1, *line_tokens)
    own_tokens = pltpu.make_async_copy(result.at[1], out_tokens.at[z], own_sem.at[1])
    own_tokens.start()

    def late(i, carry):
        reduce_tick(i)
        return carry

    lax.fori_loop(n_jobs, n_jobs + 3, late, 0)
    line_recv(1, *line_tokens)
    line_start(2, *line_tokens)
    for m in (2, 1, 0):
        for k in range(1, n_t):
            rs_line_in(m, k).wait_recv()
        total = shard_out[m]
        for k in range(1, n_t):
            total = total + wide(line_in[m, k - 1])
        shard_out[m] = total
    line_recv(2, *line_tokens)
    line_start(3, *line_tokens)

    gather_sent(0)

    def sent(j, carry):
        rs_core(j).wait_send()
        for axis in range(2):
            rs_diag(j, axis).wait_send()
            rs_direct(j, axis).wait_send()

        @pl.when(j % n_t != z)
        def _():
            rs_line_out(j).wait_send()

        return carry

    lax.fori_loop(0, n_jobs, sent, 0)
    line_recv(3, *line_block)
    line_recv(3, *line_tokens)
    for s in (1, 2, 3):
        line_sent(s, *line_block)
        line_sent(s, *line_tokens)
    own_block.wait()
    own_tokens.wait()


def run_block(n_dp, n_t, seq, pack, x_in, cot_in, mask_in, vec, mix_bias, up_bias, pad_seq, crops, heads):
    unit, width = pack.shape[1:]
    rows = crops * pad_seq
    head_cols = heads * HD
    mix_cols = 3 * head_cols
    n_jobs = PIECES * n_t
    bf16, f32 = jnp.bfloat16, jnp.float32
    vmem = pltpu.VMEM
    dma = pltpu.SemaphoreType.DMA
    inside = pl.BlockSpec(memory_space=pltpu.VMEM)
    outside = pl.BlockSpec(memory_space=pl.ANY)
    return pl.pallas_call(
        functools.partial(block_kernel, (n_dp, n_t, seq, pad_seq, crops, heads)),
        out_shape=(
            jax.ShapeDtypeStruct((n_t, rows, width), bf16),
            jax.ShapeDtypeStruct((n_t, rows, width), bf16),
            jax.ShapeDtypeStruct((PIECES, unit, width), f32),
            jax.ShapeDtypeStruct((16, width), f32),
            jax.ShapeDtypeStruct((n_t, 1, mix_cols), f32),
            jax.ShapeDtypeStruct((n_t, 1, width), f32),
        ),
        in_specs=[inside] * 7,
        out_specs=(outside, outside, inside, inside, inside, inside),
        scratch_shapes=[
            vmem((4, n_t, 4, 2, unit, width), bf16),
            vmem((rows, width), bf16),
            vmem((width, rows), bf16),
            vmem((n_t, rows, mix_cols), bf16),
            vmem((n_t, crops, heads, pad_seq, pad_seq), bf16),
            vmem((n_t, rows, head_cols), bf16),
            vmem((rows, width), f32),
            vmem((rows, width), f32),
            vmem((rows, width), bf16),
            vmem((width, rows), bf16),
            vmem((rows, width), bf16),
            vmem((width, rows), bf16),
            vmem((n_t, rows, width), bf16),
            vmem((n_t, rows, width), bf16),
            vmem((rows, width), f32),
            vmem((rows, width), f32),
            vmem((rows, width), f32),
            vmem((rows, width), bf16),
            vmem((width, rows), bf16),
            vmem((rows, mix_cols), bf16),
            vmem((2, rows, width), bf16),
            vmem((2, 4, unit, width), bf16),
            vmem((2, 2, unit // 2, width), bf16),
            vmem((2, 2, unit, width), bf16),
            vmem((PIECES, n_t - 1, unit, width), bf16),
            dma((PIECES, n_t - 1)),
            dma((PIECES, n_t - 1)),
            dma((n_jobs, 2)),
            dma((n_jobs, 2)),
            dma((n_jobs, 2)),
            dma((n_jobs, 2)),
            dma((n_jobs, 4)),
            dma((n_jobs, 4)),
            dma((n_jobs,)),
            dma((n_jobs,)),
            dma((n_jobs, 2)),
            dma((n_jobs, 2)),
            dma((n_jobs, 2)),
            dma((n_jobs, 2)),
            dma((n_jobs,)),
            dma((PIECES, n_t - 1)),
            dma((2, n_t - 1)),
            dma((2, n_t - 1)),
            dma((2, n_t - 1)),
            dma((2, n_t - 1)),
            dma((2,)),
        ],
        compiler_params=pltpu.CompilerParams(
            collective_id=0, has_side_effects=True, vmem_limit_bytes=62 * 1024 * 1024
        ),
        name="block_step",
    )(pack, x_in, cot_in, mask_in, vec, mix_bias, up_bias)


def per_device(
    tokens,
    patch_mask,
    cotangent,
    qkv_weight,
    qkv_first,
    qkv_second,
    proj_weight,
    proj_first,
    proj_second,
    fc1_weight,
    fc1_first,
    fc1_second,
    fc2_weight,
    fc2_first,
    fc2_second,
    vectors,
    vectors_first,
    vectors_second,
    head_bias,
    head_bias_first,
    head_bias_second,
    fc1_bias,
    fc1_bias_first,
    fc1_bias_second,
):
    all_crops, seq, width = tokens.shape
    n_dp = lax.axis_size("dp")
    n_t = lax.axis_size("tensor")
    tensor_at = lax.axis_index("tensor")
    crops = all_crops // n_t
    head_cols = qkv_weight.shape[2]
    heads = head_cols // HD
    pad_seq = -(-seq // 16) * 16
    rows = crops * pad_seq
    stride = n_dp // GROUP
    both = ("dp", "tensor")

    def padded(array):
        here = lax.dynamic_slice_in_dim(array, tensor_at * crops, crops, 0)
        spare = [(0, 0), (0, pad_seq - seq), (0, 0)]
        return jnp.pad(here, spare).reshape(rows, -1)

    x_in = padded(tokens)
    cot_in = padded(cotangent)
    mask_all = jnp.pad(patch_mask, [(0, 0), (1 + REG, 0)]).astype(jnp.float32)
    mask_in = padded(mask_all[:, :, None])
    pack = jnp.stack(
        [
            jnp.concatenate(
                [qkv_weight[0], qkv_weight[1], qkv_weight[2], proj_weight.T], axis=1
            ),
            fc1_weight,
            fc2_weight.T,
        ]
    ).astype(jnp.bfloat16)
    if stride > 1:
        teams = [[b * stride + i for i in range(stride)] for b in range(GROUP)]
        pack = lax.all_gather(pack, "dp", axis_index_groups=teams, axis=1, tiled=True)
    head_all = lax.all_gather(head_bias, "tensor", axis=0, tiled=False)
    up_bias = lax.all_gather(fc1_bias, "tensor", axis=0, tiled=False).reshape(n_t, 1, -1)
    mix_bias = jnp.concatenate(
        [head_all[:, :1], jnp.zeros((n_t, 1, head_cols), jnp.float32), head_all[:, 1:]], axis=2
    )
    block_all, grad_all, shard, vec_sums, mix_sums, up_sums = run_block(
        n_dp, n_t, seq, pack, x_in, cot_in, mask_in, vectors, mix_bias, up_bias, pad_seq, crops, heads
    )

    def whole(array):
        return array.reshape(all_crops, pad_seq, width)[:, :seq]

    block_out = whole(block_all)
    tokens_grad = whole(grad_all)
    if stride > 1:
        shard = lax.psum_scatter(
            shard, "dp", scatter_dimension=1, axis_index_groups=teams, tiled=True
        )
    qkv_shard = jnp.stack([shard[0, :, i * head_cols : (i + 1) * head_cols] for i in range(3)])
    proj_shard = shard[0, :, 3 * head_cols :].T
    up_shard = shard[1]
    down_shard = shard[2].T
    vector_sum, mix_all, up_all = lax.psum((vec_sums, mix_sums, up_sums), both)
    vector_sum = vector_sum[:9]
    mix_here = lax.dynamic_slice_in_dim(mix_all, tensor_at, 1, 0)[0, 0]
    head_sum = jnp.stack([mix_here[:head_cols], mix_here[2 * head_cols :]])
    fc1b_sum = lax.dynamic_slice_in_dim(up_all, tensor_at, 1, 0)[0, 0]
    first_data = (lax.axis_index("dp") == 0).astype(jnp.float32)
    first_tensor = (lax.axis_index("tensor") == 0).astype(jnp.float32)
    local_squares = (
        square_sum(qkv_shard)
        + square_sum(proj_shard)
        + square_sum(up_shard)
        + square_sum(down_shard)
    )
    local_squares = local_squares + first_data * (square_sum(head_sum) + square_sum(fc1b_sum))
    local_squares = local_squares + first_data * first_tensor * square_sum(vector_sum)
    total_squares = lax.psum(local_squares, ("dp", "tensor"))
    grad_norm = jnp.sqrt(total_squares)
    factor = jnp.minimum(1.0, clip_norm / (grad_norm + 1e-06))
    qkv_set = adam_step(
        qkv_weight, qkv_first, qkv_second, factor * qkv_shard, rate_matrix, decay_matrix
    )
    proj_set = adam_step(
        proj_weight, proj_first, proj_second, factor * proj_shard, rate_matrix, decay_matrix
    )
    fc1_set = adam_step(
        fc1_weight, fc1_first, fc1_second, factor * up_shard, rate_matrix, decay_matrix
    )
    fc2_set = adam_step(
        fc2_weight, fc2_first, fc2_second, factor * down_shard, rate_matrix, decay_matrix
    )
    vectors_set = adam_step(
        vectors, vectors_first, vectors_second, factor * vector_sum, rate_vector, 0.0
    )
    head_set = adam_step(
        head_bias, head_bias_first, head_bias_second, factor * head_sum, rate_vector, 0.0
    )
    fc1b_set = adam_step(
        fc1_bias, fc1_bias_first, fc1_bias_second, factor * fc1b_sum, rate_vector, 0.0
    )
    return (
        block_out,
        tokens_grad,
        grad_norm,
        qkv_set[0],
        qkv_set[1],
        qkv_set[2],
        proj_set[0],
        proj_set[1],
        proj_set[2],
        fc1_set[0],
        fc1_set[1],
        fc1_set[2],
        fc2_set[0],
        fc2_set[1],
        fc2_set[2],
        vectors_set[0],
        vectors_set[1],
        vectors_set[2],
        head_set[0],
        head_set[1],
        head_set[2],
        fc1b_set[0],
        fc1b_set[1],
        fc1b_set[2],
        qkv_set[0].astype(jnp.bfloat16),
        proj_set[0].astype(jnp.bfloat16),
        fc1_set[0].astype(jnp.bfloat16),
        fc2_set[0].astype(jnp.bfloat16),
    )


def solution(mesh):
    placed = (
        P("dp", None, None),
        P("dp", None),
        P("dp", None, None),
        P(None, "dp", "tensor"),
        P(None, "dp", "tensor"),
        P(None, "dp", "tensor"),
        P("tensor", "dp"),
        P("tensor", "dp"),
        P("tensor", "dp"),
        P("dp", "tensor"),
        P("dp", "tensor"),
        P("dp", "tensor"),
        P("tensor", "dp"),
        P("tensor", "dp"),
        P("tensor", "dp"),
        P(),
        P(),
        P(),
        P(None, "tensor"),
        P(None, "tensor"),
        P(None, "tensor"),
        P("tensor"),
        P("tensor"),
        P("tensor"),
    )
    return jax.shard_map(
        per_device,
        mesh=mesh,
        in_specs=placed,
        out_specs=(
            P("dp", None, None),
            P("dp", None, None),
            P(),
            P(None, "dp", "tensor"),
            P(None, "dp", "tensor"),
            P(None, "dp", "tensor"),
            P("tensor", "dp"),
            P("tensor", "dp"),
            P("tensor", "dp"),
            P("dp", "tensor"),
            P("dp", "tensor"),
            P("dp", "tensor"),
            P("tensor", "dp"),
            P("tensor", "dp"),
            P("tensor", "dp"),
            P(),
            P(),
            P(),
            P(None, "tensor"),
            P(None, "tensor"),
            P(None, "tensor"),
            P("tensor"),
            P("tensor"),
            P("tensor"),
            P(None, "dp", "tensor"),
            P("tensor", "dp"),
            P("dp", "tensor"),
            P("tensor", "dp"),
        ),
        check_vma=False,
    )
```

time: 839 us -> 489 us (0.58)
  waiting for transfers between devices: 427 us -> 106 us
  Pallas kernels: 0 us -> 250 us
  matrix products: 107 us -> 0 us
  other arithmetic: 101 us -> 20.8 us
  local copies, waits for them, and re-layouts: 87.3 us -> 20.9 us
  blocking collectives: 86.6 us -> 70.4 us
    psum x3 -> x1, waiting for transfers between devices: 389 us -> 106 us  [per_device(): vector_sum, mix_all, up_all = lax.psum((vec_sums, mix_sums, up_sums), both)]
    pallas_call x0 -> x1, Pallas kernels: none -> 250 us  [run_block(): pl.pallas_call(functools.partial(block_kernel, (n_dp, n_t, seq, pad_seq,...]
    dot_general x17 -> x0, matrix products: 102 us -> none  [the longest x4 22.1 us: outer_cols(): lax.dot_general(first_op, second_op, (((1,), (1,)), ((), ())), preferred_...]
    reduce_sum x11 -> x0, other arithmetic: 57.9 us -> none  [the longest x3 18.8 us: layer_norm(): return centred * lax.rsqrt(spread + norm_eps) * gain_row + shift_row]
    unnamed x11 -> x1, waiting for transfers between devices: 37.8 us -> 0.02 us
    reshape x16 -> x1, local copies, waits for them, and re-layouts: 36.9 us -> 0.92 us  [padded(): return jnp.pad(here, spare).reshape(rows, -1)]
    psum x1 -> x0, blocking collectives: 24.5 us -> none  [per_device(): lax.psum((vector_grads, grad_head_bias, grad_fc1_bias), 'dp')]
    unnamed x199 -> x56, local copies, waits for them, and re-layouts: 29.8 us -> 10.4 us
  transfers between devices with their start and end apart: 9 -> 1, of which waited for: 4 -> 1; matrix products, arithmetic and copies ran while one was open for 19% -> 2% of each run, Pallas kernels for 0% -> 0%
where the time goes in v2:
time: 489 us; the launch traced here: 488 us
  Pallas kernels  250 us (51%)
  waiting for transfers between devices  106 us (22%)
  blocking collectives  70.4 us (14%)
  local copies, waits for them, and re-layouts  20.9 us (4%)
  other arithmetic  20.8 us (4%)
  between operations  20.8 us (4%)
    pallas_call x1, Pallas kernels, run_block(): pl.pallas_call(functools.partial(block_kernel, (n_dp, n_t, seq, pad_seq,...  250 us
    psum x1, waiting for transfers between devices, per_device(): vector_sum, mix_all, up_all = lax.psum((vec_sums, mix_sums, up_sums), both)  106 us
    psum x1, blocking collectives, per_device(): total_squares = lax.psum(local_squares, ('dp', 'tensor'))  43 us
    all_gather x1, blocking collectives, per_device(): lax.all_gather(fc1_bias, 'tensor', axis=0, tiled=False).reshape(n_t, 1, -1)  13.9 us
    all_gather x1, blocking collectives, per_device(): head_all = lax.all_gather(head_bias, 'tensor', axis=0, tiled=False)  13.5 us
    unnamed x56, local copies, waits for them, and re-layouts  10.4 us
  transfers between devices with their start and end apart: 1, of which 1 were waited for; matrix products, arithmetic and copies ran while one was open for 2% of the time, Pallas kernels for 0%

profile of v2, /device:TPU:0, one launch (start us, length us, event | category | flops | bytes accessed | tf_op | source)
XLA Modules:
  0.0 488.1 jit_solution(12153121364759672255)
XLA Ops:
  7.2 0.0 all-reduce.7.cloned.1.call-start
  7.3 1.0 convert_bitcast_fusion
  8.2 1.0 convert_bitcast_fusion.1
  9.2 1.0 copy.79
  10.2 1.0 convert.26
  11.2 4.5 constant_dynamic-slice_fusion.3
  15.8 0.1 copy.95
  15.9 0.1 copy.96
  16.0 1.0 pad.15.clone
  16.9 1.0 pad.16.clone
  17.9 0.1 fusion.7
  18.0 0.9 reshape.106.mask_in
  18.9 13.5 %all-gather.2 = f32[4,2,192]{2,1,0:T(2,128)S(1)} all-gather(f32[1,2,192]{2,1,0:T(2,128)S(1)} %bitcast.52), channel_id=2, replica_groups=mesh['dp'=8,'tensor'=4] {'tensor'}, dimensions={0}, use_global_device_ids=true | all-gather | bytes 7680 | tf_op jit(solution)/shard_map/all_gather | solution.py:841
  32.5 13.9 %all-gather.3.up_bias = f32[4,1,768]{2,1,0:T(1,128)} all-gather(f32[1,1,768]{2,1,0:T(1,128)S(1)} %reshape.102), channel_id=3, replica_groups=mesh['dp'=8,'tensor'=4] {'tensor'}, dimensions={0}, use_global_device_ids=true | all-gather | bytes 15360 | tf_op jit(solution)/shard_map/all_gather | solution.py:842
  46.4 0.1 pad.25.clone
  46.4 0.1 maximum_bitcast_fusion
  46.6 0.8 pad_maximum_fusion.pack
  47.4 0.6 pad_maximum_fusion.2.mix_bias
  48.0 249.5 %block_step.1 = (bf16[4,544,768]{2,1,0:T(8,128)(2,1)}, bf16[4,544,768]{2,1,0:T(8,128)(2,1)}, f32[3,96,768]{2,1,0:T(8,128)}, f32[16,768]{1,0:T(8,128)}, f32[4,1,576]{2,1,0:T(1,128)}, /*index=5*/f32[4,1,768]{2,1,0:T(1,128)}) custom-call(bf16[3,96,768]{2,1,0:T(8,128)(2,1)} %pad_maximum_fusion.pack, bf16[544,768]{1,0:T(8,128)(2,1)} %bitcast.48, ...), custom_call_target="tpu_custom_call" | custom-call | tf_op jit(solution)/shard_map/block_step/pallas_call | solution.py:715
  297.5 0.0 all-reduce.7.cloned.1.call-update
  297.6 1.8 multiply_reduce_fusion.3
  299.3 1.7 multiply_reduce_fusion
  301.1 2.1 slice.74
  303.2 2.3 copy.93
  305.5 0.6 copy-done.1
  306.1 0.2 slice.75
  306.4 2.3 copy.94
  308.7 0.1 copy.85
  308.8 0.7 multiply_reduce_fusion.2
  312.1 105.6 %all-reduce.7.cloned.1.call-done = (f32[4,1,576]{2,1,0:T(1,128)}, f32[4,1,768]{2,1,0:T(1,128)}, f32[16,768]{1,0:T(8,128)}) async-done(((f32[4,1,576]{2,1,0:T(1,128)}, f32[4,1,768]{2,1,0:T(1,128)}, f32[16,768]{1,0:T(8,128)}), (f32[4,1,576]{2,1,0:T(1,128)}, f32[4,1,768]{2,1,0:T(1,128)}, f32[16,768]{1,0:T(8,128)})) %all-reduce.7.cloned.1.call-update) | async-done | bytes 70672 | tf_op jit(solution)/shard_map/psum | solution.py:863
  417.7 1.3 multiply_reduce_fusion.6
  418.9 0.7 fusion.10
  419.6 0.6 multiply_reduce_fusion.7
  421.5 1.4 multiply_reduce_fusion.4
  423.6 0.1 copy.86
  423.7 43.0 %psum.31 = f32[]{:T(128)} all-reduce(f32[]{:T(128)S(6)} %add.158), channel_id=1, replica_groups=mesh['dp'=8,'tensor'=4] {'dp','tensor'}, use_global_device_ids=true, to_apply=%region_10.11 | all-reduce | flops 1 | bytes 8 | tf_op jit(solution)/shard_map/psum | solution.py:878
  467.5 0.7 multiply_reduce_fusion.5
  468.2 0.8 fusion.15
  469.0 0.7 copy.89
  469.7 0.7 copy.90
  470.4 0.7 copy.91
  471.2 1.5 copy.92
  472.8 1.1 fusion.17
  473.9 2.1 fusion.13
  476.0 2.2 fusion.11
  478.2 0.7 multiply_subtract_fusion.4
  478.9 0.6 multiply_subtract_fusion.6
  479.5 0.6 multiply_subtract_fusion.5
  (49 shorter events, 0.2 us)
Async XLA Ops:
  7.2 410.5 %all-reduce.7.cloned.1.call-start = ((), (), s32[]{:S(2)}) async-start(), calls=%async_computation | async-start | bytes 143360 | tf_op jit(solution)/shard_map/psum | solution.py:863
  15.8 2.1 copy-start.15
  15.8 3.1 copy-start.16
  15.8 16.7 %copy-start.14 = (f32[768]{0:T(1024)S(1)}, f32[768]{0:T(1024)}, u32[]{:S(2)}) copy-start(f32[768]{0:T(1024)} %param.45) | copy-start | bytes 9220
  303.2 2.9 copy-start.1
  306.3 2.4 copy-start.10
  306.3 117.3 %copy-start.11 = (f32[192,96]{1,0:T(8,128)S(1)}, f32[192,96]{1,0:T(8,128)}, u32[]{:S(2)}) copy-start(f32[192,96]{1,0:T(8,128)} %param.32) | copy-start | bytes 221188
  306.4 161.8 %copy-start = (f32[3,96,768]{2,1,0:T(8,128)S(1)}, f32[3,96,768]{2,1,0:T(8,128)}, u32[]{:S(2)}) copy-start(f32[3,96,768]{2,1,0:T(8,128)} %get-tuple-element.36) | copy-start | bytes 2654212
  306.4 166.3 %copy-start.2 = (f32[3,96,192]{2,1,0:T(8,128)S(1)}, f32[3,96,192]{2,1,0:T(8,128)}, u32[]{:S(2)}) copy-start(f32[3,96,192]{2,1,0:T(8,128)} %param.27) | copy-start | bytes 663556
  306.4 166.3 %copy-start.5 = (f32[3,96,192]{2,1,0:T(8,128)S(1)}, f32[3,96,192]{2,1,0:T(8,128)}, u32[]{:S(2)}) copy-start(f32[3,96,192]{2,1,0:T(8,128)} %param.28) | copy-start | bytes 663556
  306.4 166.3 %copy-start.6 = (f32[3,96,192]{2,1,0:T(8,128)S(1)}, f32[3,96,192]{2,1,0:T(8,128)}, u32[]{:S(2)}) copy-start(f32[3,96,192]{2,1,0:T(8,128)} %param.29) | copy-start | bytes 663556
  308.7 165.2 %copy-start.3 = (f32[96,768]{1,0:T(8,128)S(1)}, f32[96,768]{1,0:T(8,128)}, u32[]{:S(2)}) copy-start(f32[96,768]{1,0:T(8,128)} %param.33) | copy-start | bytes 884740
  308.7 165.2 %copy-start.7 = (f32[96,768]{1,0:T(8,128)S(1)}, f32[96,768]{1,0:T(8,128)}, u32[]{:S(2)}) copy-start(f32[96,768]{1,0:T(8,128)} %param.34) | copy-start | bytes 884740
  308.8 167.2 %copy-start.4 = (f32[768,96]{0,1:T(8,128)S(1)}, f32[768,96]{0,1:T(8,128)}, u32[]{:S(2)}) copy-start(f32[768,96]{0,1:T(8,128)} %param.36) | copy-start | bytes 884740
  472.7 5.5 %copy-start.8 = (f32[16,768]{1,0:T(8,128)S(1)}, f32[16,768]{1,0:T(8,128)}, u32[]{:S(2)}) copy-start(f32[16,768]{1,0:T(8,128)} %get-tuple-element.128) | copy-start | bytes 147460
  472.7 5.5 %copy-start.9 = (f32[9,768]{1,0:T(8,128)S(1)}, f32[9,768]{1,0:T(8,128)}, u32[]{:S(2)}) copy-start(f32[9,768]{1,0:T(8,128)} %vec.1) | copy-start | bytes 82948
  472.7 5.5 %copy-start.12 = (f32[9,768]{1,0:T(8,128)S(1)}, f32[9,768]{1,0:T(8,128)}, u32[]{:S(2)}) copy-start(f32[9,768]{1,0:T(8,128)} %param.40) | copy-start | bytes 82948
  472.7 5.4 %copy-start.13 = (f32[9,768]{1,0:T(8,128)S(1)}, f32[9,768]{1,0:T(8,128)}, u32[]{:S(2)}) copy-start(f32[9,768]{1,0:T(8,128)} %param.41) | copy-start | bytes 82948
  472.8 6.1 %copy-start.17 = (f32[2,192]{1,0:T(2,128)S(1)}, f32[2,192]{1,0:T(2,128)}, u32[]{:S(2)}) copy-start(f32[2,192]{1,0:T(2,128)} %param.42) | copy-start | bytes 4612
  472.8 6.1 %copy-start.20 = (f32[2,192]{1,0:T(2,128)S(1)}, f32[2,192]{1,0:T(2,128)}, u32[]{:S(2)}) copy-start(f32[2,192]{1,0:T(2,128)} %param.43) | copy-start | bytes 4612
  472.8 6.1 %copy-start.21 = (f32[2,192]{1,0:T(2,128)S(1)}, f32[2,192]{1,0:T(2,128)}, u32[]{:S(2)}) copy-start(f32[2,192]{1,0:T(2,128)} %param.44) | copy-start | bytes 4612
  472.8 6.7 %copy-start.18 = (f32[768]{0:T(1024)S(1)}, f32[768]{0:T(1024)}, u32[]{:S(2)}) copy-start(f32[768]{0:T(1024)} %param.46) | copy-start | bytes 9220
  472.8 6.7 %copy-start.19 = (f32[768]{0:T(1024)S(1)}, f32[768]{0:T(1024)}, u32[]{:S(2)}) copy-start(f32[768]{0:T(1024)} %param.47) | copy-start | bytes 9220
Sparse Core Ops, SparseCore 0:
  297.7 119.9 all-reduce.6

commit v3 on v2

--- a/solution.py
+++ b/solution.py
@@ -78,14 +78,13 @@
     cot_in,
     mask_in,
     vec,
-    mix_bias,
-    up_bias,
+    bias_own,
     out_block,
     out_tokens,
     shard_out,
-    vec_out,
-    mix_out,
-    up_out,
+    sums_out,
+    own_out,
+    square_out,
     store,
     norm_one,
     turned_one,
@@ -111,6 +110,13 @@
     diag_ring,
     dir_ring,
     line_in,
+    bias_all,
+    sums,
+    sums_in,
+    sums_z,
+    tiles,
+    tiles_in,
+    tiles_z,
     z_send,
     z_recv,
     xy_send,
@@ -132,6 +138,12 @@
     og_send,
     og_recv,
     own_sem,
+    bs_send,
+    bs_recv,
+    vs_send,
+    vs_recv,
+    sq_send,
+    sq_recv,
 ):
     n_dp, n_t, seq, pad_seq, crops, heads = dims
     stride = n_dp // GROUP
@@ -168,6 +180,47 @@
             barrier, inc=1, device_id=peer, device_id_type=pl.DeviceIdType.MESH
         )
     pl.semaphore_wait(barrier, len(peers))
+
+    def sum_copy(step, own, arrived, by_z, send, recv):
+        if step < 3:
+            return remote(
+                own.at[step],
+                arrived.at[step],
+                send.at[step],
+                recv.at[step],
+                (to_core, to_x, to_y)[step],
+            )
+        k = step - 2
+        return remote(own.at[3], by_z.at[z], send.at[step], recv.at[step], to_line(k))
+
+    def sum_start(step, refs):
+        if step < 3:
+            sum_copy(step, *refs).start()
+        else:
+            own, arrived, by_z, send, recv = refs
+            by_z[z] = own[3]
+            for k in range(1, n_t):
+                sum_copy(2 + k, *refs).start()
+
+    def sum_finish(step, refs):
+        own, arrived, by_z, send, recv = refs
+        if step < 3:
+            sum_copy(step, *refs).wait_recv()
+            own[step + 1] = own[step] + arrived[step]
+            return None
+        for k in range(1, n_t):
+            sum_copy(2 + k, *refs).wait_recv()
+        total = by_z[0]
+        for k in range(1, n_t):
+            total = total + by_z[k]
+        return total
+
+    def sum_sent(refs):
+        for step in range(3 + n_t - 1):
+            sum_copy(step, *refs).wait_send()
+
+    grad_sums = (sums, sums_in, sums_z, vs_send, vs_recv)
+    square_sums = (tiles, tiles_in, tiles_z, sq_send, sq_recv)
 
     n_jobs = PIECES * n_t
 
@@ -419,8 +472,18 @@
 
     for m in range(PIECES):
         store[m, z, yx, c] = pack[m]
+    bias_all[z] = bias_own[...]
+
+    def bias_copy(k):
+        return remote(
+            bias_own, bias_all.at[z], bs_send.at[k - 1], bs_recv.at[k - 1], to_line(k)
+        )
+
+    for k in range(1, n_t):
+        bias_copy(k).start()
     start_line(0)
     gather_tick(0)
+    sums[0] = jnp.zeros(sums.shape[1:], jnp.float32)
 
     def matrix(slot, t):
         return store[slot, t].reshape(GROUP * unit, width)
@@ -450,7 +513,7 @@
 
     zero8 = jnp.zeros((8, width), jnp.float32)
     cot_total = lax.fori_loop(0, n_chunks, first_norm, zero8)
-    vec_out[7:8, :] = vec[6:7, :] * jnp.sum(cot_total, axis=0, keepdims=True)
+    sums[0, 7:8, :] = vec[6:7, :] * jnp.sum(cot_total, axis=0, keepdims=True)
     turned_one[...] = norm_one[...].T
     turned_mlp[...] = mlp_grad[...].T
     attn_sum[...] = jnp.zeros_like(attn_sum)
@@ -461,11 +524,13 @@
 
     lax.fori_loop(1, n_t + 2, early, 0)
     gather_end(0)
+    for k in range(1, n_t):
+        bias_copy(k).wait_recv()
 
     key_ok = lax.broadcasted_iota(jnp.int32, (1, pad_seq), 1) < seq
 
     def attend(t, carry):
-        mixed[t] = low(nn(norm_one[...], matrix(0, t)[:, :mix_cols]) + mix_bias[t])
+        mixed[t] = low(nn(norm_one[...], matrix(0, t)[:, :mix_cols]) + bias_all[t, 0:1, :mix_cols])
 
         def crop_body(b, inner):
             at = pl.ds(pl.multiple_of(b * pad_seq, CHUNK), pad_seq)
@@ -504,7 +569,7 @@
     gather_end(1)
 
     def hidden_units(t, carry):
-        wide_one[...] = nn(norm_two[...], matrix(1, t)) + up_bias[t]
+        wide_one[...] = nn(norm_two[...], matrix(1, t)) + bias_all[t, 1:2, :]
 
         def bend(i, inner):
             at = chunk_at(i)
@@ -539,7 +604,7 @@
         return total + fold(wide(cot_in[at, :]) * mlp)
 
     mlp_total = lax.fori_loop(0, n_chunks, finish_block, zero8)
-    vec_out[6:7, :] = jnp.sum(mlp_total, axis=0, keepdims=True)
+    sums[0, 6:7, :] = jnp.sum(mlp_total, axis=0, keepdims=True)
     line_start(1, *line_block)
     own_block = pltpu.make_async_copy(result.at[0], out_block.at[z], own_sem.at[0])
     own_block.start()
@@ -557,7 +622,7 @@
             return inner
 
         lax.fori_loop(0, n_chunks, bend, 0)
-        up_out[t] = nn(ones, slope[t])[:1]
+        sums[0, pl.ds(9 + n_t + t, 1), :] = nn(ones, slope[t])[:1]
         store[2, t] = low(nn(turned_two[...], slope[t])).reshape(4, 2, unit, width)
         wide_one[...] += nt(slope[t], matrix(1, t))
         reduce_tick(n_t + t)
@@ -586,10 +651,10 @@
         )
 
     gain, shift, scale_one, bias_proj = lax.fori_loop(0, n_chunks, second_back, (zero8,) * 4)
-    vec_out[4:5, :] = jnp.sum(gain, axis=0, keepdims=True)
-    vec_out[5:6, :] = jnp.sum(shift, axis=0, keepdims=True)
-    vec_out[2:3, :] = jnp.sum(scale_one, axis=0, keepdims=True)
-    vec_out[3:4, :] = vec[2:3, :] * jnp.sum(bias_proj, axis=0, keepdims=True)
+    sums[0, 4:5, :] = jnp.sum(gain, axis=0, keepdims=True)
+    sums[0, 5:6, :] = jnp.sum(shift, axis=0, keepdims=True)
+    sums[0, 2:3, :] = jnp.sum(scale_one, axis=0, keepdims=True)
+    sums[0, 3:4, :] = vec[2:3, :] * jnp.sum(bias_proj, axis=0, keepdims=True)
     turned_attn[...] = attn_grad[...].T
     wide_one[...] = jnp.zeros_like(wide_one)
 
@@ -618,7 +683,7 @@
             return inner
 
         lax.fori_loop(0, crops, crop_body, 0)
-        mix_out[t] = nn(ones, gmixed[...])[:1]
+        sums[0, pl.ds(9 + t, 1), :mix_cols] = nn(ones, gmixed[...])[:1]
         fresh = jnp.concatenate(
             [
                 low(nn(turned_one[...], gmixed[...])),
@@ -653,20 +718,18 @@
         )
 
     gain, shift, token = lax.fori_loop(0, n_chunks, first_back, (zero8,) * 3)
-    vec_out[0:1, :] = jnp.sum(gain, axis=0, keepdims=True)
-    vec_out[1:2, :] = jnp.sum(shift, axis=0, keepdims=True)
-    vec_out[8:9, :] = jnp.sum(token, axis=0, keepdims=True)
+    sums[0, 0:1, :] = jnp.sum(gain, axis=0, keepdims=True)
+    sums[0, 1:2, :] = jnp.sum(shift, axis=0, keepdims=True)
+    sums[0, 8:9, :] = jnp.sum(token, axis=0, keepdims=True)
     line_start(1, *line_tokens)
     own_tokens = pltpu.make_async_copy(result.at[1], out_tokens.at[z], own_sem.at[1])
     own_tokens.start()
 
-    def late(i, carry):
-        reduce_tick(i)
-        return carry
-
-    lax.fori_loop(n_jobs, n_jobs + 3, late, 0)
-    line_recv(1, *line_tokens)
-    line_start(2, *line_tokens)
+    sum_start(0, grad_sums)
+    for step in range(3):
+        reduce_tick(n_jobs + step)
+        sum_finish(step, grad_sums)
+        sum_start(step + 1, grad_sums)
     for m in (2, 1, 0):
         for k in range(1, n_t):
             rs_line_in(m, k).wait_recv()
@@ -674,8 +737,30 @@
         for k in range(1, n_t):
             total = total + wide(line_in[m, k - 1])
         shard_out[m] = total
+    sums_out[...] = sum_finish(3, grad_sums)
+    own_out[0:1, :] = sums_out[pl.ds(9 + z, 1), :]
+    own_out[1:2, :] = sums_out[pl.ds(9 + n_t + z, 1), :]
+    if stride == 1:
+        first = jnp.where(d == 0, 1.0, 0.0)
+        both = jnp.where(z == 0, first, 0.0)
+        squares = first * square_sum(own_out[...]) + both * square_sum(sums_out[0:9, :])
+        for m in range(PIECES):
+            squares = squares + square_sum(shard_out[m])
+        tiles[0] = jnp.full(tiles.shape[1:], 1.0, jnp.float32) * squares
+        for step in range(4):
+            sum_start(step, square_sums)
+            total = sum_finish(step, square_sums)
+        square_out[...] = total
+        sum_sent(square_sums)
+    else:
+        square_out[...] = jnp.zeros_like(square_out)
+    line_recv(1, *line_tokens)
+    line_start(2, *line_tokens)
     line_recv(2, *line_tokens)
     line_start(3, *line_tokens)
+    sum_sent(grad_sums)
+    for k in range(1, n_t):
+        bias_copy(k).wait_send()
 
     gather_sent(0)
 
@@ -701,28 +786,30 @@
     own_tokens.wait()
 
 
-def run_block(n_dp, n_t, seq, pack, x_in, cot_in, mask_in, vec, mix_bias, up_bias, pad_seq, crops, heads):
+def run_block(dims, pack, x_in, cot_in, mask_in, vec, bias_own):
+    n_dp, n_t, seq, pad_seq, crops, heads = dims
     unit, width = pack.shape[1:]
     rows = crops * pad_seq
     head_cols = heads * HD
     mix_cols = 3 * head_cols
     n_jobs = PIECES * n_t
+    n_sums = -(-(9 + 2 * n_t) // 8) * 8
     bf16, f32 = jnp.bfloat16, jnp.float32
     vmem = pltpu.VMEM
     dma = pltpu.SemaphoreType.DMA
     inside = pl.BlockSpec(memory_space=pltpu.VMEM)
     outside = pl.BlockSpec(memory_space=pl.ANY)
     return pl.pallas_call(
-        functools.partial(block_kernel, (n_dp, n_t, seq, pad_seq, crops, heads)),
+        functools.partial(block_kernel, dims),
         out_shape=(
             jax.ShapeDtypeStruct((n_t, rows, width), bf16),
             jax.ShapeDtypeStruct((n_t, rows, width), bf16),
             jax.ShapeDtypeStruct((PIECES, unit, width), f32),
-            jax.ShapeDtypeStruct((16, width), f32),
-            jax.ShapeDtypeStruct((n_t, 1, mix_cols), f32),
-            jax.ShapeDtypeStruct((n_t, 1, width), f32),
+            jax.ShapeDtypeStruct((n_sums, width), f32),
+            jax.ShapeDtypeStruct((2, width), f32),
+            jax.ShapeDtypeStruct((8, 128), f32),
         ),
-        in_specs=[inside] * 7,
+        in_specs=[inside] * 6,
         out_specs=(outside, outside, inside, inside, inside, inside),
         scratch_shapes=[
             vmem((4, n_t, 4, 2, unit, width), bf16),
@@ -750,6 +837,13 @@
             vmem((2, 2, unit // 2, width), bf16),
             vmem((2, 2, unit, width), bf16),
             vmem((PIECES, n_t - 1, unit, width), bf16),
+            vmem((n_t, 8, width), f32),
+            vmem((4, n_sums, width), f32),
+            vmem((3, n_sums, width), f32),
+            vmem((n_t, n_sums, width), f32),
+            vmem((4, 8, 128), f32),
+            vmem((3, 8, 128), f32),
+            vmem((n_t, 8, 128), f32),
             dma((PIECES, n_t - 1)),
             dma((PIECES, n_t - 1)),
             dma((n_jobs, 2)),
@@ -771,12 +865,72 @@
             dma((2, n_t - 1)),
             dma((2, n_t - 1)),
             dma((2,)),
+            dma((n_t - 1,)),
+            dma((n_t - 1,)),
+            dma((n_t + 2,)),
+            dma((n_t + 2,)),
+            dma((n_t + 2,)),
+            dma((n_t + 2,)),
         ],
         compiler_params=pltpu.CompilerParams(
             collective_id=0, has_side_effects=True, vmem_limit_bytes=62 * 1024 * 1024
         ),
         name="block_step",
-    )(pack, x_in, cot_in, mask_in, vec, mix_bias, up_bias)
+    )(pack, x_in, cot_in, mask_in, vec, bias_own)
+
+
+def adam_kernel(*refs):
+    shard, sums, own_sums, square_tile = refs[:4]
+    states = [refs[4 + 3 * i : 7 + 3 * i] for i in range(7)]
+    norm_out = refs[25]
+    results = [refs[26 + 3 * i : 29 + 3 * i] for i in range(7)]
+    copies = refs[47:51]
+    norm = jnp.sqrt(square_tile[0:1, 0:1])
+    norm_out[...] = jnp.broadcast_to(norm, norm_out.shape)
+    factor = jnp.minimum(1.0, clip_norm / (norm + 1e-06))
+    cols = states[0][0].shape[2]
+
+    def update(i, grad, rate, decay, at=None):
+        old = [ref[...] if at is None else ref[at] for ref in states[i]]
+        fresh = adam_step(*old, factor * grad, rate, decay)
+        for ref, value in zip(results[i], fresh):
+            if at is None:
+                ref[...] = value
+            else:
+                ref[at] = value
+        if i < 4:
+            if at is None:
+                copies[i][...] = low(fresh[0])
+            else:
+                copies[i][at] = low(fresh[0])
+
+    mixed = shard[0]
+    for j in range(3):
+        update(0, mixed[:, j * cols : (j + 1) * cols], rate_matrix, decay_matrix, j)
+    update(1, mixed[:, 3 * cols :].T, rate_matrix, decay_matrix)
+    update(2, shard[1], rate_matrix, decay_matrix)
+    update(3, shard[2].T, rate_matrix, decay_matrix)
+    update(4, sums[0:9, :], rate_vector, 0.0)
+    mix = own_sums[0:1, :]
+    heads = jnp.concatenate([mix[:, :cols], mix[:, 2 * cols : 3 * cols]], axis=0)
+    update(5, heads, rate_vector, 0.0)
+    update(6, own_sums[1:2, :], rate_vector, 0.0)
+
+
+def run_adam(shard, sums, own_sums, square_tile, *states):
+    flat = [array for state in states for array in state]
+    like = [jax.ShapeDtypeStruct(array.shape, array.dtype) for array in flat]
+    copies = [jax.ShapeDtypeStruct(state[0].shape, jnp.bfloat16) for state in states[:4]]
+    inside = pl.BlockSpec(memory_space=pltpu.VMEM)
+    out_shape = [jax.ShapeDtypeStruct((8, 128), jnp.float32)] + like + copies
+    return pl.pallas_call(
+        adam_kernel,
+        out_shape=out_shape,
+        in_specs=[inside] * (4 + len(flat)),
+        out_specs=[inside] * len(out_shape),
+        compiler_params=pltpu.CompilerParams(vmem_limit_bytes=48 * 1024 * 1024),
+        name="adam_step",
+    )(shard, sums, own_sums, square_tile, *flat)
 
 
 def per_device(
@@ -815,7 +969,6 @@
     pad_seq = -(-seq // 16) * 16
     rows = crops * pad_seq
     stride = n_dp // GROUP
-    both = ("dp", "tensor")
 
     def padded(array):
         here = lax.dynamic_slice_in_dim(array, tensor_at * crops, crops, 0)
@@ -838,13 +991,12 @@
     if stride > 1:
         teams = [[b * stride + i for i in range(stride)] for b in range(GROUP)]
         pack = lax.all_gather(pack, "dp", axis_index_groups=teams, axis=1, tiled=True)
-    head_all = lax.all_gather(head_bias, "tensor", axis=0, tiled=False)
-    up_bias = lax.all_gather(fc1_bias, "tensor", axis=0, tiled=False).reshape(n_t, 1, -1)
-    mix_bias = jnp.concatenate(
-        [head_all[:, :1], jnp.zeros((n_t, 1, head_cols), jnp.float32), head_all[:, 1:]], axis=2
-    )
-    block_all, grad_all, shard, vec_sums, mix_sums, up_sums = run_block(
-        n_dp, n_t, seq, pack, x_in, cot_in, mask_in, vectors, mix_bias, up_bias, pad_seq, crops, heads
+    mix_row = jnp.concatenate([head_bias[0], jnp.zeros((head_cols,), jnp.float32), head_bias[1]])
+    mix_row = jnp.pad(mix_row, (0, width - 3 * head_cols))
+    bias_own = jnp.pad(jnp.stack([mix_row, fc1_bias]), [(0, 6), (0, 0)])
+    dims = (n_dp, n_t, seq, pad_seq, crops, heads)
+    block_all, grad_all, shard, sums, own_sums, square_tile = run_block(
+        dims, pack, x_in, cot_in, mask_in, vectors, bias_own
     )
 
     def whole(array):
@@ -852,19 +1004,38 @@
 
     block_out = whole(block_all)
     tokens_grad = whole(grad_all)
-    if stride > 1:
-        shard = lax.psum_scatter(
-            shard, "dp", scatter_dimension=1, axis_index_groups=teams, tiled=True
-        )
+    if stride == 1:
+        updated = run_adam(
+            shard,
+            sums,
+            own_sums,
+            square_tile,
+            (qkv_weight, qkv_first, qkv_second),
+            (proj_weight, proj_first, proj_second),
+            (fc1_weight, fc1_first, fc1_second),
+            (fc2_weight, fc2_first, fc2_second),
+            (vectors, vectors_first, vectors_second),
+            (head_bias, head_bias_first, head_bias_second),
+            (fc1_bias[None], fc1_bias_first[None], fc1_bias_second[None]),
+        )
+        norm_tile = updated[0]
+        updated = list(updated[1:])
+        for at in (18, 19, 20):
+            updated[at] = updated[at][0]
+        return (block_out, tokens_grad, norm_tile[0, 0], *updated)
+    both = ("dp", "tensor")
+    shard = lax.psum_scatter(
+        shard, "dp", scatter_dimension=1, axis_index_groups=teams, tiled=True
+    )
     qkv_shard = jnp.stack([shard[0, :, i * head_cols : (i + 1) * head_cols] for i in range(3)])
     proj_shard = shard[0, :, 3 * head_cols :].T
     up_shard = shard[1]
     down_shard = shard[2].T
-    vector_sum, mix_all, up_all = lax.psum((vec_sums, mix_sums, up_sums), both)
-    vector_sum = vector_sum[:9]
-    mix_here = lax.dynamic_slice_in_dim(mix_all, tensor_at, 1, 0)[0, 0]
-    head_sum = jnp.stack([mix_here[:head_cols], mix_here[2 * head_cols :]])
-    fc1b_sum = lax.dynamic_slice_in_dim(up_all, tensor_at, 1, 0)[0, 0]
+    sums, own_sums = lax.psum((sums, own_sums), "dp", axis_index_groups=teams)
+    vector_sum = sums[:9]
+    mix_here = own_sums[0]
+    head_sum = jnp.stack([mix_here[:head_cols], mix_here[2 * head_cols : 3 * head_cols]])
+    fc1b_sum = own_sums[1]
     first_data = (lax.axis_index("dp") == 0).astype(jnp.float32)
     first_tensor = (lax.axis_index("tensor") == 0).astype(jnp.float32)
     local_squares = (

time: 489 us -> 301 us (0.62)
  waiting for transfers between devices: 106 us -> 0 us
  blocking collectives: 70.4 us -> 0 us
  between operations: 20.8 us -> 1.07 us
  Pallas kernels: 250 us -> 269 us
  other arithmetic: 20.8 us -> 7.16 us
    psum x1 -> x0, waiting for transfers between devices: 106 us -> none  [per_device(): vector_sum, mix_all, up_all = lax.psum((vec_sums, mix_sums, up_sums), both)]
    psum x1 -> x0, blocking collectives: 43 us -> none  [per_device(): total_squares = lax.psum(local_squares, ('dp', 'tensor'))]
    all_gather x2 -> x0, blocking collectives: 27.4 us -> none  [the longest x1 13.9 us: per_device(): lax.all_gather(fc1_bias, 'tensor', axis=0, tiled=False).reshape(n_t, 1, -1)]
    pallas_call x1 -> x2, Pallas kernels: 250 us -> 269 us  [the longest x1 267 us: run_block(): pl.pallas_call(functools.partial(block_kernel, dims), out_shape=(jax.Shap...]
    reduce_sum x6 -> x0, other arithmetic: 7.51 us -> none  [square_sum(): return jnp.sum(values * values)]
    convert_element_type x4 -> x0, other arithmetic: 6.13 us -> none  [the longest x1 2.16 us: per_device(): fc2_set[0].astype(jnp.bfloat16)]
    unnamed x56 -> x58, local copies, waits for them, and re-layouts: 10.4 us -> 10.3 us
  transfers between devices with their start and end apart: 1 -> 0, of which waited for: 1 -> 0; matrix products, arithmetic and copies ran while one was open for 2% -> 0% of each run, Pallas kernels for 0% -> 0%
where the time goes in v3:
time: 301 us
  Pallas kernels  269 us (89%)
  local copies, waits for them, and re-layouts  23.4 us (8%)
  other arithmetic  7.16 us (2%)
    pallas_call x1, Pallas kernels, run_block(): pl.pallas_call(functools.partial(block_kernel, dims), out_shape=(jax.Shap...  267 us
    unnamed x58, local copies, waits for them, and re-layouts  10.3 us

profile of v3, /device:TPU:0, one launch (start us, length us, event | category | flops | bytes accessed | tf_op | source)
XLA Modules:
  0.0 300.7 jit_solution(5057584202176478894)
XLA Ops:
  0.7 0.0 copy-start.20
  0.7 0.8 fusion.2
  1.5 0.1 select_maximum_fusion.1
  1.6 0.7 stack.30.refs_22_
  2.3 0.8 fusion.1
  3.0 0.7 broadcast_in_dim.12.refs_23_
  3.7 0.7 broadcast_in_dim.13.refs_24_
  4.4 0.6 select_maximum_fusion.bias_own
  5.0 1.0 copy.64
  6.0 1.0 convert.26
  7.0 0.1 maximum_bitcast_fusion
  7.1 1.0 convert_bitcast_fusion.1
  8.1 1.0 convert_bitcast_fusion
  9.1 0.8 pad_maximum_fusion.pack
  9.9 0.9 reshape.77.mask_in
  10.9 0.2 copy.71.refs_14_
  11.0 0.2 copy.72.refs_15_
  11.2 0.2 copy.70.refs_13_
  11.4 4.5 %constant_dynamic-slice_fusion = (bf16[2,261,768]{2,0,1:T(2,128)(2,1)S(1)}, bf16[2,261,768]{2,0,1:T(2,128)(2,1)S(1)}) fusion(bf16[8,261,768]{2,0,1:T(8,128)(2,1)} %param.26, s32[]{:T(128)S(6)} %select_n.2, bf16[8,261,768]{2,0,1:T(8,128)(2,1)} %param.24), kind=kLoop, calls=%fused_computation.16 | loop fusion | bytes 3207172 | tf_op jit(solution)/shard_map/dynamic_slice | solution.py:974
  15.9 0.1 copy.80
  16.0 1.0 pad.24.clone
  17.0 0.1 copy.79
  17.1 1.0 pad.23.clone
  18.0 267.0 %block_step.1 = (bf16[4,544,768]{2,1,0:T(8,128)(2,1)}, bf16[4,544,768]{2,1,0:T(8,128)(2,1)}, f32[3,96,768]{2,1,0:T(8,128)}, f32[24,768]{1,0:T(8,128)}, f32[2,768]{1,0:T(2,128)}, /*index=5*/f32[8,128]{1,0:T(8,128)}) custom-call(bf16[3,96,768]{2,1,0:T(8,128)(2,1)} %pad_maximum_fusion.pack, bf16[544,768]{1,0:T(8,128)(2,1)} %bitcast.29, ...), custom_call_target="tpu_custom_call" | custom-call | tf_op jit(solution)/shard_map/block_step/pallas_call | solution.py:802
  285.0 2.1 slice.38
  287.2 2.3 copy.77
  289.5 0.5 copy-done.19
  290.0 0.2 slice.39
  290.2 0.0 copy-start
  290.2 0.0 copy-start.1
  290.2 0.0 copy-start.3
  290.3 0.0 copy-start.4
  290.3 0.0 copy-start.5
  290.3 0.0 copy-start.6
  290.3 0.0 copy-start.8
  290.3 0.0 copy-start.9
  290.4 0.0 copy-start.13
  290.4 0.0 copy-start.14
  290.4 2.3 copy.78
  292.9 2.0 adam_step.1
  294.9 0.5 slice.34
  295.5 0.6 reduce
  296.1 0.6 reduce.1
  296.7 0.6 reduce.2
  297.3 0.8 copy.76
  298.1 0.9 copy.73
  298.9 0.9 copy.74
  299.8 0.9 copy.75
  (38 shorter events, 0.1 us)
Async XLA Ops:
  0.7 10.5 %copy-start.20 = (f32[768,96]{0,1:T(8,128)S(1)}, f32[768,96]{0,1:T(8,128)}, u32[]{:S(2)}) copy-start(f32[768,96]{0,1:T(8,128)} %param.36) | copy-start | bytes 884740
  0.7 10.3 %copy-start.22 = (f32[768,96]{0,1:T(8,128)S(1)}, f32[768,96]{0,1:T(8,128)}, u32[]{:S(2)}) copy-start(f32[768,96]{0,1:T(8,128)} %param.38) | copy-start | bytes 884740
  0.7 10.2 %copy-start.21 = (f32[768,96]{0,1:T(8,128)S(1)}, f32[768,96]{0,1:T(8,128)}, u32[]{:S(2)}) copy-start(f32[768,96]{0,1:T(8,128)} %param.37) | copy-start | bytes 884740
  287.2 2.8 copy-start.19
  290.2 2.5 copy-start
  290.2 2.5 copy-start.1
  290.2 2.5 copy-start.2
  290.2 2.5 copy-start.3
  290.3 2.5 copy-start.4
  290.3 2.5 copy-start.5
  290.3 2.5 copy-start.6
  290.3 2.5 copy-start.7
  290.3 2.5 copy-start.8
  290.3 2.5 copy-start.9
  290.3 2.5 copy-start.10
  290.3 2.5 copy-start.11
  290.4 2.5 copy-start.12
  290.4 2.5 copy-start.13
  290.4 2.5 copy-start.14
  290.4 2.5 copy-start.15
  290.4 2.5 copy-start.16
  290.4 2.5 copy-start.17
  290.4 2.5 copy-start.18

commit v4 on v3

--- a/solution.py
+++ b/solution.py
@@ -11,8 +11,11 @@
 REG = 4
 STEP = 10
 GROUP = 8
+LAG = 2
+RING = 4
+
 PIECES = 3
-CHUNK = 16
+CHUNK = 32
 
 norm_eps = 1e-06
 clip_norm = 1.0
@@ -57,7 +60,7 @@
 
 
 def fold(values):
-    return values[:8] + values[8:]
+    return jnp.sum(values.reshape(-1, 8, values.shape[-1]), axis=0)
 
 
 def remote(src, dst, send, recv, device):
@@ -75,6 +78,7 @@
     dims,
     pack,
     x_in,
+    x_next,
     cot_in,
     mask_in,
     vec,
@@ -94,17 +98,10 @@
     attn_sum,
     middle,
     norm_two,
-    turned_two,
     mlp_grad,
     turned_mlp,
-    active,
-    slope,
     wide_one,
     wide_two,
-    grad_mid,
-    attn_grad,
-    turned_attn,
-    gmixed,
     result,
     core_ring,
     diag_ring,
@@ -174,7 +171,15 @@
         return (d, (z + k) % n_t)
 
     barrier = pltpu.get_barrier_semaphore()
-    peers = [to_core, to_x, to_y] + [to_line(k) for k in range(1, n_t)]
+    def to_place(r):
+        other = (
+            c + (r % 2) * (1 - 2 * c)
+            + 2 * (xbit + (r // 2 % 2) * (1 - 2 * xbit))
+            + 4 * (ybit + (r // 4) * (1 - 2 * ybit))
+        )
+        return (d + (other - place) * stride, z)
+
+    peers = [to_place(r) for r in range(1, GROUP)] + [to_line(k) for k in range(1, n_t)]
     for peer in peers:
         pl.semaphore_signal(
             barrier, inc=1, device_id=peer, device_id_type=pl.DeviceIdType.MESH
@@ -220,7 +225,15 @@
             sum_copy(step, *refs).wait_send()
 
     grad_sums = (sums, sums_in, sums_z, vs_send, vs_recv)
-    square_sums = (tiles, tiles_in, tiles_z, sq_send, sq_recv)
+
+    def tile_copy(i):
+        if i < GROUP - 1:
+            dst = tiles_in.at[place]
+            return remote(tiles.at[0], dst, sq_send.at[i], sq_recv.at[i], to_place(i + 1))
+        k = i - GROUP + 2
+        return remote(tiles.at[1], tiles_z.at[z], sq_send.at[i], sq_recv.at[i], to_line(k))
+
+    n_tiles = GROUP - 1 + n_t - 1
 
     n_jobs = PIECES * n_t
 
@@ -228,8 +241,16 @@
         src = store.at[m, z, yx, c]
         return remote(src, src, z_send.at[m, k - 1], z_recv.at[m, k - 1], to_line(k))
 
+    def job_of(i):
+        others = jnp.maximum(i - PIECES, 0)
+        m = jnp.where(i < PIECES, i, others // (n_t - 1))
+        return m, jnp.where(i < PIECES, 0, others % (n_t - 1) + 1)
+
+    def job_at(m, k):
+        return jnp.where(k == 0, m, PIECES + m * (n_t - 1) + k - 1)
+
     def block_at(i, which):
-        m, k = i // n_t, i % n_t
+        m, k = job_of(i)
         return store.at[m, (z + n_t - k) % n_t, which, c]
 
     def direct(i, axis):
@@ -253,55 +274,58 @@
         for k in range(1, n_t):
             z_copy(m, k).start()
 
-    def gather_tick(i):
-        @pl.when(jnp.logical_and(i >= 2, i - 2 < n_jobs))
+    def first_stage(i):
+        m, k = job_of(i)
+
+        @pl.when(k > 0)
         def _():
-            j = jnp.maximum(i - 2, 0)
-            diagonal(j, 0).wait_recv()
-            diagonal(j, 1).wait_recv()
-            across(j, 3).start()
-
-        @pl.when(jnp.logical_and(i >= 1, i - 1 < n_jobs))
-        def _():
-            j = jnp.maximum(i - 1, 0)
-            direct(j, 0).wait_recv()
-            diagonal(j, 1).start()
-            direct(j, 1).wait_recv()
-            diagonal(j, 0).start()
-            across(j, 1).start()
-            across(j, 2).start()
-
-        @pl.when(i < n_jobs)
-        def _():
-            j = jnp.minimum(i, n_jobs - 1)
-            m, k = j // n_t, j % n_t
-
-            @pl.when(k > 0)
+            z_copy(m, jnp.maximum(k, 1)).wait_recv()
+
+        direct(i, 0).start()
+        direct(i, 1).start()
+        across(i, 0).start()
+
+    def second_stage(i):
+        direct(i, 0).wait_recv()
+        diagonal(i, 1).start()
+        direct(i, 1).wait_recv()
+        diagonal(i, 0).start()
+        across(i, 1).start()
+        across(i, 2).start()
+
+    def third_stage(i):
+        diagonal(i, 0).wait_recv()
+        diagonal(i, 1).wait_recv()
+        across(i, 3).start()
+
+    def gather_steps(text):
+        for stage, i in text:
+            {"a": first_stage, "b": second_stage, "c": third_stage, "z": start_line}[stage](i)
+
+    def at_step(value, table):
+        for key, text in table.items():
+
+            @pl.when(value == key)
             def _():
-                z_copy(m, jnp.maximum(k, 1)).wait_recv()
-
-            direct(j, 0).start()
-            direct(j, 1).start()
-            across(j, 0).start()
-
-            @pl.when(jnp.logical_and(k == n_t - 1, m < PIECES - 1))
-            def _():
-                start_line(m + 1)
+                gather_steps(text)
 
     def gather_end(m):
         def body(k, carry):
-            for slot in range(4):
-                across(m * n_t + k, slot).wait_recv()
+            gather_part(m, k)
             return carry
 
         lax.fori_loop(0, n_t, body, 0)
+
+    def gather_part(m, k):
+        for slot in range(4):
+            across(job_at(m, k), slot).wait_recv()
 
     def gather_sent(m):
         for k in range(1, n_t):
             z_copy(m, k).wait_send()
 
         def body(k, carry):
-            i = m * n_t + k
+            i = job_at(m, k)
             for axis in range(2):
                 direct(i, axis).wait_send()
                 diagonal(i, axis).wait_send()
@@ -311,14 +335,32 @@
 
         lax.fori_loop(0, n_t, body, 0)
 
+    late_jobs = 3 * n_t + 2
+    n_slots = late_jobs + 2 * n_t
+
+    def late_group(i):
+        return jnp.where(i % 2 == 0, i // 2, n_t - 1 - i // 2)
+
     def job_slot(j):
-        return 3 - j // n_t, j % n_t
+        early = j < 2 * n_t
+        return (
+            jnp.where(early, 3 + j % 2, 5),
+            jnp.where(early, j // 2, late_group(jnp.maximum(j - late_jobs, 0) // 2)),
+        )
+
+    def ring_slot(j):
+        return jnp.where(j < 2 * n_t, j % RING, jnp.maximum(j - late_jobs, 0) // 2 % 2)
+
+    def job_valid(j):
+        late = jnp.logical_and(j >= late_jobs, (j - late_jobs) % 2 == 0)
+        busy = jnp.logical_or(j < 2 * n_t, late)
+        return jnp.logical_and(busy, jnp.logical_and(j >= 0, j < n_slots))
 
     def rs_core(j):
         slot, t = job_slot(j)
         return remote(
             store.at[slot, t, :, 1 - c],
-            core_ring.at[j % 2],
+            core_ring.at[ring_slot(j)],
             rc_send.at[j],
             rc_recv.at[j],
             to_core,
@@ -328,7 +370,7 @@
         slot, t = job_slot(j)
         return remote(
             store.at[slot, t, yx_d, c, pl.ds(axis * half, half)],
-            diag_ring.at[j % 2, axis],
+            diag_ring.at[ring_slot(j), axis],
             rd_send.at[j, axis],
             rd_recv.at[j, axis],
             to_x if axis == 0 else to_y,
@@ -338,32 +380,26 @@
         slot, t = job_slot(j)
         return remote(
             store.at[slot, t, yx_x if axis == 0 else yx_y, c],
-            dir_ring.at[j % 2, axis],
+            dir_ring.at[ring_slot(j), axis],
             rx_send.at[j, axis],
             rx_recv.at[j, axis],
             to_x if axis == 0 else to_y,
         )
 
-    def rs_line_out(j):
-        slot, t = job_slot(j)
-        k = (z + n_t - t) % n_t
-        m = PIECES - 1 - j // n_t
+    def rs_line(slot, t, up):
+        to = z + 1 if up else z - 1
+        at = t if up else jnp.where(t == to, n_t, t)
         return remote(
             store.at[slot, t, yx, c],
-            line_in.at[m, jnp.maximum(k, 1) - 1],
-            rz_send.at[j],
-            rz_recv.at[m, jnp.maximum(k, 1) - 1],
-            (d, t),
+            line_in.at[5 - slot, at],
+            rz_send.at[5 - slot, t],
+            rz_recv.at[5 - slot, at],
+            to_line(1 if up else n_t - 1),
         )
 
-    def rs_line_in(m, k):
-        return remote(
-            line_in.at[m, k - 1],
-            line_in.at[m, k - 1],
-            rz_send.at[0],
-            rz_recv.at[m, k - 1],
-            to_line(1),
-        )
+    def rs_line_in(m, at):
+        here = line_in.at[m, at]
+        return remote(here, here, rz_send.at[m, 0], rz_recv.at[m, at], to_line(1))
 
     def reduce_stage(stage, j):
         slot, t = job_slot(j)
@@ -377,7 +413,7 @@
                 at = pl.ds(pl.multiple_of((s % per) * CHUNK, CHUNK), CHUNK)
                 which = s // per
                 store[slot, t, which, c, at] = low(
-                    wide(store[slot, t, which, c, at]) + wide(core_ring[j % 2, which, at])
+                    wide(store[slot, t, which, c, at]) + wide(core_ring[ring_slot(j), which, at])
                 )
                 return carry
 
@@ -390,7 +426,7 @@
                 which = yx_y if axis == 0 else yx_x
                 at = pl.ds(axis * half, half)
                 store[slot, t, which, c, at] = low(
-                    wide(store[slot, t, which, c, at]) + wide(diag_ring[j % 2, axis])
+                    wide(store[slot, t, which, c, at]) + wide(diag_ring[ring_slot(j), axis])
                 )
             rs_direct(j, 0).start()
             rs_direct(j, 1).start()
@@ -399,73 +435,91 @@
             rs_direct(j, 1).wait_recv()
             total = (
                 wide(store[slot, t, yx, c])
-                + wide(dir_ring[j % 2, 0])
-                + wide(dir_ring[j % 2, 1])
+                + wide(dir_ring[ring_slot(j), 0])
+                + wide(dir_ring[ring_slot(j), 1])
             )
 
             @pl.when(t == z)
             def _():
-                shard_out[PIECES - 1 - j // n_t] = total
+                shard_out[5 - slot] = total
 
             @pl.when(t != z)
             def _():
                 store[slot, t, yx, c] = low(total)
-                rs_line_out(j).start()
+
+        if stage >= 3:
+            hop = stage - 3
+            for up in (True, False):
+                here = z == (hop if up else n_t - 1 - hop)
+
+                @pl.when(jnp.logical_and(here, t > z if up else t < z))
+                def _():
+                    if hop > 0:
+                        rs_line_in(5 - slot, t).wait_recv()
+                        store[slot, t, yx, c] = low(
+                            wide(store[slot, t, yx, c]) + wide(line_in[5 - slot, t])
+                        )
+                    rs_line(slot, t, up).start()
 
     def reduce_tick(i):
-        for stage in (3, 2, 1, 0):
-
-            @pl.when(jnp.logical_and(i >= stage, i - stage < n_jobs))
+        for stage in range(n_t + 1, -1, -1):
+
+            @pl.when(job_valid(i - stage * LAG))
             def _():
-                reduce_stage(stage, jnp.clip(i - stage, 0, n_jobs - 1))
-
-    def line_step(s, out, send, recv, first_src):
-        def up():
-            shard = jnp.maximum(z - s + 1, 0)
-            src = first_src if s == 1 else out.at[shard]
-            return remote(src, out.at[shard], send.at[0, s - 1], recv.at[0, s - 1], to_line(1))
-
-        def down():
-            shard = jnp.minimum(z + s - 1, n_t - 1)
-            src = first_src if s == 1 else out.at[shard]
-            return remote(
-                src, out.at[shard], send.at[1, s - 1], recv.at[1, s - 1], to_line(n_t - 1)
-            )
-
-        return up, down
-
-    def line_start(s, out, send, recv, first_src):
-        up, down = line_step(s, out, send, recv, first_src)
-
-        @pl.when(jnp.logical_and(z - s + 1 >= 0, z < n_t - 1))
-        def _():
-            up().start()
-
-        @pl.when(jnp.logical_and(z + s - 1 <= n_t - 1, z > 0))
-        def _():
-            down().start()
-
-    def line_recv(s, out, send, recv, first_src):
-        up, down = line_step(s, out, send, recv, first_src)
-
-        @pl.when(z - s >= 0)
-        def _():
-            up().wait_recv()
-
-        @pl.when(z + s <= n_t - 1)
-        def _():
-            down().wait_recv()
-
-    def line_sent(s, out, send, recv, first_src):
-        up, down = line_step(s, out, send, recv, first_src)
-
-        @pl.when(jnp.logical_and(z - s + 1 >= 0, z < n_t - 1))
-        def _():
-            up().wait_send()
-
-        @pl.when(jnp.logical_and(z + s - 1 <= n_t - 1, z > 0))
-        def _():
-            down().wait_send()
+                reduce_stage(stage, jnp.clip(i - stage * LAG, 0, n_slots - 1))
+
+    def line_copy(q, up, out, send, recv, first_src):
+        s, b = q // crops + 1, q % crops
+        shard = jnp.maximum(z - s + 1, 0) if up else jnp.minimum(z + s - 1, n_t - 1)
+        at = pl.ds(b * pad_seq, pad_seq)
+        src = first_src.at[at] if s == 1 else out.at[shard, at]
+        way = 0 if up else 1
+        return remote(
+            src,
+            out.at[shard, at],
+            send.at[way, q],
+            recv.at[way, q],
+            to_line(1 if up else n_t - 1),
+        )
+
+    def line_go(q, action, refs):
+        s = q // crops + 1
+        skip = refs is line_block and s == 1
+        sends = action != "wait_recv"
+        for up in (True, False):
+            if up:
+                ok = jnp.logical_and(z - s + 1 >= 0, z < n_t - 1) if sends else z - s >= 0
+                if skip:
+                    ok = jnp.logical_and(ok, z != (n_t - 2 if sends else n_t - 1))
+            else:
+                ok = jnp.logical_and(z + s - 1 <= n_t - 1, z > 0) if sends else z + s <= n_t - 1
+                if skip:
+                    ok = jnp.logical_and(ok, z != (1 if sends else 0))
+
+            @pl.when(ok)
+            def _():
+                copy = line_copy(q, up, *refs)
+                if action == "start":
+                    copy.start()
+                elif action == "wait_send":
+                    copy.wait_send()
+                else:
+                    copy.wait_recv()
+
+    n_hops = crops * (n_t - 1)
+
+    def line_begin(refs):
+        for q in range(crops):
+            line_go(q, "start", refs)
+
+    def line_forward(q, refs):
+        line_go(q, "wait_recv", refs)
+        if q + crops < n_hops:
+            line_go(q + crops, "start", refs)
+
+    def line_end(refs, begin=0):
+        for q in range(begin, n_hops):
+            line_go(q, "wait_send", refs)
 
     line_block = (out_block, ob_send, ob_recv, result.at[0])
     line_tokens = (out_tokens, og_send, og_recv, result.at[1])
@@ -481,19 +535,32 @@
 
     for k in range(1, n_t):
         bias_copy(k).start()
-    start_line(0)
-    gather_tick(0)
+    gather_steps((("z", 0), ("a", 0), ("a", 1), ("a", 2),))
     sums[0] = jnp.zeros(sums.shape[1:], jnp.float32)
 
     def matrix(slot, t):
         return store[slot, t].reshape(GROUP * unit, width)
 
+    def active_of(t):
+        return store[4, t].reshape(GROUP * unit, width)[:rows]
+
+    def slope_of(t):
+        return store[5, t].reshape(GROUP * unit, width)[:rows]
+
+    per_unit = unit // CHUNK
+
+    def spot(i):
+        block = i // per_unit
+        at = pl.ds(pl.multiple_of((i % per_unit) * CHUNK, CHUNK), CHUNK)
+        return block // 2, block % 2, at
+
     def chunk_at(i):
         return pl.ds(pl.multiple_of(i * CHUNK, CHUNK), CHUNK)
 
-    def start_of(at):
-        chosen = mask_in[at, :] > 0.5
-        return jnp.where(chosen, vec[8:9, :], wide(x_in[at, :])), chosen
+    def start_of(at, extra=False):
+        chosen = mask_in[at, 1:2] > 0.5 if extra else mask_in[at, 0:1] > 0.5
+        source = mlp_grad if extra else x_in
+        return jnp.where(chosen, vec[8:9, :], wide(source[at, :])), chosen
 
     def normal(values):
         mean = jnp.mean(values, axis=-1, keepdims=True)
@@ -502,38 +569,33 @@
         rate = lax.rsqrt(spread + norm_eps)
         return centred * rate, rate
 
-    def first_norm(i, total):
+    def first_norm(i, carry, extra=False):
         at = chunk_at(i)
-        begin, _ = start_of(at)
+        begin, _ = start_of(at, extra)
         hat, _ = normal(begin)
         norm_one[at, :] = low(hat * vec[0:1, :] + vec[1:2, :])
-        cot = wide(cot_in[at, :])
-        mlp_grad[at, :] = low(vec[6:7, :] * cot)
-        return total + fold(cot)
+        return carry
 
     zero8 = jnp.zeros((8, width), jnp.float32)
-    cot_total = lax.fori_loop(0, n_chunks, first_norm, zero8)
-    sums[0, 7:8, :] = vec[6:7, :] * jnp.sum(cot_total, axis=0, keepdims=True)
-    turned_one[...] = norm_one[...].T
-    turned_mlp[...] = mlp_grad[...].T
     attn_sum[...] = jnp.zeros_like(attn_sum)
 
     def early(i, carry):
-        gather_tick(i)
+        lax.fori_loop(i * n_chunks // 3, (i + 1) * n_chunks // 3, first_norm, 0)
+        at_step(i, {0: (("b", 0),), 1: (("z", 1), ("b", 1),), 2: (("b", 2), ("c", 0), ("c", 1), ("c", 2),)})
         return carry
 
-    lax.fori_loop(1, n_t + 2, early, 0)
-    gather_end(0)
+    lax.fori_loop(0, 3, early, 0)
+    gather_steps((("a", 3), ("a", 4), ("a", 5), ("z", 2),))
     for k in range(1, n_t):
         bias_copy(k).wait_recv()
 
     key_ok = lax.broadcasted_iota(jnp.int32, (1, pad_seq), 1) < seq
 
-    def attend(t, carry):
+    def attend(t, extra=False):
         mixed[t] = low(nn(norm_one[...], matrix(0, t)[:, :mix_cols]) + bias_all[t, 0:1, :mix_cols])
 
         def crop_body(b, inner):
-            at = pl.ds(pl.multiple_of(b * pad_seq, CHUNK), pad_seq)
+            at = pl.ds(pl.multiple_of(b * pad_seq, 16), pad_seq)
             mine = mixed[t, at, :]
             parts = []
             for h in range(heads):
@@ -543,29 +605,35 @@
                 s = jnp.where(key_ok, nt(q, k) * scale, -1e30)
                 e = jnp.exp(s - jnp.max(s, axis=-1, keepdims=True))
                 p = low(e / jnp.sum(e, axis=-1, keepdims=True))
-                probs[t, b, h] = p
+                if not extra:
+                    probs[t, b, h] = p
                 parts.append(low(nn(p, v)))
             context[t, at, :] = jnp.concatenate(parts, axis=1)
             return inner
 
         lax.fori_loop(0, crops, crop_body, 0)
         attn_sum[...] += nt(context[t], matrix(0, t)[:, mix_cols:])
-        gather_tick(n_t + 2 + t)
+
+    def attend_step(k, carry):
+        at_step(k, {1: (("b", 3), ("b", 4), ("c", 3), ("b", 5),), 2: (("c", 4), ("a", 6), ("a", 7), ("a", 8),), 3: (("c", 5), ("b", 6), ("b", 7),)})
+        gather_part(0, k)
+        attend((z + n_t - k) % n_t)
         return carry
 
-    lax.fori_loop(0, n_t, attend, 0)
-
-    def second_norm(i, carry):
+    lax.fori_loop(0, n_t, attend_step, 0)
+
+    def second_norm(i, carry, extra=False):
         at = chunk_at(i)
-        begin, _ = start_of(at)
+        begin, _ = start_of(at, extra)
         mid = begin + vec[2:3, :] * (attn_sum[at, :] + vec[3:4, :])
         middle[at, :] = mid
         hat, _ = normal(mid)
         norm_two[at, :] = low(hat * vec[4:5, :] + vec[5:6, :])
         return carry
 
+    gather_steps((("b", 8), ("c", 6), ("a", 9), ("a", 10), ("a", 11),))
     lax.fori_loop(0, n_chunks, second_norm, 0)
-    turned_two[...] = norm_two[...].T
+    gather_steps((("c", 7), ("c", 8), ("b", 9),))
     gather_end(1)
 
     def hidden_units(t, carry):
@@ -575,24 +643,23 @@
             at = chunk_at(i)
             h = wide_one[at, :]
             cdf = 0.5 + 0.5 * lax.erf(h * 0.7071067811865476)
-            active[t, at, :] = low(h * cdf)
-            slope[t, at, :] = low(cdf + h * jnp.exp(-0.5 * h * h) * 0.3989422804014327)
+            a, b, within = spot(i)
+            store[4, t, a, b, within] = low(h * cdf)
+            store[5, t, a, b, within] = low(cdf + h * jnp.exp(-0.5 * h * h) * 0.3989422804014327)
             return inner
 
         lax.fori_loop(0, n_chunks, bend, 0)
-        store[3, t] = low(nn(turned_mlp[...], active[t])).reshape(4, 2, unit, width)
-        reduce_tick(t)
-        gather_tick(2 * n_t + 2 + t)
+        at_step(t, {0: (("b", 10), ("b", 11), ("c", 9),), 1: (("c", 10),), 2: (("c", 11),)})
         return carry
 
     lax.fori_loop(0, n_t, hidden_units, 0)
-    gather_sent(1)
-    gather_end(2)
 
     wide_one[...] = jnp.zeros_like(wide_one)
 
-    def mlp_out(t, carry):
-        wide_one[...] += nt(active[t], matrix(2, t))
+    def mlp_out(k, carry):
+        gather_part(2, k)
+        t = (z + n_t - k) % n_t
+        wide_one[...] += nt(active_of(t), matrix(2, t))
         return carry
 
     lax.fori_loop(0, n_t, mlp_out, 0)
@@ -605,32 +672,53 @@
 
     mlp_total = lax.fori_loop(0, n_chunks, finish_block, zero8)
     sums[0, 6:7, :] = jnp.sum(mlp_total, axis=0, keepdims=True)
-    line_start(1, *line_block)
+    line_begin(line_block)
     own_block = pltpu.make_async_copy(result.at[0], out_block.at[z], own_sem.at[0])
     own_block.start()
-    gather_sent(2)
-
+
+    turned_one[...] = norm_two[...].T
+
+    def scale_cot(i, total):
+        at = chunk_at(i)
+        cot = wide(cot_in[at, :])
+        mlp_grad[at, :] = low(vec[6:7, :] * cot)
+        return total + fold(cot)
+
+    cot_total = lax.fori_loop(0, n_chunks, scale_cot, zero8)
+    sums[0, 7:8, :] = vec[6:7, :] * jnp.sum(cot_total, axis=0, keepdims=True)
+    turned_mlp[...] = mlp_grad[...].T
     wide_one[...] = jnp.zeros_like(wide_one)
     ones = jnp.ones((CHUNK, rows), jnp.bfloat16)
 
     def hidden_back(t, carry):
+        store[3, t] = low(nn(turned_mlp[...], active_of(t))).reshape(4, 2, unit, width)
+        reduce_tick(2 * t)
         wide_two[...] = nn(mlp_grad[...], matrix(2, t))
 
         def bend(i, inner):
             at = chunk_at(i)
-            slope[t, at, :] = low(wide(slope[t, at, :]) * wide_two[at, :])
+            a, b, within = spot(i)
+            store[5, t, a, b, within] = low(wide(store[5, t, a, b, within]) * wide_two[at, :])
             return inner
 
         lax.fori_loop(0, n_chunks, bend, 0)
-        sums[0, pl.ds(9 + n_t + t, 1), :] = nn(ones, slope[t])[:1]
-        store[2, t] = low(nn(turned_two[...], slope[t])).reshape(4, 2, unit, width)
-        wide_one[...] += nt(slope[t], matrix(1, t))
-        reduce_tick(n_t + t)
+        bent = slope_of(t)
+        sums[0, pl.ds(9 + n_t + t, 1), :] = nn(ones, bent)[:1]
+        store[4, t] = low(nn(turned_one[...], bent)).reshape(4, 2, unit, width)
+        wide_one[...] += nt(bent, matrix(1, t))
+        reduce_tick(2 * t + 1)
+
+        @pl.when(t == 1)
+        def _():
+            line_forward(0, line_block)
+
         return carry
 
     lax.fori_loop(0, n_t, hidden_back, 0)
-    line_recv(1, *line_block)
-    line_start(2, *line_block)
+    reduce_tick(2 * n_t)
+    next_copy = pltpu.make_async_copy(x_next, mlp_grad, own_sem.at[2])
+    next_copy.start()
+    turned_one[...] = norm_one[...].T
 
     def second_back(i, totals):
         gain, shift, scale_one, bias_proj = totals
@@ -641,8 +729,8 @@
         inner = e - jnp.mean(e, axis=-1, keepdims=True)
         inner = inner - hat * jnp.mean(e * hat, axis=-1, keepdims=True)
         g = wide(cot_in[at, :]) + rate * inner
-        grad_mid[at, :] = g
-        attn_grad[at, :] = low(vec[2:3, :] * g)
+        wide_two[at, :] = g
+        norm_two[at, :] = low(vec[2:3, :] * g)
         return (
             gain + fold(upstream * hat),
             shift + fold(upstream),
@@ -655,61 +743,78 @@
     sums[0, 5:6, :] = jnp.sum(shift, axis=0, keepdims=True)
     sums[0, 2:3, :] = jnp.sum(scale_one, axis=0, keepdims=True)
     sums[0, 3:4, :] = vec[2:3, :] * jnp.sum(bias_proj, axis=0, keepdims=True)
-    turned_attn[...] = attn_grad[...].T
+    reduce_tick(2 * n_t + 1)
+    turned_mlp[...] = norm_two[...].T
+    line_forward(1, line_block)
     wide_one[...] = jnp.zeros_like(wide_one)
 
-    def attend_back(t, carry):
-        gctx = low(nn(attn_grad[...], matrix(0, t)[:, mix_cols:]))
-        gmixed[:, :head_cols] = gctx
-
-        def crop_body(b, inner):
-            at = pl.ds(pl.multiple_of(b * pad_seq, CHUNK), pad_seq)
-            mine = mixed[t, at, :]
-            theirs = gmixed[at, :head_cols]
-            gq, gk, gv = [], [], []
-            for h in range(heads):
-                q = mine[:, h * HD : (h + 1) * HD]
-                k = mine[:, head_cols + h * HD : head_cols + (h + 1) * HD]
-                v = mine[:, 2 * head_cols + h * HD : 2 * head_cols + (h + 1) * HD]
-                g = theirs[:, h * HD : (h + 1) * HD]
-                p_low = probs[t, b, h]
-                p = wide(p_low)
-                gp = nt(g, v)
-                gs = low(p * (gp - jnp.sum(gp * p, axis=-1, keepdims=True)))
-                gq.append(low(nn(gs, k) * scale))
-                gk.append(low(tn(gs, q) * scale))
-                gv.append(low(tn(p_low, g)))
-            gmixed[at, :] = jnp.concatenate(gq + gk + gv, axis=1)
-            return inner
-
-        lax.fori_loop(0, crops, crop_body, 0)
-        sums[0, pl.ds(9 + t, 1), :mix_cols] = nn(ones, gmixed[...])[:1]
-        fresh = jnp.concatenate(
-            [
-                low(nn(turned_one[...], gmixed[...])),
-                low(nn(turned_attn[...], context[t])),
-            ],
-            axis=1,
-        )
-        store[1, t] = fresh.reshape(4, 2, unit, width)
-        wide_one[...] += nt(gmixed[...], matrix(0, t)[:, :mix_cols])
-        reduce_tick(2 * n_t + t)
+    def attend_back(i, carry):
+        b, turn = i // n_t, i % n_t
+        t = late_group(turn)
+        at = pl.ds(pl.multiple_of(b * pad_seq, 16), pad_seq)
+        theirs = low(nn(norm_two[at, :], matrix(0, t)[:, mix_cols:]))
+        mine = mixed[t, at, :]
+        gq, gk, gv = [], [], []
+        for h in range(heads):
+            q = mine[:, h * HD : (h + 1) * HD]
+            k = mine[:, head_cols + h * HD : head_cols + (h + 1) * HD]
+            v = mine[:, 2 * head_cols + h * HD : 2 * head_cols + (h + 1) * HD]
+            g = theirs[:, h * HD : (h + 1) * HD]
+            p_low = probs[t, b, h]
+            p = wide(p_low)
+            gp = nt(g, v)
+            gs = low(p * (gp - jnp.sum(gp * p, axis=-1, keepdims=True)))
+            gq.append(low(nn(gs, k) * scale))
+            gk.append(low(tn(gs, q) * scale))
+            gv.append(low(tn(p_low, g)))
+        fresh = jnp.concatenate(gq + gk + gv, axis=1)
+        mixed[t, at, :] = fresh
+        wide_one[at, :] += nt(fresh, matrix(0, t)[:, :mix_cols])
+
+        @pl.when(b == 0)
+        def _():
+            reduce_tick(2 * n_t + 2 + turn)
+
+        @pl.when(b == 1)
+        def _():
+            sums[0, pl.ds(9 + t, 1), :mix_cols] = nn(ones, mixed[t])[:1]
+            grads = jnp.concatenate(
+                [
+                    low(nn(turned_one[...], mixed[t])),
+                    low(nn(turned_mlp[...], context[t])),
+                ],
+                axis=1,
+            )
+            store[5, t] = grads.reshape(4, 2, unit, width)
+            reduce_tick(late_jobs + 2 * turn)
+            reduce_tick(late_jobs + 2 * turn + 1)
+
+        for key, (q, refs) in {
+            1: (2, line_block),
+            3: (3, line_block),
+            5: (4, line_block),
+            6: (0, line_tokens),
+        }.items():
+
+            @pl.when(i == key)
+            def _():
+                line_forward(q, refs)
+
+        @pl.when(turn == n_t - 1)
+        def _():
+            start_back(b)
+
         return carry
 
-    lax.fori_loop(0, n_t, attend_back, 0)
-    line_recv(2, *line_block)
-    line_start(3, *line_block)
-
-    def first_back(i, totals):
+    def first_back(at, totals):
         gain, shift, token = totals
-        at = chunk_at(i)
         upstream = wide_one[at, :]
         begin, chosen = start_of(at)
         hat, rate = normal(begin)
         e = vec[0:1, :] * upstream
         inner = e - jnp.mean(e, axis=-1, keepdims=True)
         inner = inner - hat * jnp.mean(e * hat, axis=-1, keepdims=True)
-        g = grad_mid[at, :] + rate * inner
+        g = wide_two[at, :] + rate * inner
         result[1, at, :] = low(jnp.where(chosen, 0.0, g))
         return (
             gain + fold(upstream * hat),
@@ -717,26 +822,137 @@
             token + fold(jnp.where(chosen, g, 0.0)),
         )
 
-    gain, shift, token = lax.fori_loop(0, n_chunks, first_back, (zero8,) * 3)
-    sums[0, 0:1, :] = jnp.sum(gain, axis=0, keepdims=True)
-    sums[0, 1:2, :] = jnp.sum(shift, axis=0, keepdims=True)
-    sums[0, 8:9, :] = jnp.sum(token, axis=0, keepdims=True)
-    line_start(1, *line_tokens)
+    def start_back(b):
+        base = b * pad_seq
+        full = pad_seq // CHUNK
+
+        def body(i, totals):
+            at = pl.ds(pl.multiple_of(base + i * CHUNK, 16), CHUNK)
+            return first_back(at, totals)
+
+        totals = lax.fori_loop(0, full, body, (zero8,) * 3)
+        if pad_seq % CHUNK:
+            at = pl.ds(pl.multiple_of(base + full * CHUNK, 16), pad_seq % CHUNK)
+            totals = first_back(at, totals)
+        for row, total in zip((0, 1, 8), totals):
+            sums[0, row : row + 1, :] += jnp.sum(total, axis=0, keepdims=True)
+        for q in range(crops):
+
+            @pl.when(b == q)
+            def _():
+                line_go(q, "start", line_tokens)
+
+    lax.fori_loop(0, crops * n_t, attend_back, 0)
     own_tokens = pltpu.make_async_copy(result.at[1], out_tokens.at[z], own_sem.at[1])
     own_tokens.start()
 
     sum_start(0, grad_sums)
-    for step in range(3):
-        reduce_tick(n_jobs + step)
-        sum_finish(step, grad_sums)
-        sum_start(step + 1, grad_sums)
-    for m in (2, 1, 0):
-        for k in range(1, n_t):
-            rs_line_in(m, k).wait_recv()
-        total = shard_out[m]
-        for k in range(1, n_t):
-            total = total + wide(line_in[m, k - 1])
-        shard_out[m] = total
+    next_copy.wait()
+    at_end = jnp.logical_or(z == 0, z == n_t - 1)
+    beside = jnp.where(z == 0, 1, n_t - 2)
+
+    @pl.when(at_end)
+    def _():
+        lax.fori_loop(0, n_chunks, functools.partial(first_norm, extra=True), 0)
+        attn_sum[...] = jnp.zeros_like(attn_sum)
+
+    reduce_tick(n_slots)
+    sum_finish(0, grad_sums)
+    sum_start(1, grad_sums)
+
+    def attend_more(t, carry):
+        @pl.when(at_end)
+        def _():
+            attend((beside + n_t - t) % n_t, extra=True)
+
+        reduce_tick(n_slots + 1 + t)
+
+        @pl.when(t == 0)
+        def _():
+            line_forward(2, line_tokens)
+
+        @pl.when(t == 1)
+        def _():
+            sum_finish(1, grad_sums)
+            sum_start(2, grad_sums)
+
+        @pl.when(t == 2)
+        def _():
+            line_forward(1, line_tokens)
+
+        @pl.when(t == 3)
+        def _():
+            sum_finish(2, grad_sums)
+            sum_start(3, grad_sums)
+
+        return carry
+
+    lax.fori_loop(0, n_t, attend_more, 0)
+    reduce_tick(n_slots + n_t + 1)
+
+    @pl.when(at_end)
+    def _():
+        lax.fori_loop(0, n_chunks, functools.partial(second_norm, extra=True), 0)
+        wide_two[...] = jnp.zeros_like(wide_two)
+
+    reduce_tick(n_slots + n_t + 2)
+
+    def hidden_more(k, carry):
+        t = (beside + n_t - k) % n_t
+
+        @pl.when(at_end)
+        def _():
+            wide_one[...] = nn(norm_two[...], matrix(1, t)) + bias_all[t, 1:2, :]
+
+            def bend(i, inner):
+                at = chunk_at(i)
+                h = wide_one[at, :]
+                mlp_grad[at, :] = low(h * (0.5 + 0.5 * lax.erf(h * 0.7071067811865476)))
+                return inner
+
+            lax.fori_loop(0, n_chunks, bend, 0)
+            wide_two[...] += nt(mlp_grad[...], matrix(2, t))
+
+        reduce_tick(n_slots + n_t + 3 + k)
+
+        @pl.when(k == 0)
+        def _():
+            line_forward(3, line_tokens)
+
+        return carry
+
+    lax.fori_loop(0, n_t, hidden_more, 0)
+    for step in range(2 * n_t + 3, LAG * (n_t + 1)):
+        reduce_tick(n_slots + step)
+    line_forward(n_hops - 1, line_block)
+    for q in range(crops):
+        line_go(q, "wait_send", line_block)
+    own_block.wait()
+    more_block = pltpu.make_async_copy(result.at[0], out_block.at[beside], own_sem.at[0])
+
+    @pl.when(at_end)
+    def _():
+        def finish_more(i, carry):
+            at = chunk_at(i)
+            mlp = wide_two[at, :] + vec[7:8, :]
+            result[0, at, :] = low(middle[at, :] + vec[6:7, :] * mlp)
+            return carry
+
+        lax.fori_loop(0, n_chunks, finish_more, 0)
+        more_block.start()
+
+    @pl.when(z > 0)
+    def _():
+        for m in range(PIECES):
+            rs_line_in(m, z).wait_recv()
+            shard_out[m] = shard_out[m] + wide(line_in[m, z])
+
+    @pl.when(z < n_t - 1)
+    def _():
+        for m in range(PIECES):
+            rs_line_in(m, n_t).wait_recv()
+            shard_out[m] = shard_out[m] + wide(line_in[m, n_t])
+
     sums_out[...] = sum_finish(3, grad_sums)
     own_out[0:1, :] = sums_out[pl.ds(9 + z, 1), :]
     own_out[1:2, :] = sums_out[pl.ds(9 + n_t + z, 1), :]
@@ -747,22 +963,36 @@
         for m in range(PIECES):
             squares = squares + square_sum(shard_out[m])
         tiles[0] = jnp.full(tiles.shape[1:], 1.0, jnp.float32) * squares
-        for step in range(4):
-            sum_start(step, square_sums)
-            total = sum_finish(step, square_sums)
+        tiles_in[place] = tiles[0]
+        for i in range(GROUP - 1):
+            tile_copy(i).start()
+        for i in range(GROUP - 1):
+            tile_copy(i).wait_recv()
+        total = tiles_in[0]
+        for i in range(1, GROUP):
+            total = total + tiles_in[i]
+        tiles[1] = total
+        tiles_z[z] = total
+        for i in range(GROUP - 1, n_tiles):
+            tile_copy(i).start()
+        for i in range(GROUP - 1, n_tiles):
+            tile_copy(i).wait_recv()
+        total = tiles_z[0]
+        for k in range(1, n_t):
+            total = total + tiles_z[k]
         square_out[...] = total
-        sum_sent(square_sums)
+        for i in range(n_tiles):
+            tile_copy(i).wait_send()
     else:
         square_out[...] = jnp.zeros_like(square_out)
-    line_recv(1, *line_tokens)
-    line_start(2, *line_tokens)
-    line_recv(2, *line_tokens)
-    line_start(3, *line_tokens)
+    for q in range(4, n_hops):
+        line_forward(q, line_tokens)
     sum_sent(grad_sums)
     for k in range(1, n_t):
         bias_copy(k).wait_send()
 
-    gather_sent(0)
+    for m in range(PIECES):
+        gather_sent(m)
 
     def sent(j, carry):
         rs_core(j).wait_send()
@@ -770,23 +1000,31 @@
             rs_diag(j, axis).wait_send()
             rs_direct(j, axis).wait_send()
 
-        @pl.when(j % n_t != z)
+        slot, t = job_slot(j)
+
+        @pl.when(t > z)
         def _():
-            rs_line_out(j).wait_send()
+            rs_line(slot, t, True).wait_send()
+
+        @pl.when(t < z)
+        def _():
+            rs_line(slot, t, False).wait_send()
 
         return carry
 
-    lax.fori_loop(0, n_jobs, sent, 0)
-    line_recv(3, *line_block)
-    line_recv(3, *line_tokens)
-    for s in (1, 2, 3):
-        line_sent(s, *line_block)
-        line_sent(s, *line_tokens)
-    own_block.wait()
+    lax.fori_loop(0, 2 * n_t, sent, 0)
+    lax.fori_loop(0, n_t, lambda t, carry: sent(late_jobs + 2 * t, carry), 0)
+    line_end(line_block, crops)
+    line_end(line_tokens)
+
+    @pl.when(at_end)
+    def _():
+        more_block.wait()
+
     own_tokens.wait()
 
 
-def run_block(dims, pack, x_in, cot_in, mask_in, vec, bias_own):
+def run_block(dims, pack, x_in, x_next, cot_in, mask_in, vec, bias_own):
     n_dp, n_t, seq, pad_seq, crops, heads = dims
     unit, width = pack.shape[1:]
     rows = crops * pad_seq
@@ -809,10 +1047,10 @@
             jax.ShapeDtypeStruct((2, width), f32),
             jax.ShapeDtypeStruct((8, 128), f32),
         ),
-        in_specs=[inside] * 6,
+        in_specs=[inside, inside, outside, inside, inside, inside, inside],
         out_specs=(outside, outside, inside, inside, inside, inside),
         scratch_shapes=[
-            vmem((4, n_t, 4, 2, unit, width), bf16),
+            vmem((6, n_t, 4, 2, unit, width), bf16),
             vmem((rows, width), bf16),
             vmem((width, rows), bf16),
             vmem((n_t, rows, mix_cols), bf16),
@@ -821,28 +1059,21 @@
             vmem((rows, width), f32),
             vmem((rows, width), f32),
             vmem((rows, width), bf16),
-            vmem((width, rows), bf16),
             vmem((rows, width), bf16),
             vmem((width, rows), bf16),
-            vmem((n_t, rows, width), bf16),
-            vmem((n_t, rows, width), bf16),
             vmem((rows, width), f32),
             vmem((rows, width), f32),
-            vmem((rows, width), f32),
-            vmem((rows, width), bf16),
-            vmem((width, rows), bf16),
-            vmem((rows, mix_cols), bf16),
             vmem((2, rows, width), bf16),
-            vmem((2, 4, unit, width), bf16),
-            vmem((2, 2, unit // 2, width), bf16),
-            vmem((2, 2, unit, width), bf16),
-            vmem((PIECES, n_t - 1, unit, width), bf16),
+            vmem((RING, 4, unit, width), bf16),
+            vmem((RING, 2, unit // 2, width), bf16),
+            vmem((RING, 2, unit, width), bf16),
+            vmem((PIECES, n_t + 1, unit, width), bf16),
             vmem((n_t, 8, width), f32),
             vmem((4, n_sums, width), f32),
             vmem((3, n_sums, width), f32),
             vmem((n_t, n_sums, width), f32),
-            vmem((4, 8, 128), f32),
-            vmem((3, 8, 128), f32),
+            vmem((2, 8, 128), f32),
+            vmem((GROUP, 8, 128), f32),
             vmem((n_t, 8, 128), f32),
             dma((PIECES, n_t - 1)),
             dma((PIECES, n_t - 1)),
@@ -852,31 +1083,112 @@
             dma((n_jobs, 2)),
             dma((n_jobs, 4)),
             dma((n_jobs, 4)),
-            dma((n_jobs,)),
-            dma((n_jobs,)),
-            dma((n_jobs, 2)),
-            dma((n_jobs, 2)),
-            dma((n_jobs, 2)),
-            dma((n_jobs, 2)),
-            dma((n_jobs,)),
-            dma((PIECES, n_t - 1)),
-            dma((2, n_t - 1)),
-            dma((2, n_t - 1)),
-            dma((2, n_t - 1)),
-            dma((2, n_t - 1)),
-            dma((2,)),
+            dma((5 * n_t + 2,)),
+            dma((5 * n_t + 2,)),
+            dma((5 * n_t + 2, 2)),
+            dma((5 * n_t + 2, 2)),
+            dma((5 * n_t + 2, 2)),
+            dma((5 * n_t + 2, 2)),
+            dma((PIECES, n_t)),
+            dma((PIECES, n_t + 1)),
+            dma((2, crops * (n_t - 1))),
+            dma((2, crops * (n_t - 1))),
+            dma((2, crops * (n_t - 1))),
+            dma((2, crops * (n_t - 1))),
+            dma((3,)),
             dma((n_t - 1,)),
             dma((n_t - 1,)),
             dma((n_t + 2,)),
             dma((n_t + 2,)),
-            dma((n_t + 2,)),
-            dma((n_t + 2,)),
+            dma((GROUP + n_t - 2,)),
+            dma((GROUP + n_t - 2,)),
         ],
         compiler_params=pltpu.CompilerParams(
-            collective_id=0, has_side_effects=True, vmem_limit_bytes=62 * 1024 * 1024
+            collective_id=0, has_side_effects=True, vmem_limit_bytes=63 * 1024 * 1024
         ),
         name="block_step",
-    )(pack, x_in, cot_in, mask_in, vec, bias_own)
+    )(pack, x_in, x_next, cot_in, mask_in, vec, bias_own)
+
+
+def prepare_kernel(
+    dims,
+    tokens,
+    cot,
+    mask,
+    qkv,
+    proj,
+    up,
+    down,
+    head_bias,
+    up_bias,
+    x_in,
+    x_next,
+    cot_in,
+    mask_in,
+    pack,
+    bias_own,
+    landing,
+    sems,
+):
+    n_dp, n_t, seq, pad_seq, crops, heads = dims
+    z = lax.axis_index("tensor")
+    mine = z * crops
+    other = jnp.where(z == 0, 1, n_t - 2) * crops
+    copies = []
+    for source, base in ((tokens, mine), (cot, mine), (tokens, other)):
+        for b in range(crops):
+            i = len(copies)
+            copies.append(pltpu.make_async_copy(source.at[base + b], landing.at[i], sems.at[i]))
+            copies[-1].start()
+    pack[0] = low(jnp.concatenate([qkv[0], qkv[1], qkv[2], proj[...].T], axis=1))
+    pack[1] = low(up[...])
+    pack[2] = low(down[...])
+    cols = head_bias.shape[1]
+    spare = jnp.zeros((1, up_bias.shape[1] - 3 * cols), jnp.float32)
+    none = jnp.zeros((1, cols), jnp.float32)
+    bias_own[...] = jnp.zeros_like(bias_own)
+    bias_own[0:1, :] = jnp.concatenate([head_bias[0:1, :], none, head_bias[1:2, :], spare], axis=1)
+    bias_own[1:2, :] = up_bias[...]
+    for b in range(crops):
+        columns = []
+        for base in (mine, other):
+            line = jnp.broadcast_to(mask[pl.ds(base + b, 1), :], (8, mask.shape[1]))
+            columns.append(line.T[:pad_seq, :1])
+        mask_in[b * pad_seq : (b + 1) * pad_seq, :] = jnp.concatenate(columns, axis=1)
+    for target in (x_in, cot_in, x_next):
+        target[...] = jnp.zeros_like(target)
+    for i, copy in enumerate(copies):
+        copy.wait()
+        begin = i % crops * pad_seq
+        (x_in, cot_in, x_next)[i // crops][begin : begin + seq, :] = landing[i]
+
+
+def run_prepare(dims, *arrays):
+    n_dp, n_t, seq, pad_seq, crops, heads = dims
+    unit, width = arrays[5].shape
+    rows = crops * pad_seq
+    inside = pl.BlockSpec(memory_space=pltpu.VMEM)
+    outside = pl.BlockSpec(memory_space=pl.ANY)
+    activation = jax.ShapeDtypeStruct((rows, width), jnp.bfloat16)
+    return pl.pallas_call(
+        functools.partial(prepare_kernel, dims),
+        out_shape=(
+            activation,
+            activation,
+            activation,
+            jax.ShapeDtypeStruct((rows, 2), jnp.float32),
+            jax.ShapeDtypeStruct((PIECES, unit, width), jnp.bfloat16),
+            jax.ShapeDtypeStruct((8, width), jnp.float32),
+        ),
+        in_specs=[outside, outside] + [inside] * (len(arrays) - 2),
+        out_specs=(inside,) * 6,
+        scratch_shapes=[
+            pltpu.VMEM((3 * crops, seq, width), jnp.bfloat16),
+            pltpu.SemaphoreType.DMA((3 * crops,)),
+        ],
+        compiler_params=pltpu.CompilerParams(vmem_limit_bytes=32 * 1024 * 1024),
+        name="prepare",
+    )(*arrays)
 
 
 def adam_kernel(*refs):
@@ -909,7 +1221,7 @@
         update(0, mixed[:, j * cols : (j + 1) * cols], rate_matrix, decay_matrix, j)
     update(1, mixed[:, 3 * cols :].T, rate_matrix, decay_matrix)
     update(2, shard[1], rate_matrix, decay_matrix)
-    update(3, shard[2].T, rate_matrix, decay_matrix)
+    update(3, shard[2], rate_matrix, decay_matrix)
     update(4, sums[0:9, :], rate_vector, 0.0)
     mix = own_sums[0:1, :]
     heads = jnp.concatenate([mix[:, :cols], mix[:, 2 * cols : 3 * cols]], axis=0)
@@ -970,33 +1282,52 @@
     rows = crops * pad_seq
     stride = n_dp // GROUP
 
-    def padded(array):
-        here = lax.dynamic_slice_in_dim(array, tensor_at * crops, crops, 0)
-        spare = [(0, 0), (0, pad_seq - seq), (0, 0)]
-        return jnp.pad(here, spare).reshape(rows, -1)
-
-    x_in = padded(tokens)
-    cot_in = padded(cotangent)
-    mask_all = jnp.pad(patch_mask, [(0, 0), (1 + REG, 0)]).astype(jnp.float32)
-    mask_in = padded(mask_all[:, :, None])
-    pack = jnp.stack(
-        [
-            jnp.concatenate(
-                [qkv_weight[0], qkv_weight[1], qkv_weight[2], proj_weight.T], axis=1
-            ),
+    dims = (n_dp, n_t, seq, pad_seq, crops, heads)
+    teams = [[b * stride + i for i in range(stride)] for b in range(GROUP)]
+    if stride == 1:
+        lanes = -(-pad_seq // 128) * 128
+        margins = [(0, 0), (1 + REG, lanes - patch_mask.shape[1] - 1 - REG)]
+        x_in, x_next, cot_in, mask_in, pack, bias_own = run_prepare(
+            dims,
+            tokens,
+            cotangent,
+            jnp.pad(patch_mask, margins).astype(jnp.float32),
+            qkv_weight,
+            proj_weight,
             fc1_weight,
             fc2_weight.T,
-        ]
-    ).astype(jnp.bfloat16)
-    if stride > 1:
-        teams = [[b * stride + i for i in range(stride)] for b in range(GROUP)]
+            head_bias,
+            fc1_bias[None],
+        )
+    else:
+        beside = jnp.where(tensor_at == 0, 1, n_t - 2)
+
+        def padded(array, at=tensor_at):
+            here = lax.dynamic_slice_in_dim(array, at * crops, crops, 0)
+            spare = [(0, 0), (0, pad_seq - seq), (0, 0)]
+            return jnp.pad(here, spare).reshape(rows, -1)
+
+        x_in = padded(tokens)
+        x_next = padded(tokens, beside)
+        cot_in = padded(cotangent)
+        mask_all = jnp.pad(patch_mask, [(0, 0), (1 + REG, 0)]).astype(jnp.float32)
+        mask_all = mask_all[:, :, None]
+        mask_in = jnp.concatenate([padded(mask_all), padded(mask_all, beside)], axis=1)
+        pack = jnp.stack(
+            [
+                jnp.concatenate(
+                    [qkv_weight[0], qkv_weight[1], qkv_weight[2], proj_weight.T], axis=1
+                ),
+                fc1_weight,
+                fc2_weight.T,
+            ]
+        ).astype(jnp.bfloat16)
         pack = lax.all_gather(pack, "dp", axis_index_groups=teams, axis=1, tiled=True)
-    mix_row = jnp.concatenate([head_bias[0], jnp.zeros((head_cols,), jnp.float32), head_bias[1]])
-    mix_row = jnp.pad(mix_row, (0, width - 3 * head_cols))
-    bias_own = jnp.pad(jnp.stack([mix_row, fc1_bias]), [(0, 6), (0, 0)])
-    dims = (n_dp, n_t, seq, pad_seq, crops, heads)
+        mix_row = jnp.concatenate([head_bias[0], jnp.zeros((head_cols,), jnp.float32), head_bias[1]])
+        mix_row = jnp.pad(mix_row, (0, width - 3 * head_cols))
+        bias_own = jnp.pad(jnp.stack([mix_row, fc1_bias]), [(0, 6), (0, 0)])
     block_all, grad_all, shard, sums, own_sums, square_tile = run_block(
-        dims, pack, x_in, cot_in, mask_in, vectors, bias_own
+        dims, pack, x_in, x_next, cot_in, mask_in, vectors, bias_own
     )
 
     def whole(array):
@@ -1013,7 +1344,7 @@
             (qkv_weight, qkv_first, qkv_second),
             (proj_weight, proj_first, proj_second),
             (fc1_weight, fc1_first, fc1_second),
-            (fc2_weight, fc2_first, fc2_second),
+            (fc2_weight.T, fc2_first.T, fc2_second.T),
             (vectors, vectors_first, vectors_second),
             (head_bias, head_bias_first, head_bias_second),
             (fc1_bias[None], fc1_bias_first[None], fc1_bias_second[None]),
@@ -1022,6 +1353,8 @@
         updated = list(updated[1:])
         for at in (18, 19, 20):
             updated[at] = updated[at][0]
+        for at in (9, 10, 11, 24):
+            updated[at] = updated[at].T
         return (block_out, tokens_grad, norm_tile[0, 0], *updated)
     both = ("dp", "tensor")
     shard = lax.psum_scatter(

time: 301 us -> 253 us (0.84)
  Pallas kernels: 269 us -> 228 us
  other arithmetic: 7.16 us -> 2.58 us
  local copies, waits for them, and re-layouts: 23.4 us -> 20.1 us
    pallas_call x1, Pallas kernels: 267 us -> 224 us  [run_block(): pl.pallas_call(functools.partial(block_kernel, dims), out_shape=(jax.Shap...]
    dynamic_slice x1 -> x0, local copies, waits for them, and re-layouts: 4.54 us -> none  [padded(): here = lax.dynamic_slice_in_dim(array, tensor_at * crops, crops, 0)]
    another operation x6 -> x0, other arithmetic: 4.5 us -> none  [the longest x4 2.9 us: per_device(): jnp.stack([jnp.concatenate([qkv_weight[0], qkv_weight[1], qkv_weight[2],...]
    unnamed x58 -> x74, local copies, waits for them, and re-layouts: 10.3 us -> 13.8 us
where the time goes in v4:
time: 253 us; the launch traced here: 252 us
  Pallas kernels  228 us (90%)
  local copies, waits for them, and re-layouts  20.1 us (8%)
  other arithmetic  2.58 us (1%)
    pallas_call x1, Pallas kernels, run_block(): pl.pallas_call(functools.partial(block_kernel, dims), out_shape=(jax.Shap...  224 us
    unnamed x74, local copies, waits for them, and re-layouts  13.8 us

profile of v4, /device:TPU:0, one launch (start us, length us, event | category | flops | bytes accessed | tf_op | source)
XLA Modules:
  0.0 252.2 jit_solution(13607401501838063385)
XLA Ops:
  0.7 0.7 broadcast_in_dim.10.up_bias.refs_22_
  1.4 1.4 broadcast_in_dim.11.refs_23_
  2.8 1.3 broadcast_in_dim.12.refs_24_
  4.0 0.8 pad_convert_fusion.mask
  4.8 2.5 %copy.52.tokens = bf16[8,261,768]{2,1,0:T(8,128)(2,1)S(1)} copy(bf16[8,261,768]{2,0,1:T(8,128)(2,1)} %param.24) | data formatting | bytes 6414336 | tf_op args[0]
  7.4 0.0 copy-start
  7.4 0.0 copy-start.1
  7.4 0.0 copy-start.2
  7.4 0.0 copy-start.8
  7.4 0.0 copy-start.27
  7.4 0.6 copy.53.cot
  8.1 0.3 copy-done
  8.3 0.1 copy-done.1
  8.4 0.1 copy-done.2
  8.5 0.0 copy-done.8
  8.5 2.0 prepare.1
  10.5 0.0 copy-start.4
  10.5 0.9 copy-done.4
  11.4 0.9 copy-done.5
  12.3 1.0 copy-done.6
  13.3 0.8 copy-done.7
  14.1 0.7 copy-done.15
  14.8 0.6 copy-done.24
  15.5 223.9 %block_step.1 = (bf16[4,544,768]{2,1,0:T(8,128)(2,1)}, bf16[4,544,768]{2,1,0:T(8,128)(2,1)}, f32[3,96,768]{2,1,0:T(8,128)}, f32[24,768]{1,0:T(8,128)}, f32[2,768]{1,0:T(2,128)}, /*index=5*/f32[8,128]{1,0:T(8,128)}) custom-call(bf16[3,96,768]{2,1,0:T(8,128)(2,1)} %copy-done.7, bf16[544,768]{1,0:T(8,128)(2,1)} %copy-done.4, bf16[544,768]{1,0:T(8,128)(2,1)} %copy-done.5, ...), custom_call_target="tpu_custom_call" | custom-call | tf_op jit(solution)/shard_map/block_step/pallas_call | solution.py:1040
  239.4 2.1 slice.12
  241.5 2.3 copy.56
  243.8 0.5 copy-done.34
  244.4 0.2 slice.13
  244.6 0.0 copy-start.9
  244.6 0.0 copy-start.10
  244.6 0.0 copy-start.11
  244.6 0.0 copy-start.12
  244.6 0.0 copy-start.13
  244.7 0.0 copy-start.14
  244.7 0.0 copy-start.16
  244.7 0.0 copy-start.17
  244.7 0.0 copy-start.18
  244.7 0.0 copy-start.20
  244.7 0.0 copy-start.23
  244.8 0.0 copy-start.25
  244.8 0.0 copy-start.31
  244.8 0.0 copy-start.32
  244.8 2.3 copy.57
  247.3 2.6 %adam_step.1 = (f32[8,128]{1,0:T(8,128)S(1)}, f32[3,96,192]{2,1,0:T(8,128)}, f32[3,96,192]{2,1,0:T(8,128)}, f32[3,96,192]{2,1,0:T(8,128)}, f32[192,96]{1,0:T(8,1...) custom-call(f32[3,96,768]{2,1,0:T(8,128)S(1)} %copy-done.3, ...), custom_call_target="tpu_custom_call" | custom-call | tf_op jit(solution)/shard_map/adam_step/pallas_call | solution.py:1238
  249.9 0.5 slice.11
  250.4 0.6 reduce
  251.0 0.6 reduce.1
  251.6 0.6 reduce.2
  (39 shorter events, 0.1 us)
Async XLA Ops:
  1.4 6.7 %copy-start.22 = (f32[1,768]{1,0:T(1,128)}, f32[1,768]{1,0:T(1,128)S(1)}, u32[]{:S(2)}) copy-start(f32[1,768]{1,0:T(1,128)S(1)} %broadcast_in_dim.10.up_bias.refs_22_) | copy-start | bytes 9220
  1.4 6.0 %copy-start.33 = (bf16[8,261,768]{2,0,1:T(8,128)(2,1)S(1)}, bf16[8,261,768]{2,0,1:T(8,128)(2,1)}, u32[]{:S(2)}) copy-start(bf16[8,261,768]{2,0,1:T(8,128)(2,1)} %param.26) | copy-start | bytes 9621508
  7.4 1.0 copy-start
  7.4 1.0 copy-start.1
  7.4 1.1 copy-start.2
  7.4 1.1 copy-start.8
  7.4 1.1 copy-start.27
  10.5 0.9 copy-start.4
  11.4 0.9 copy-start.5
  12.3 1.0 copy-start.6
  13.3 0.8 copy-start.7
  14.1 0.7 copy-start.15
  14.8 0.6 copy-start.24
  241.5 2.8 %copy-start.34 = (bf16[4,544,768]{2,1,0:T(8,128)(2,1)S(1)}, bf16[4,544,768]{2,1,0:T(8,128)(2,1)}, u32[]{:S(2)}) copy-start(bf16[4,544,768]{2,1,0:T(8,128)(2,1)} %get-tuple-element.73) | copy-start | bytes 10027012
  244.6 2.5 %copy-start.3 = (f32[3,96,768]{2,1,0:T(8,128)S(1)}, f32[3,96,768]{2,1,0:T(8,128)}, u32[]{:S(2)}) copy-start(f32[3,96,768]{2,1,0:T(8,128)} %get-tuple-element.74.refs_0_) | copy-start | bytes 2654212
  244.6 2.5 %copy-start.9 = (f32[3,96,192]{2,1,0:T(8,128)S(1)}, f32[3,96,192]{2,1,0:T(8,128)}, u32[]{:S(2)}) copy-start(f32[3,96,192]{2,1,0:T(8,128)} %refs_5_.1) | copy-start | bytes 663556
  244.6 2.5 %copy-start.10 = (f32[3,96,192]{2,1,0:T(8,128)S(1)}, f32[3,96,192]{2,1,0:T(8,128)}, u32[]{:S(2)}) copy-start(f32[3,96,192]{2,1,0:T(8,128)} %refs_6_.1) | copy-start | bytes 663556
  244.6 2.5 copy-start.11
  244.6 2.5 copy-start.12
  244.6 2.5 copy-start.13
  244.7 2.5 copy-start.14
  244.7 2.5 copy-start.16
  244.7 2.5 copy-start.17
  244.7 2.5 copy-start.18
  244.7 2.5 copy-start.19
  244.7 2.5 copy-start.20
  244.7 2.5 copy-start.21
  244.7 2.5 copy-start.23
  244.8 2.5 copy-start.25
  244.8 2.5 copy-start.26
  244.8 2.5 copy-start.28
  244.8 2.5 copy-start.29
  244.8 2.5 copy-start.30
  244.8 2.5 copy-start.31
  244.8 2.5 copy-start.32

commit v5 on v4

--- a/solution.py
+++ b/solution.py
@@ -708,9 +708,11 @@
         wide_one[...] += nt(bent, matrix(1, t))
         reduce_tick(2 * t + 1)
 
-        @pl.when(t == 1)
-        def _():
-            line_forward(0, line_block)
+        for q in range(crops):
+
+            @pl.when(t == 2 * q)
+            def _():
+                line_forward(q, line_block)
 
         return carry
 
@@ -745,7 +747,7 @@
     sums[0, 3:4, :] = vec[2:3, :] * jnp.sum(bias_proj, axis=0, keepdims=True)
     reduce_tick(2 * n_t + 1)
     turned_mlp[...] = norm_two[...].T
-    line_forward(1, line_block)
+    line_forward(2, line_block)
     wide_one[...] = jnp.zeros_like(wide_one)
 
     def attend_back(i, carry):
@@ -790,10 +792,8 @@
             reduce_tick(late_jobs + 2 * turn + 1)
 
         for key, (q, refs) in {
-            1: (2, line_block),
-            3: (3, line_block),
-            5: (4, line_block),
-            6: (0, line_tokens),
+            0: (3, line_block),
+            5: (0, line_tokens),
         }.items():
 
             @pl.when(i == key)
@@ -857,6 +857,7 @@
         attn_sum[...] = jnp.zeros_like(attn_sum)
 
     reduce_tick(n_slots)
+    line_forward(2, line_tokens)
     sum_finish(0, grad_sums)
     sum_start(1, grad_sums)
 
@@ -866,10 +867,6 @@
             attend((beside + n_t - t) % n_t, extra=True)
 
         reduce_tick(n_slots + 1 + t)
-
-        @pl.when(t == 0)
-        def _():
-            line_forward(2, line_tokens)
 
         @pl.when(t == 1)
         def _():
@@ -924,7 +921,8 @@
     lax.fori_loop(0, n_t, hidden_more, 0)
     for step in range(2 * n_t + 3, LAG * (n_t + 1)):
         reduce_tick(n_slots + step)
-    line_forward(n_hops - 1, line_block)
+    for q in range(4, n_hops):
+        line_forward(q, line_block)
     for q in range(crops):
         line_go(q, "wait_send", line_block)
     own_block.wait()

time: 253 us -> 250 us (0.988)
  no operation moved by 1% of the time
where the time goes in v5:
time: 250 us
  Pallas kernels  226 us (90%)
  local copies, waits for them, and re-layouts  20.1 us (8%)
  other arithmetic  2.58 us (1%)
    pallas_call x1, Pallas kernels, run_block(): pl.pallas_call(functools.partial(block_kernel, dims), out_shape=(jax.Shap...  222 us
    unnamed x74, local copies, waits for them, and re-layouts  13.8 us

profile of v5, /device:TPU:0, one launch (start us, length us, event | category | flops | bytes accessed | tf_op | source)
XLA Modules:
  0.0 250.0 jit_solution(368853576580490688)
XLA Ops:
  0.7 0.7 broadcast_in_dim.10.up_bias.refs_22_
  1.4 1.4 broadcast_in_dim.11.refs_23_
  2.8 1.3 broadcast_in_dim.12.refs_24_
  4.0 0.8 pad_convert_fusion.mask
  4.8 2.5 %copy.52.tokens = bf16[8,261,768]{2,1,0:T(8,128)(2,1)S(1)} copy(bf16[8,261,768]{2,0,1:T(8,128)(2,1)} %param.24) | data formatting | bytes 6414336 | tf_op args[0]
  7.4 0.0 copy-start
  7.4 0.0 copy-start.1
  7.4 0.0 copy-start.2
  7.4 0.0 copy-start.8
  7.4 0.0 copy-start.27
  7.4 0.6 copy.53.cot
  8.1 0.3 copy-done
  8.3 0.1 copy-done.1
  8.4 0.1 copy-done.2
  8.5 0.0 copy-done.8
  8.5 2.0 prepare.1
  10.5 0.0 copy-start.4
  10.5 0.9 copy-done.4
  11.4 0.9 copy-done.5
  12.3 1.0 copy-done.6
  13.3 0.8 copy-done.7
  14.1 0.7 copy-done.15
  14.8 0.6 copy-done.24
  15.5 221.7 %block_step.1 = (bf16[4,544,768]{2,1,0:T(8,128)(2,1)}, bf16[4,544,768]{2,1,0:T(8,128)(2,1)}, f32[3,96,768]{2,1,0:T(8,128)}, f32[24,768]{1,0:T(8,128)}, f32[2,768]{1,0:T(2,128)}, /*index=5*/f32[8,128]{1,0:T(8,128)}) custom-call(bf16[3,96,768]{2,1,0:T(8,128)(2,1)} %copy-done.7, bf16[544,768]{1,0:T(8,128)(2,1)} %copy-done.4, bf16[544,768]{1,0:T(8,128)(2,1)} %copy-done.5, ...), custom_call_target="tpu_custom_call" | custom-call | tf_op jit(solution)/shard_map/block_step/pallas_call | solution.py:1038
  237.2 2.1 slice.12
  239.3 2.3 copy.56
  241.6 0.5 copy-done.34
  242.2 0.2 slice.13
  242.4 0.0 copy-start.9
  242.4 0.0 copy-start.10
  242.4 0.0 copy-start.11
  242.4 0.0 copy-start.12
  242.5 0.0 copy-start.13
  242.5 0.0 copy-start.14
  242.5 0.0 copy-start.16
  242.5 0.0 copy-start.17
  242.5 0.0 copy-start.18
  242.5 0.0 copy-start.20
  242.5 0.0 copy-start.23
  242.6 0.0 copy-start.25
  242.6 0.0 copy-start.31
  242.6 0.0 copy-start.32
  242.6 2.3 copy.57
  245.1 2.6 %adam_step.1 = (f32[8,128]{1,0:T(8,128)S(1)}, f32[3,96,192]{2,1,0:T(8,128)}, f32[3,96,192]{2,1,0:T(8,128)}, f32[3,96,192]{2,1,0:T(8,128)}, f32[192,96]{1,0:T(8,1...) custom-call(f32[3,96,768]{2,1,0:T(8,128)S(1)} %copy-done.3, ...), custom_call_target="tpu_custom_call" | custom-call | tf_op jit(solution)/shard_map/adam_step/pallas_call | solution.py:1236
  247.7 0.5 slice.11
  248.2 0.6 reduce
  248.8 0.6 reduce.1
  249.4 0.6 reduce.2
  (39 shorter events, 0.1 us)
Async XLA Ops:
  1.4 6.7 %copy-start.22 = (f32[1,768]{1,0:T(1,128)}, f32[1,768]{1,0:T(1,128)S(1)}, u32[]{:S(2)}) copy-start(f32[1,768]{1,0:T(1,128)S(1)} %broadcast_in_dim.10.up_bias.refs_22_) | copy-start | bytes 9220
  1.4 6.0 %copy-start.33 = (bf16[8,261,768]{2,0,1:T(8,128)(2,1)S(1)}, bf16[8,261,768]{2,0,1:T(8,128)(2,1)}, u32[]{:S(2)}) copy-start(bf16[8,261,768]{2,0,1:T(8,128)(2,1)} %param.26) | copy-start | bytes 9621508
  7.4 1.0 copy-start
  7.4 1.0 copy-start.1
  7.4 1.1 copy-start.2
  7.4 1.1 copy-start.8
  7.4 1.1 copy-start.27
  10.5 0.9 copy-start.4
  11.4 0.9 copy-start.5
  12.3 1.0 copy-start.6
  13.3 0.8 copy-start.7
  14.1 0.7 copy-start.15
  14.8 0.6 copy-start.24
  239.3 2.8 %copy-start.34 = (bf16[4,544,768]{2,1,0:T(8,128)(2,1)S(1)}, bf16[4,544,768]{2,1,0:T(8,128)(2,1)}, u32[]{:S(2)}) copy-start(bf16[4,544,768]{2,1,0:T(8,128)(2,1)} %get-tuple-element.73) | copy-start | bytes 10027012
  242.4 2.5 %copy-start.3 = (f32[3,96,768]{2,1,0:T(8,128)S(1)}, f32[3,96,768]{2,1,0:T(8,128)}, u32[]{:S(2)}) copy-start(f32[3,96,768]{2,1,0:T(8,128)} %get-tuple-element.74.refs_0_) | copy-start | bytes 2654212
  242.4 2.5 %copy-start.9 = (f32[3,96,192]{2,1,0:T(8,128)S(1)}, f32[3,96,192]{2,1,0:T(8,128)}, u32[]{:S(2)}) copy-start(f32[3,96,192]{2,1,0:T(8,128)} %refs_5_.1) | copy-start | bytes 663556
  242.4 2.5 %copy-start.10 = (f32[3,96,192]{2,1,0:T(8,128)S(1)}, f32[3,96,192]{2,1,0:T(8,128)}, u32[]{:S(2)}) copy-start(f32[3,96,192]{2,1,0:T(8,128)} %refs_6_.1) | copy-start | bytes 663556
  242.4 2.5 %copy-start.11 = (f32[96,768]{1,0:T(8,128)S(1)}, f32[96,768]{1,0:T(8,128)}, u32[]{:S(2)}) copy-start(f32[96,768]{1,0:T(8,128)} %refs_11_.1) | copy-start | bytes 884740
  242.4 2.5 %copy-start.12 = (f32[96,768]{1,0:T(8,128)S(1)}, f32[96,768]{1,0:T(8,128)}, u32[]{:S(2)}) copy-start(f32[96,768]{1,0:T(8,128)} %refs_12_.1) | copy-start | bytes 884740
  242.5 2.5 %copy-start.13 = (f32[768,96]{0,1:T(8,128)S(1)}, f32[768,96]{0,1:T(8,128)}, u32[]{:S(2)}) copy-start(f32[768,96]{0,1:T(8,128)} %param.37) | copy-start | bytes 884740
  242.5 2.5 %copy-start.14 = (f32[768,96]{0,1:T(8,128)S(1)}, f32[768,96]{0,1:T(8,128)}, u32[]{:S(2)}) copy-start(f32[768,96]{0,1:T(8,128)} %param.38) | copy-start | bytes 884740
  242.5 2.5 %copy-start.16 = (f32[9,768]{1,0:T(8,128)S(1)}, f32[9,768]{1,0:T(8,128)}, u32[]{:S(2)}) copy-start(f32[9,768]{1,0:T(8,128)} %refs_16_.1) | copy-start | bytes 82948
  242.5 2.5 %copy-start.17 = (f32[192,96]{1,0:T(8,128)S(1)}, f32[192,96]{1,0:T(8,128)}, u32[]{:S(2)}) copy-start(f32[192,96]{1,0:T(8,128)} %refs_8_.1) | copy-start | bytes 221188
  242.5 2.5 %copy-start.18 = (f32[192,96]{1,0:T(8,128)S(1)}, f32[192,96]{1,0:T(8,128)}, u32[]{:S(2)}) copy-start(f32[192,96]{1,0:T(8,128)} %refs_9_.1) | copy-start | bytes 221188
  242.5 2.5 %copy-start.19 = (f32[24,768]{1,0:T(8,128)S(1)}, f32[24,768]{1,0:T(8,128)}, u32[]{:S(2)}) copy-start(f32[24,768]{1,0:T(8,128)} %get-tuple-element.75.refs_1_) | copy-start | bytes 221188
  242.5 2.5 %copy-start.20 = (f32[9,768]{1,0:T(8,128)S(1)}, f32[9,768]{1,0:T(8,128)}, u32[]{:S(2)}) copy-start(f32[9,768]{1,0:T(8,128)} %refs_17_.1) | copy-start | bytes 82948
  242.5 2.5 copy-start.21
  242.5 2.5 copy-start.23
  242.6 2.5 copy-start.25
  242.6 2.5 copy-start.26
  242.6 2.5 copy-start.28
  242.6 2.5 copy-start.29
  242.6 2.5 copy-start.30
  242.6 2.5 copy-start.31
  242.6 2.5 copy-start.32
